TPU v7x, 32 devices: a whole 2x2x4 slice. The times are simulated.
32 devices in a mesh: seq: 8 (over y, x, core), dp: 4 (over z).
Axes of the slice: x: 2, y: 2, z: 4, core: 2. Of those that a mesh axis runs over, the one named last changes fastest.
Arguments:
- queries: bfloat16 [4, 8, 1024, 1024], P('dp', 'seq'), may hold values from -6 to 6
- keys: bfloat16 [4, 8, 1024, 1024], P('dp', 'seq'), may hold values from -6 to 6
- values: bfloat16 [4, 8, 1024, 1024], P('dp', 'seq'), may hold values from -6 to 6
- out_weight: bfloat16 [1024, 2048], P(('seq', 'dp')), may hold values from -0.1875 to 0.1875
- cotangent: bfloat16 [4, 8, 1024, 2048], P('dp', 'seq'), may hold values from -6 to 6
Outputs:
- layer_out: bfloat16 [4, 8, 1024, 2048], P('dp', 'seq')
- query_grad: bfloat16 [4, 8, 1024, 1024], P('dp', 'seq')
- key_grad: bfloat16 [4, 8, 1024, 1024], P('dp', 'seq')
- value_grad: bfloat16 [4, 8, 1024, 1024], P('dp', 'seq')
- weight_grad: float32 [1024, 2048], P(('seq', 'dp'))
All inputs are finite; a program needn't handle non-finite values.
Results may differ from a plain program's by a relative error of at most 0.0071.
Values may be sent and summed in bfloat16 or wider, within the bound.
No kernel may reach another device: no remote copies, remote signals or barrier semaphores. Data moves between devices by JAX's collectives and lax.ppermute only.
A program may use at most 128 MiB of HBM per device.

v0:
```python
import math

import jax
import jax.numpy as jnp
from jax import lax
from jax.sharding import PartitionSpec as P

ROW_HEADS = 4
COL_HEADS = 4
DH = 128


def attend_sets(query_set, key_set, value_set, upstream_set):
    factor = 1.0 / math.sqrt(query_set.shape[-1])
    scores = (
        jnp.einsum("...ld,...md->...lm", query_set, key_set, preferred_element_type=jnp.float32)
        * factor
    )
    length = scores.shape[-1]
    masked_out = lax.broadcasted_iota(jnp.int32, (length, length), 1) > lax.broadcasted_iota(
        jnp.int32, (length, length), 0
    )
    scores = jnp.where(masked_out, -jnp.inf, scores)
    peak_score = jnp.max(scores, axis=-1, keepdims=True)
    raised = jnp.exp(scores - peak_score)
    shares = raised / jnp.sum(raised, axis=-1, keepdims=True)
    shares_low = shares.astype(jnp.bfloat16)
    output = jnp.einsum(
        "...lm,...md->...ld", shares_low, value_set, preferred_element_type=jnp.float32
    ).astype(jnp.bfloat16)
    share_grad = jnp.einsum(
        "...ld,...md->...lm", upstream_set, value_set, preferred_element_type=jnp.float32
    )
    value_grad = jnp.einsum(
        "...lm,...ld->...md", shares_low, upstream_set, preferred_element_type=jnp.float32
    ).astype(jnp.bfloat16)
    row_total = jnp.sum(shares * share_grad, axis=-1, keepdims=True)
    score_low = (shares * (share_grad - row_total)).astype(jnp.bfloat16)
    query_grad = (
        jnp.einsum("...lm,...md->...ld", score_low, key_set, preferred_element_type=jnp.float32)
        * factor
    ).astype(jnp.bfloat16)
    key_grad = (
        jnp.einsum("...lm,...ld->...md", score_low, query_set, preferred_element_type=jnp.float32)
        * factor
    ).astype(jnp.bfloat16)
    return (output, query_grad, key_grad, value_grad)


def group_step(grouped):
    return attend_sets(grouped[0], grouped[1], grouped[2], grouped[3])


def column_sets(gathered):
    reordered = [jnp.moveaxis(member, 1, 3) for member in gathered]
    results = attend_sets(reordered[0], reordered[1], reordered[2], reordered[3])
    return tuple((jnp.moveaxis(member, 3, 1) for member in results))


def body(queries, keys, values, out_weight, cotangent):
    seq_count, rows_here, stride, head_width = queries.shape
    model_width = cotangent.shape[-1]
    row_width = ROW_HEADS * DH
    flat_cot = cotangent.reshape(-1, model_width)
    weight_full = lax.all_gather(out_weight, ("seq", "dp"), axis=0, tiled=True)
    upstream_wide = jnp.einsum(
        "td,hd->th", flat_cot, weight_full, preferred_element_type=jnp.float32
    )
    upstream = upstream_wide.astype(jnp.bfloat16).reshape(seq_count, rows_here, stride, head_width)

    def column_part(member):
        return member[..., row_width:].reshape(seq_count, rows_here, stride, COL_HEADS, DH)

    column_query = column_part(queries)
    column_key = column_part(keys)
    column_value = column_part(values)
    column_upstream = column_part(upstream)
    column_output, column_qgrad, column_kgrad, column_vgrad = column_sets(
        (
            lax.all_to_all(column_query, "seq", split_axis=2, concat_axis=1, tiled=True),
            lax.all_to_all(column_key, "seq", split_axis=2, concat_axis=1, tiled=True),
            lax.all_to_all(column_value, "seq", split_axis=2, concat_axis=1, tiled=True),
            lax.all_to_all(column_upstream, "seq", split_axis=2, concat_axis=1, tiled=True),
        )
    )

    def row_part(member):
        return jnp.moveaxis(
            member[..., :row_width].reshape(seq_count, rows_here, stride, ROW_HEADS, DH), 3, 0
        )

    row_results = lax.map(
        group_step, (row_part(queries), row_part(keys), row_part(values), row_part(upstream))
    )
    row_layout = (
        lax.all_to_all(column_output, "seq", split_axis=1, concat_axis=2, tiled=True),
        lax.all_to_all(column_qgrad, "seq", split_axis=1, concat_axis=2, tiled=True),
        lax.all_to_all(column_kgrad, "seq", split_axis=1, concat_axis=2, tiled=True),
        lax.all_to_all(column_vgrad, "seq", split_axis=1, concat_axis=2, tiled=True),
    )
    joined = []
    for row_member, col_member in zip(row_results, row_layout):
        row_flat = jnp.moveaxis(row_member, 0, 3).reshape(seq_count, rows_here, stride, row_width)
        col_flat = col_member.reshape(seq_count, rows_here, stride, COL_HEADS * DH)
        joined.append(jnp.concatenate([row_flat, col_flat], axis=-1))
    attn_flat = joined[0].reshape(-1, head_width)
    projected = jnp.dot(attn_flat, weight_full, preferred_element_type=jnp.float32)
    layer_out = projected.astype(jnp.bfloat16).reshape(seq_count, rows_here, stride, model_width)
    seq_devices = lax.axis_size("seq")
    dp_devices = lax.axis_size("dp")
    token_total = seq_count * dp_devices * rows_here * seq_devices * stride
    grad_factor = 1.0 / math.sqrt(token_total)
    weight_grad = lax.psum_scatter(
        jnp.einsum("th,td->hd", attn_flat, flat_cot, preferred_element_type=jnp.float32)
        * grad_factor,
        ("seq", "dp"),
        scatter_dimension=0,
        tiled=True,
    )
    return (layer_out, joined[1], joined[2], joined[3], weight_grad)


def solution(mesh):
    return jax.shard_map(
        body,
        mesh=mesh,
        in_specs=(
            P("dp", "seq", None, None),
            P("dp", "seq", None, None),
            P("dp", "seq", None, None),
            P(("seq", "dp"), None),
            P("dp", "seq", None, None),
        ),
        out_specs=(
            P("dp", "seq", None, None),
            P("dp", "seq", None, None),
            P("dp", "seq", None, None),
            P("dp", "seq", None, None),
            P(("seq", "dp"), None),
        ),
        check_vma=False,
    )
```

profile of v0, /device:TPU:0, one launch (start us, length us, event | category | flops | bytes accessed | tf_op | source)
XLA Modules:
  0.0 392.4 jit_solution(6216739479635003085)
XLA Ops:
  12.6 5.2 %all-to-all-start = ((bf16[1,1,1024,4,128]{4,3,1,0,2:T(4,128)(2,1)}), bf16[1,1,1024,4,128]{4,3,1,0,2:T(4,128)(2,1)S(1)}, u32[]{:S(2)}, u32[]{:S(2)}) async-start(bf16[1,1,1024,4,128]{4,3,1,0,2:T(4,128)(2,1)} %copy.81), calls=%async_computation | async-start | bytes 2097152 | tf_op jit(solution)/shard_map/all_to_all | solution.py:80
  22.4 11.7 %all-to-all-done = bf16[1,1,1024,4,128]{4,3,1,0,2:T(4,128)(2,1)S(1)} async-done(((bf16[1,1,1024,4,128]{4,3,1,0,2:T(4,128)(2,1)}), bf16[1,1,1024,4,128]{4,3,1,0,2:T(4,128)(2,1)S(1)}, u32[]{:S(2)}, u32[]{:S(2)}) %all-to-all-start) | async-done | bytes 1048608 | tf_op jit(solution)/shard_map/all_to_all | solution.py:80
  34.0 3.6 all-to-all-start.1
  43.6 13.0 %all-to-all-done.1 = bf16[1,1,1024,4,128]{4,3,1,0,2:T(4,128)(2,1)S(1)} async-done(((bf16[1,1,1024,4,128]{4,3,1,0,2:T(4,128)(2,1)}), bf16[1,1,1024,4,128]{4,3,1,0,2:T(4,128)(2,1)S(1)}, u32[]{:S(2)}, u32[]{:S(2)}) %all-to-all-start.1) | async-done | bytes 1048608 | tf_op jit(solution)/shard_map/all_to_all | solution.py:81
  56.6 3.6 all-to-all-start.2
  60.2 3.6 fusion.82
  63.8 19.2 %all-to-all-done.2 = bf16[1,1,1024,4,128]{4,3,1,0,2:T(4,128)(2,1)S(1)} async-done(((bf16[1,1,1024,4,128]{4,3,1,0,2:T(4,128)(2,1)}), bf16[1,1,1024,4,128]{4,3,1,0,2:T(4,128)(2,1)S(1)}, u32[]{:S(2)}, u32[]{:S(2)}) %all-to-all-start.2) | async-done | bytes 1048608 | tf_op jit(solution)/shard_map/all_to_all | solution.py:82
  88.0 3.6 all-to-all-start.3
  96.8 10.1 %all-to-all-done.3 = bf16[1,8,128,4,128]{4,3,2,0,1:T(4,128)(2,1)S(1)} async-done(((bf16[1,8,128,4,128]{4,3,2,0,1:T(4,128)(2,1)}), bf16[1,8,128,4,128]{4,3,2,0,1:T(4,128)(2,1)S(1)}, u32[]{:S(2)}, u32[]{:S(2)}) %all-to-all-start.3) | async-done | bytes 1048608 | tf_op jit(solution)/shard_map/all_to_all | solution.py:96
  107.9 8.3 %convert_bitcast_fusion.1 = bf16[1,1,1024,1024]{2,3,1,0:T(8,128)(2,1)S(1)} fusion(bf16[1024,2048]{1,0:T(8,128)(2,1)} %all-gather.2.cloned.1.call-done, bf16[1,1,1024,2048]{3,2,1,0:T(8,128)(2,1)} %param.11), kind=kOutput, calls=%fused_computation.64 | convolution fusion | flops 4296015872 | bytes 10485760 | tf_op jit(solution)/shard_map/td,hd->th/dot_general | solution.py:66
  117.8 72.3 %while.16 = (s32[]{:T(128)}, bf16[4,1,1,1024,128]{3,4,0,2,1:T(8,128)(2,1)}, bf16[4,1,1,1024,128]{4,3,2,1,0:T(8,128)(2,1)}, bf16[4,1,1,1024,128]{4,3,2,1,0:T(8,12...) while((s32[]{:T(128)}, ...), condition=%wide.region_4.5_spmd, body=%wide.region_0.4_spmd.sunk | while | flops 1649144832 | bytes 77653160 | solution.py:92
  124.3 3.8 fusion.124
  142.3 3.8 fusion.124
  160.4 3.8 fusion.124
  178.5 3.8 fusion.124
  190.0 10.2 %convolution_multiply_fusion.2 = f32[1024,2048]{1,0:T(8,128)} fusion(bf16[1,1,1024,2048]{3,2,1,0:T(8,128)(2,1)} %param.11, bf16[1,1,1024,512]{2,3,1,0:T(8,128)(2,1)S(1)} %copy.119, bf16[1,1,1024,512]{2,3,1,0:T(8,128)(2,1)} %bitcast.212), kind=kOutput, calls=%fused_computation.49 | convolution fusion | flops 4301258752 | bytes 14680064 | tf_op jit(solution)/shard_map/th,td->hd/dot_general | solution.py:114
  201.0 20.5 %all_to_all.84 = bf16[1,1,1024,4,128]{4,3,1,0,2:T(4,128)(2,1)S(1)} all-to-all(bf16[1,1,1024,4,128]{4,3,1,0,2:T(4,128)(2,1)S(1)} %copy.96), channel_id=1, replica_groups=mesh['seq'=8,'dp'=4] {'seq'}, dimensions={2} | all-to-all | bytes 2097152 | tf_op jit(solution)/shard_map/all_to_all | solution.py:83
  225.9 3.6 all-to-all-start.7
  236.5 12.1 %all-to-all-done.7 = bf16[1,8,128,4,128]{4,3,2,0,1:T(4,128)(2,1)S(1)} async-done(((bf16[1,8,128,4,128]{4,3,2,0,1:T(4,128)(2,1)}), bf16[1,8,128,4,128]{4,3,2,0,1:T(4,128)(2,1)S(1)}, u32[]{:S(2)}, u32[]{:S(2)}) %all-to-all-start.7) | async-done | bytes 1048608 | tf_op jit(solution)/shard_map/all_to_all | solution.py:99
  248.6 4.2 %all-to-all-start.6 = ((bf16[1,8,128,4,128]{4,3,2,0,1:T(4,128)(2,1)}), bf16[1,8,128,4,128]{4,3,2,0,1:T(4,128)(2,1)}, u32[]{:S(2)}, u32[]{:S(2)}) async-start(bf16[1,8,128,4,128]{4,3,2,0,1:T(4,128)(2,1)} %copy.103), calls=%async_computation.6 | async-start | bytes 2097152 | tf_op jit(solution)/shard_map/all_to_all | solution.py:98
  262.1 9.6 %all-to-all-done.6 = bf16[1,8,128,4,128]{4,3,2,0,1:T(4,128)(2,1)} async-done(((bf16[1,8,128,4,128]{4,3,2,0,1:T(4,128)(2,1)}), bf16[1,8,128,4,128]{4,3,2,0,1:T(4,128)(2,1)}, u32[]{:S(2)}, u32[]{:S(2)}) %all-to-all-start.6) | async-done | bytes 1048608 | tf_op jit(solution)/shard_map/all_to_all | solution.py:98
  271.7 4.5 %all-to-all-start.5 = ((bf16[1,8,128,4,128]{4,3,2,0,1:T(4,128)(2,1)}), bf16[1,8,128,4,128]{4,3,2,0,1:T(4,128)(2,1)}, u32[]{:S(2)}, u32[]{:S(2)}) async-start(bf16[1,8,128,4,128]{4,3,2,0,1:T(4,128)(2,1)} %copy.100), calls=%async_computation.5 | async-start | bytes 2097152 | tf_op jit(solution)/shard_map/all_to_all | solution.py:97
  276.3 8.3 %convert_bitcast_fusion = bf16[1,1,1024,2048]{3,2,1,0:T(8,128)(2,1)} fusion(bf16[1024,2048]{1,0:T(8,128)(2,1)} %all-gather.2.cloned.1.call-done, bf16[1,1,1024,512]{2,3,1,0:T(8,128)(2,1)S(1)} %copy-done.13, bf16[1,1,1024,512]{2,3,1,0:T(8,128)(2,1)S(1)} %bitcast.213), kind=kOutput, calls=%fused_computation.53 | convolution fusion | flops 4301258752 | bytes 10485760 | tf_op jit(solution)/shard_map/dot_general | solution.py:107
  303.4 82.1 %reduce-scatter.2.cloned.1.call-done = f32[32,2048]{1,0:T(8,128)} async-done(((f32[1024,2048]{1,0:T(8,128)}), f32[32,2048]{1,0:T(8,128)}) %reduce-scatter.2.cloned.1.call-update) | async-done | bytes 262160 | tf_op jit(solution)/shard_map/reduce_scatter | solution.py:113
  (137 shorter events, 125.6 us)
Async XLA Ops:
  7.2 100.8 %all-gather.2.cloned.1.call-start = ((), (), s32[]{:S(2)}) async-start(), calls=%async_computation.9 | async-start | bytes 4325376 | tf_op jit(solution)/shard_map/all_gather | solution.py:65
  12.6 21.5 %all-to-all-start = ((bf16[1,1,1024,4,128]{4,3,1,0,2:T(4,128)(2,1)}), bf16[1,1,1024,4,128]{4,3,1,0,2:T(4,128)(2,1)S(1)}, u32[]{:S(2)}, u32[]{:S(2)}) async-start(bf16[1,1,1024,4,128]{4,3,1,0,2:T(4,128)(2,1)} %copy.81), calls=%async_computation | async-start | bytes 2097152 | tf_op jit(solution)/shard_map/all_to_all | solution.py:80
  34.0 26.1 %copy-start.4 = (bf16[1,1,1024,4,128]{4,3,1,0,2:T(4,128)(2,1)}, bf16[1,1,1024,4,128]{4,3,1,0,2:T(4,128)(2,1)S(1)}, u32[]{:S(2)}) copy-start(bf16[1,1,1024,4,128]{4,3,1,0,2:T(4,128)(2,1)S(1)} %all-to-all-done) | copy-start | bytes 3145732
  34.0 22.5 %all-to-all-start.1 = ((bf16[1,1,1024,4,128]{4,3,1,0,2:T(4,128)(2,1)}), bf16[1,1,1024,4,128]{4,3,1,0,2:T(4,128)(2,1)S(1)}, u32[]{:S(2)}, u32[]{:S(2)}) async-start(bf16[1,1,1024,4,128]{4,3,1,0,2:T(4,128)(2,1)} %copy.85), calls=%async_computation.1 | async-start | bytes 2097152 | tf_op jit(solution)/shard_map/all_to_all | solution.py:81
  56.6 7.2 %copy-start.2 = (bf16[1,1,1024,4,128]{4,3,1,0,2:T(4,128)(2,1)}, bf16[1,1,1024,4,128]{4,3,1,0,2:T(4,128)(2,1)S(1)}, u32[]{:S(2)}) copy-start(bf16[1,1,1024,4,128]{4,3,1,0,2:T(4,128)(2,1)S(1)} %all-to-all-done.1) | copy-start | bytes 3145732
  56.6 26.4 %all-to-all-start.2 = ((bf16[1,1,1024,4,128]{4,3,1,0,2:T(4,128)(2,1)}), bf16[1,1,1024,4,128]{4,3,1,0,2:T(4,128)(2,1)S(1)}, u32[]{:S(2)}, u32[]{:S(2)}) async-start(bf16[1,1,1024,4,128]{4,3,1,0,2:T(4,128)(2,1)} %copy.89), calls=%async_computation.2 | async-start | bytes 2097152 | tf_op jit(solution)/shard_map/all_to_all | solution.py:82
  63.8 52.5 %copy-start.15 = (f32[128,4,8]{2,1,0:T(4,128)}, f32[128,4,8]{2,1,0:T(4,128)S(1)}, u32[]{:S(2)}) copy-start(f32[128,4,8]{2,1,0:T(4,128)S(1)} %get-tuple-element.131) | copy-start | bytes 49156
  86.6 5.2 %copy-start.6 = (bf16[1,1,1024,512]{3,2,1,0:T(8,128)(2,1)S(1)}, bf16[1,1,1024,512]{3,2,1,0:T(8,128)(2,1)}, u32[]{:S(2)}) copy-start(bf16[1,1,1024,512]{3,2,1,0:T(8,128)(2,1)} %get-tuple-element.129) | copy-start | bytes 3145732
  86.6 6.6 %copy-start.7 = (bf16[1,1,1024,512]{3,2,1,0:T(8,128)(2,1)S(1)}, bf16[1,1,1024,512]{3,2,1,0:T(8,128)(2,1)}, u32[]{:S(2)}) copy-start(bf16[1,1,1024,512]{3,2,1,0:T(8,128)(2,1)} %get-tuple-element.127) | copy-start | bytes 3145732
  88.0 18.9 %all-to-all-start.3 = ((bf16[1,8,128,4,128]{4,3,2,0,1:T(4,128)(2,1)}), bf16[1,8,128,4,128]{4,3,2,0,1:T(4,128)(2,1)S(1)}, u32[]{:S(2)}, u32[]{:S(2)}) async-start(bf16[1,8,128,4,128]{4,3,2,0,1:T(4,128)(2,1)} %copy.93), calls=%async_computation.3 | async-start | bytes 2097152 | tf_op jit(solution)/shard_map/all_to_all | solution.py:96
  91.6 294.0 %reduce-scatter.2.cloned.1.call-start = ((), (), s32[]{:S(2)}) async-start(), calls=%async_computation.10 | async-start | bytes 8650752 | tf_op jit(solution)/shard_map/reduce_scatter | solution.py:113
  107.9 82.1 %copy-start.12 = (bf16[1,1,1024,512]{2,3,1,0:T(8,128)(2,1)}, bf16[1,1,1024,512]{2,3,1,0:T(8,128)(2,1)S(1)}, u32[]{:S(2)}) copy-start(bf16[1,1,1024,512]{2,3,1,0:T(8,128)(2,1)S(1)} %copy.119) | copy-start | bytes 3145732
  124.2 3.8 copy-start.1
  160.4 3.8 copy-start.1
  178.4 3.8 copy-start.1
  200.3 21.3 %copy-start.16 = (f32[128,4,8]{2,1,0:T(4,128)S(1)}, f32[128,4,8]{2,1,0:T(4,128)}, u32[]{:S(2)}) copy-start(f32[128,4,8]{2,1,0:T(4,128)} %copy-done.15) | copy-start | bytes 49156
  224.5 5.0 %copy-start.9 = (f32[128,4,8,8]{2,3,1,0:T(8,128)S(1)}, f32[128,4,8,8]{2,3,1,0:T(8,128)}, u32[]{:S(2)}) copy-start(f32[128,4,8,8]{2,3,1,0:T(8,128)} %get-tuple-element.132) | copy-start | bytes 393220
  225.9 22.7 %all-to-all-start.7 = ((bf16[1,8,128,4,128]{4,3,2,0,1:T(4,128)(2,1)}), bf16[1,8,128,4,128]{4,3,2,0,1:T(4,128)(2,1)S(1)}, u32[]{:S(2)}, u32[]{:S(2)}) async-start(bf16[1,8,128,4,128]{4,3,2,0,1:T(4,128)(2,1)} %copy.106), calls=%async_computation.7 | async-start | bytes 2097152 | tf_op jit(solution)/shard_map/all_to_all | solution.py:99
  236.5 23.3 %copy-start.3 = (bf16[1,1,1024,4,128]{4,3,1,0,2:T(4,128)(2,1)S(1)}, bf16[1,1,1024,4,128]{4,3,1,0,2:T(4,128)(2,1)}, u32[]{:S(2)}) copy-start(bf16[1,1,1024,4,128]{4,3,1,0,2:T(4,128)(2,1)} %copy-done.2) | copy-start | bytes 3145732
  248.6 23.2 %all-to-all-start.6 = ((bf16[1,8,128,4,128]{4,3,2,0,1:T(4,128)(2,1)}), bf16[1,8,128,4,128]{4,3,2,0,1:T(4,128)(2,1)}, u32[]{:S(2)}, u32[]{:S(2)}) async-start(bf16[1,8,128,4,128]{4,3,2,0,1:T(4,128)(2,1)} %copy.103), calls=%async_computation.6 | async-start | bytes 2097152 | tf_op jit(solution)/shard_map/all_to_all | solution.py:98
  260.7 15.6 %copy-start.13 = (bf16[1,1,1024,512]{2,3,1,0:T(8,128)(2,1)S(1)}, bf16[1,1,1024,512]{2,3,1,0:T(8,128)(2,1)}, u32[]{:S(2)}) copy-start(bf16[1,1,1024,512]{2,3,1,0:T(8,128)(2,1)} %copy-done.12) | copy-start | bytes 3145732
  260.7 15.6 %copy-start.17 = (bf16[4,1,1,1024,128]{3,4,0,2,1:T(8,128)(2,1)S(1)}, bf16[4,1,1,1024,128]{3,4,0,2,1:T(8,128)(2,1)}, u32[]{:S(2)}) copy-start(bf16[4,1,1,1024,128]{3,4,0,2,1:T(8,128)(2,1)} %get-tuple-element.55) | copy-start | bytes 3145732
  271.7 24.9 %all-to-all-start.5 = ((bf16[1,8,128,4,128]{4,3,2,0,1:T(4,128)(2,1)}), bf16[1,8,128,4,128]{4,3,2,0,1:T(4,128)(2,1)}, u32[]{:S(2)}, u32[]{:S(2)}) async-start(bf16[1,8,128,4,128]{4,3,2,0,1:T(4,128)(2,1)} %copy.100), calls=%async_computation.5 | async-start | bytes 2097152 | tf_op jit(solution)/shard_map/all_to_all | solution.py:97
  294.1 5.4 %copy-start.8 = (bf16[1,1,1024,4,128]{2,4,3,1,0:T(8,128)(2,1)S(1)}, bf16[1,1,1024,4,128]{2,4,3,1,0:T(8,128)(2,1)}, u32[]{:S(2)}) copy-start(bf16[1,1,1024,4,128]{2,4,3,1,0:T(8,128)(2,1)} %copy.95) | copy-start | bytes 3145732
  (9 other events, 20.6 us)
Sparse Core Ops, SparseCore 0:
  11.0 77.0 all-gather.1
  200.4 185.1 reduce-scatter.1
where the time goes:
time: 394 us; the launch traced here: 392 us
  waiting for transfers between devices  159 us (40%)
  matrix products  98 us (25%)
  local copies, waits for them, and re-layouts  61.1 us (16%)
  starting transfers between devices  28.4 us (7%)
  blocking collectives  20.5 us (5%)
  between operations  14.4 us (4%)
  other arithmetic  11.2 us (3%)
    reduce_scatter x1, waiting for transfers between devices, body(): lax.psum_scatter(jnp.einsum('th,td->hd', attn_flat, flat_cot, preferred_e...  82.1 us
    all_to_all x1, blocking collectives, body(): lax.all_to_all(column_upstream, 'seq', split_axis=2, concat_axis=1, tiled...  20.5 us
    all_to_all x1, waiting for transfers between devices, body(): lax.all_to_all(column_value, 'seq', split_axis=2, concat_axis=1, tiled=True)  19.2 us
    dot_general x5, matrix products, attend_sets(): jnp.einsum('...lm,...ld->...md', shares_low, upstream_set, preferred_elem...  18.1 us
    unnamed x41, local copies, waits for them, and re-layouts  16.9 us
    all_to_all x1, waiting for transfers between devices, body(): lax.all_to_all(column_key, 'seq', split_axis=2, concat_axis=1, tiled=True)  13 us
    all_to_all x1, waiting for transfers between devices, body(): lax.all_to_all(column_vgrad, 'seq', split_axis=1, concat_axis=2, tiled=True)  12.1 us
    all_to_all x1, waiting for transfers between devices, body(): lax.all_to_all(column_query, 'seq', split_axis=2, concat_axis=1, tiled=True)  11.7 us
  transfers between devices with their start and end apart: 9, of which 7 were waited for; matrix products, arithmetic and copies ran while one was open for 19% of the time, Pallas kernels for 0%

commit v1 on v0

v1 whole, which is shorter than its diff:
```python
import functools
import math

import jax
import jax.numpy as jnp
from jax import lax
from jax.experimental import pallas as pl
from jax.experimental.pallas import tpu as pltpu
from jax.sharding import PartitionSpec as P

ROW_HEADS = 4
COL_HEADS = 4
DH = 128
ROW_WIDTH = ROW_HEADS * DH
COL_WIDTH = COL_HEADS * DH
FACTOR = 1.0 / math.sqrt(DH)
EXP_SCALE = FACTOR * math.log2(math.e)
BLOCK = 256
LOW = -1e30
BF16 = jnp.bfloat16
F32 = jnp.float32
VMEM = 56 * 1024 * 1024
DECLARED = {
    "pack": 0.6, "unpack": 0.6, "row_forward": 1.0, "row_backward": 1.4,
    "column_forward": 110.0, "column_backward": 120.0, "upstream_col": 0.7, "upstream_row": 0.7,
    "weight_row": 0.6, "weight_col": 0.6, "layer_output": 0.9,
}
DECLARED_FLOPS = 1.15e9


def cost(name):
    return pl.CostEstimate(
        flops=int(DECLARED[name] * DECLARED_FLOPS), transcendentals=0, bytes_accessed=0
    )


def params():
    return pltpu.CompilerParams(vmem_limit_bytes=VMEM)


def dot(a, b, a_dim, b_dim):
    return lax.dot_general(a, b, (((a_dim,), (b_dim,)), ((), ())), preferred_element_type=F32)


def whole(shape):
    return pl.BlockSpec(shape, lambda *_: (0,) * len(shape))


def softmax_chunks(score_chunks):
    peak = functools.reduce(
        jnp.maximum, [jnp.max(s, axis=0, keepdims=True) for s in score_chunks]
    )
    shift = peak * EXP_SCALE
    raised = [jnp.exp2(s * EXP_SCALE - shift) for s in score_chunks]
    total = functools.reduce(jnp.add, [jnp.sum(e, axis=0, keepdims=True) for e in raised])
    inverse = 1.0 / total
    return [e * inverse for e in raised]


def backward_chunks(shares, query, upstream, keys, values):
    lows = [p.astype(BF16) for p in shares]
    share_grads = [dot(v, upstream, 1, 1) for v in values]
    row_total = functools.reduce(
        jnp.add, [jnp.sum(p * g, axis=0, keepdims=True) for p, g in zip(shares, share_grads)]
    )
    score_lows = [(p * (g - row_total)).astype(BF16) for p, g in zip(shares, share_grads)]
    value_parts = [dot(p, upstream, 1, 0) for p in lows]
    key_parts = [dot(s, query, 1, 0) for s in score_lows]
    query_part = functools.reduce(jnp.add, [dot(k, s, 0, 0) for k, s in zip(keys, score_lows)])
    return query_part.T, key_parts, value_parts


def causal_mask(block):
    return lax.broadcasted_iota(jnp.int32, (block, block), 0) <= lax.broadcasted_iota(
        jnp.int32, (block, block), 1
    )


def row_scores(q_ref, k_ref, i, block):
    query = q_ref[pl.ds(i * block, block), :]
    chunks = []
    for j in range(i + 1):
        s = dot(k_ref[pl.ds(j * block, block), :], query, 1, 1)
        if j == i:
            s = jnp.where(causal_mask(block), s, LOW)
        chunks.append(s)
    return query, chunks


def row_forward_kernel(q_ref, k_ref, v_ref, out_ref):
    steps = q_ref.shape[0]
    block = min(BLOCK, steps)
    for i in range(steps // block):
        _, chunks = row_scores(q_ref, k_ref, i, block)
        shares = softmax_chunks(chunks)
        total = functools.reduce(
            jnp.add,
            [
                dot(v_ref[pl.ds(j * block, block), :], p.astype(BF16), 0, 0)
                for j, p in enumerate(shares)
            ],
        )
        out_ref[pl.ds(i * block, block), :] = total.T.astype(BF16)


def row_backward_kernel(q_ref, k_ref, v_ref, u_ref, dq_ref, dk_ref, dv_ref, dk_sum, dv_sum):
    steps = q_ref.shape[0]
    block = min(BLOCK, steps)
    for i in range(steps // block):
        query, chunks = row_scores(q_ref, k_ref, i, block)
        shares = softmax_chunks(chunks)
        upstream = u_ref[pl.ds(i * block, block), :]
        keys = [k_ref[pl.ds(j * block, block), :] for j in range(i + 1)]
        values = [v_ref[pl.ds(j * block, block), :] for j in range(i + 1)]
        query_part, key_parts, value_parts = backward_chunks(
            shares, query, upstream, keys, values
        )
        dq_ref[pl.ds(i * block, block), :] = (query_part * FACTOR).astype(BF16)
        for j in range(i + 1):
            rows = pl.ds(j * block, block)
            if j == i:
                dk_sum[rows, :] = key_parts[j]
                dv_sum[rows, :] = value_parts[j]
            else:
                dk_sum[rows, :] += key_parts[j]
                dv_sum[rows, :] += value_parts[j]
    dk_ref[...] = (dk_sum[...] * FACTOR).astype(BF16)
    dv_ref[...] = dv_sum[...].astype(BF16)


def row_forward(queries, keys, values):
    steps = queries.shape[0]
    head = pl.BlockSpec((steps, DH), lambda h: (0, h))
    return pl.pallas_call(
        row_forward_kernel,
        grid=(ROW_HEADS,),
        in_specs=[head] * 3,
        out_specs=head,
        out_shape=jax.ShapeDtypeStruct((steps, ROW_WIDTH), BF16),
        compiler_params=params(),
        cost_estimate=cost("row_forward"),
        name="row_forward",
    )(queries, keys, values)


def row_backward(queries, keys, values, upstream):
    steps = queries.shape[0]
    head = pl.BlockSpec((steps, DH), lambda h: (0, h))
    return pl.pallas_call(
        row_backward_kernel,
        grid=(ROW_HEADS,),
        in_specs=[head] * 4,
        out_specs=[head] * 3,
        out_shape=[jax.ShapeDtypeStruct(queries.shape, BF16)] * 3,
        scratch_shapes=[pltpu.VMEM((steps, DH), F32)] * 2,
        compiler_params=params(),
        cost_estimate=cost("row_backward"),
        name="row_backward",
    )(queries, keys, values, upstream)


def pack_kernel(q_ref, k_ref, v_ref, out_ref):
    group, _, cols, width = out_ref.shape
    for n, ref in enumerate((q_ref, k_ref, v_ref)):
        out_ref[:, n] = ref[...].reshape(group, cols, width)


def pack_specs(peers, cols):
    group = peers // 2
    return (
        pl.BlockSpec((group * cols, COL_WIDTH), lambda j: (j, ROW_WIDTH // COL_WIDTH)),
        pl.BlockSpec((group, 3, cols, COL_WIDTH), lambda j: (j, 0, 0, 0)),
    )


def pack(queries, keys, values, peers):
    cols = queries.shape[0] // peers
    apart, together = pack_specs(peers, cols)
    return pl.pallas_call(
        pack_kernel,
        grid=(2,),
        in_specs=[apart] * 3,
        out_specs=together,
        out_shape=jax.ShapeDtypeStruct((peers, 3, cols, COL_WIDTH), BF16),
        compiler_params=params(),
        cost_estimate=cost("pack"),
        name="pack",
    )(queries, keys, values)


def unpack_kernel(in_ref, _q, _k, _v, dq_ref, dk_ref, dv_ref):
    for n, ref in enumerate((dq_ref, dk_ref, dv_ref)):
        ref[...] = in_ref[:, n].reshape(ref.shape)


def unpack(packed, dq, dk, dv):
    peers, _, cols, _ = packed.shape
    apart, together = pack_specs(peers, cols)
    anywhere = pl.BlockSpec(memory_space=pl.ANY)
    return pl.pallas_call(
        unpack_kernel,
        grid=(2,),
        in_specs=[together] + [anywhere] * 3,
        out_specs=[apart] * 3,
        out_shape=[jax.ShapeDtypeStruct(dq.shape, BF16)] * 3,
        input_output_aliases={1: 0, 2: 1, 3: 2},
        compiler_params=params(),
        cost_estimate=cost("unpack"),
        name="unpack",
    )(packed, dq, dk, dv)


def column_mask(rows, cols):
    key = lax.broadcasted_iota(jnp.int32, (rows * cols, rows * cols), 0)
    query = lax.broadcasted_iota(jnp.int32, (rows * cols, rows * cols), 1)
    return (key <= query) & (key % cols == query % cols)


def head_tokens(block, h):
    rows, cols, _ = block.shape
    return block[:, :, h * DH : (h + 1) * DH].reshape(rows * cols, DH)


def column_forward_kernel(in_ref, out_ref):
    rows, _, cols, _ = in_ref.shape
    mask = column_mask(rows, cols)
    for h in range(COL_HEADS):
        query, key, value = [head_tokens(in_ref[:, n], h) for n in range(3)]
        scores = jnp.where(mask, dot(key, query, 1, 1), LOW)
        (share,) = softmax_chunks([scores])
        result = dot(value, share.astype(BF16), 0, 0).T
        out_ref[:, :, h * DH : (h + 1) * DH] = result.astype(BF16).reshape(rows, cols, DH)


def column_backward_kernel(in_ref, u_ref, out_ref):
    rows, _, cols, _ = in_ref.shape
    mask = column_mask(rows, cols)
    for h in range(COL_HEADS):
        query, key, value = [head_tokens(in_ref[:, n], h) for n in range(3)]
        upstream = head_tokens(u_ref[...], h)
        scores = jnp.where(mask, dot(key, query, 1, 1), LOW)
        shares = softmax_chunks([scores])
        query_grad, (key_grad,), (value_grad,) = backward_chunks(
            shares, query, upstream, [key], [value]
        )
        span = slice(h * DH, (h + 1) * DH)
        out_ref[:, 0, :, span] = (query_grad * FACTOR).astype(BF16).reshape(rows, cols, DH)
        out_ref[:, 1, :, span] = (key_grad * FACTOR).astype(BF16).reshape(rows, cols, DH)
        out_ref[:, 2, :, span] = value_grad.astype(BF16).reshape(rows, cols, DH)


def column_call(kernel, packed, upstream, name):
    rows, _, cols, width = packed.shape
    span = min(16, cols)
    three = pl.BlockSpec((rows, 3, span, width), lambda c: (0, 0, c, 0))
    one = pl.BlockSpec((rows, span, width), lambda c: (0, c, 0))
    forward = upstream is None
    return pl.pallas_call(
        kernel,
        grid=(cols // span,),
        in_specs=[three] if forward else [three, one],
        out_specs=one if forward else three,
        out_shape=jax.ShapeDtypeStruct(
            (rows, cols, width) if forward else (rows, 3, cols, width), BF16
        ),
        compiler_params=params(),
        cost_estimate=cost(name),
        name=name,
    )(*((packed,) if forward else (packed, upstream)))


def upstream_kernel(place_ref, *refs):
    *w_refs, cot_ref, up_ref, full_ref = refs
    each, rows, _ = w_refs[0].shape

    @pl.when(pl.program_id(0) == 0)
    def _():
        for n, w_ref in enumerate(w_refs):
            for m in range(each):
                at = pl.multiple_of(place_ref[n * each + m], rows)
                full_ref[pl.ds(at, rows), :] = w_ref[m]

    up_ref[...] = dot(cot_ref[...], full_ref[...], 1, 1).astype(BF16)


def upstream_of(place, pieces, cotangent, name):
    steps, model = cotangent.shape
    each, rows, _ = pieces[0].shape
    count = each * len(pieces)
    block = min(BLOCK, steps)
    return pl.pallas_call(
        upstream_kernel,
        grid=(steps // block,),
        in_specs=[
            pl.BlockSpec(memory_space=pltpu.SMEM),
            *[whole(piece.shape) for piece in pieces],
            pl.BlockSpec((block, model), lambda t: (t, 0)),
        ],
        out_specs=[
            pl.BlockSpec((block, count * rows), lambda t: (t, 0)),
            whole((count * rows, model)),
        ],
        out_shape=[
            jax.ShapeDtypeStruct((steps, count * rows), BF16),
            jax.ShapeDtypeStruct((count * rows, model), BF16),
        ],
        compiler_params=params(),
        cost_estimate=cost(name),
        name=name,
    )(place, *pieces, cotangent)


def layer_kernel(row_ref, col_ref, w_row_ref, w_col_ref, out_ref):
    out_ref[...] = (
        dot(row_ref[...], w_row_ref[...], 1, 0) + dot(col_ref[...], w_col_ref[...], 1, 0)
    ).astype(BF16)


def layer_output(attn_row, attn_col, w_row, w_col):
    steps, width = attn_row.shape
    model = w_row.shape[1]
    block = min(BLOCK, steps)
    return pl.pallas_call(
        layer_kernel,
        grid=(steps // block,),
        in_specs=[pl.BlockSpec((block, width), lambda t: (t, 0))] * 2 + [whole(w_row.shape)] * 2,
        out_specs=pl.BlockSpec((block, model), lambda t: (t, 0)),
        out_shape=jax.ShapeDtypeStruct((steps, model), BF16),
        compiler_params=params(),
        cost_estimate=cost("layer_output"),
        name="layer_output",
    )(attn_row, attn_col, w_row, w_col)


def weight_kernel(factor, core_ref, attn_ref, cot_ref, keep_ref, send_ref):
    product = dot(attn_ref[...], cot_ref[...], 0, 0) * factor
    first = core_ref[0] == 0
    for n in range(keep_ref.shape[0]):
        even = product[2 * n * DH : (2 * n + 1) * DH]
        odd = product[(2 * n + 1) * DH : (2 * n + 2) * DH]
        keep_ref[n] = jnp.where(first, even, odd)
        send_ref[n] = jnp.where(first, odd, even).astype(BF16)


def weight_part(core, attn, cotangent, factor, name):
    steps, width = attn.shape
    model = cotangent.shape[1]
    block = min(2 * BLOCK, model)
    pairs = width // DH // 2
    out = pl.BlockSpec((pairs, DH, block), lambda n: (0, 0, n))
    return pl.pallas_call(
        functools.partial(weight_kernel, factor),
        grid=(model // block,),
        in_specs=[
            pl.BlockSpec(memory_space=pltpu.SMEM),
            whole((steps, width)),
            pl.BlockSpec((steps, block), lambda n: (0, n)),
        ],
        out_specs=[out, out],
        out_shape=[
            jax.ShapeDtypeStruct((pairs, DH, model), F32),
            jax.ShapeDtypeStruct((pairs, DH, model), BF16),
        ],
        compiler_params=params(),
        cost_estimate=cost(name),
        name=name,
    )(core, attn, cotangent)


def flip(array, axis, bits, size):
    return lax.ppermute(array, axis, [(n, n ^ bits) for n in range(size)])


def after(member, *others):
    return lax.optimization_barrier((member, *others))[0]


def gather_plane(shard, seq_size):
    pairs = seq_size // 2
    near = [shard] + [flip(shard, "seq", 2 * d, seq_size) for d in range(1, pairs)]
    close, far = jnp.stack(near[: pairs // 2]), jnp.stack(near[pairs // 2 :])
    upper = lax.axis_index("seq") // 2 >= pairs // 2
    return near[1:], jnp.where(upper, close, far), jnp.where(upper, far, close)


def gather_dp(mine, dp_size):
    return [mine] + [flip(mine, "dp", e, dp_size) for e in range(1, dp_size)]


def gather_core(column, seq_size):
    return column + [flip(member, "seq", 1, seq_size) for member in column]


def piece_places(rows, seq_size, dp_size):
    me = lax.axis_index("seq")
    half = seq_size // 4
    c = (jnp.arange(2) ^ (me % 2))[:, None, None]
    z = (jnp.arange(dp_size) ^ lax.axis_index("dp"))[None, :, None]
    pair = (jnp.arange(half) ^ (me // 2 % half))[None, None, :]
    return (((pair * 2 + c) * dp_size + z) * rows).reshape(-1).astype(jnp.int32)


def dp_pieces(keep, received, dp_size):
    pairs, _, model = keep.shape
    depth = lax.axis_index("dp")
    rows = DH // dp_size
    own = keep.reshape(pairs, dp_size, rows, model)
    other = received.reshape(pairs, dp_size, rows, model)

    def part(e):
        at = depth ^ e
        return lax.dynamic_index_in_dim(own, at, 1, False) + lax.dynamic_index_in_dim(
            other, at, 1, False
        ).astype(F32)

    return part(0), [part(e).astype(BF16) for e in range(1, dp_size)]


def send_over_dp(pieces, dp_size):
    return [flip(piece, "dp", e, dp_size) for e, piece in enumerate(pieces, 1)]


def sum_up(own, arrived):
    return functools.reduce(jnp.add, [member.astype(F32) for member in arrived], own)


def scatter_over_seq(parts, seq_size):
    pair = lax.axis_index("seq") // 2
    total = lax.dynamic_index_in_dim(parts, pair, 0, False)
    for d in range(1, seq_size // 2):
        piece = lax.dynamic_index_in_dim(parts, pair ^ d, 0, False).astype(BF16)
        total = total + flip(piece, "seq", 2 * d, seq_size).astype(F32)
    return total


def body(queries, keys, values, out_weight, cotangent):
    seq_size, dp_size = lax.axis_size("seq"), lax.axis_size("dp")
    shape, cot_shape = queries.shape, cotangent.shape
    queries, keys, values, cotangent = [
        member.reshape(-1, member.shape[-1]) for member in (queries, keys, values, cotangent)
    ]
    steps = queries.shape[0]
    model = cotangent.shape[1]
    rows = out_weight.shape[0]
    factor = 1.0 / math.sqrt(steps * seq_size * dp_size)
    core = (lax.axis_index("seq") % 2).reshape(1).astype(jnp.int32)
    staged = seq_size == ROW_HEADS + COL_HEADS and rows % 16 == 0

    def exchange(member):
        return lax.all_to_all(member, "seq", split_axis=0, concat_axis=0, tiled=True)

    packed = pack(queries, keys, values, seq_size)
    if not staged:
        place = jnp.zeros((1,), jnp.int32)
        full = lax.all_gather(out_weight, ("seq", "dp"), axis=0, tiled=True)
        row_pieces, col_pieces = [full[None, :ROW_WIDTH]], [full[None, ROW_WIDTH:]]
        row_near = []
    else:
        place = piece_places(rows, seq_size, dp_size)
        near, col_mine, row_mine = gather_plane(out_weight, seq_size)
        packed = after(packed, *near)
        queries_then = after(queries, col_mine)
    arrived = exchange(packed)
    attn_row = row_forward(queries_then if staged else queries, keys, values)
    row_keep, row_send = weight_part(core, attn_row, cotangent, factor, "weight_row")
    if staged:
        col_depth = gather_dp(col_mine, dp_size)
        col_pieces = gather_core([after(member, row_send) for member in col_depth], seq_size)
        row_depth = gather_dp(after(row_mine, *col_depth), dp_size)
        row_near = row_depth[1:2]
        row_received = flip(after(row_send, *col_pieces), "seq", 1, seq_size)

    up_col, w_col = upstream_of(place, col_pieces, cotangent, "upstream_col")
    up_arrived = exchange(after(up_col, arrived).reshape(seq_size, -1, COL_WIDTH))
    out_col = column_call(
        column_forward_kernel, after(arrived, up_col, *row_near), None, "column_forward"
    )
    attn_col = exchange(after(out_col, up_arrived)).reshape(steps, COL_WIDTH)
    if staged:
        row_pieces = gather_core([after(member, out_col) for member in row_depth], seq_size)
    if staged:
        row_own, row_out = dp_pieces(row_keep, row_received, dp_size)
        row_sent = send_over_dp([after(piece, *row_depth) for piece in row_out], dp_size)
        up_arrived = after(up_arrived, *row_out, *row_pieces)
    grads_col = column_call(column_backward_kernel, arrived, up_arrived, "column_backward")
    attn_col = after(attn_col, grads_col)
    grads_arrived = exchange(after(grads_col, attn_col))
    if staged:
        attn_col = after(attn_col, *row_sent[:2])
    col_keep, col_send = weight_part(core, attn_col, cotangent, factor, "weight_col")
    then = [col_send]
    if staged:
        col_own, col_out = dp_pieces(col_keep, flip(col_send, "seq", 1, seq_size), dp_size)
        col_sent = send_over_dp(col_out, dp_size)
        then += col_out
    up_row, w_row = upstream_of(place, row_pieces, after(cotangent, *then), "upstream_row")
    dq, dk, dv = row_backward(queries, keys, values, up_row)
    layer_out = layer_output(after(attn_row, dq), attn_col, w_row, w_col)
    if staged:
        row_total = sum_up(row_own, [after(member, layer_out) for member in row_sent])
        col_total = sum_up(col_own, [after(member, layer_out) for member in col_sent])
        weight_grad = scatter_over_seq(jnp.concatenate([row_total, col_total]), seq_size)
    else:
        keep = jnp.stack([row_keep, col_keep])
        send = jnp.stack([row_send, col_send]).astype(F32)
        even, odd = jnp.where(core[0] == 0, keep, send), jnp.where(core[0] == 0, send, keep)
        local = jnp.stack([even, odd], axis=2).reshape(-1, model)
        weight_grad = lax.psum_scatter(local, ("seq", "dp"), scatter_dimension=0, tiled=True)
    dq, dk, dv = unpack(grads_arrived, dq, dk, dv)
    return (
        layer_out.reshape(cot_shape),
        dq.reshape(shape),
        dk.reshape(shape),
        dv.reshape(shape),
        weight_grad,
    )


def solution(mesh):
    tokens = P("dp", "seq", None, None)
    weights = P(("seq", "dp"), None)
    return jax.shard_map(
        body,
        mesh=mesh,
        in_specs=(tokens, tokens, tokens, weights, tokens),
        out_specs=(tokens, tokens, tokens, tokens, weights),
        check_vma=False,
    )
```

time: 394 us -> 168 us (0.43)
  waiting for transfers between devices: 159 us -> 15.1 us
  matrix products: 98 us -> 0 us
  Pallas kernels: 0 us -> 88.2 us
  local copies, waits for them, and re-layouts: 61.1 us -> 4.79 us
  blocking collectives: 20.5 us -> 0 us
  starting transfers between devices: 28.4 us -> 46.6 us
  between operations: 14.4 us -> 0.99 us
    dot_general x32 -> x0, matrix products: 94.4 us -> none  [the longest x5 18.1 us: attend_sets(): jnp.einsum('...lm,...ld->...md', shares_low, upstream_set, preferred_elem...]
    pallas_call x0 -> x11, Pallas kernels: none -> 88.2 us  [the longest x2 22.7 us: column_call(): pl.pallas_call(kernel, grid=(cols // span,), in_specs=[three] if forward...]
    reduce_scatter x1 -> x0, waiting for transfers between devices: 82.1 us -> none  [body(): lax.psum_scatter(jnp.einsum('th,td->hd', attn_flat, flat_cot, preferred_e...]
    all_to_all x7 -> x4, waiting for transfers between devices: 75.8 us -> 3.74 us  [exchange(): lax.all_to_all(member, 'seq', split_axis=0, concat_axis=0, tiled=True)]
    ppermute x0 -> x28, starting transfers between devices: none -> 31 us  [flip(): return lax.ppermute(array, axis, [(n, n ^ bits) for n in range(size)])]
    all_to_all x1 -> x0, blocking collectives: 20.5 us -> none  [body(): lax.all_to_all(column_upstream, 'seq', split_axis=2, concat_axis=1, tiled...]
    reshape x13 -> x0, local copies, waits for them, and re-layouts: 13.9 us -> none  [the longest x8 7.48 us: body(): col_flat = col_member.reshape(seq_count, rows_here, stride, COL_HEADS * DH)]
    unnamed x41 -> x36, local copies, waits for them, and re-layouts: 16.9 us -> 4.18 us
  transfers between devices with their start and end apart: 9 -> 32, of which waited for: 7 -> 5; matrix products, arithmetic and copies ran while one was open for 19% -> 7% of each run, Pallas kernels for 0% -> 47%
where the time goes in v1:
time: 168 us; the launch traced here: 167 us
  Pallas kernels  88.2 us (52%)
  starting transfers between devices  46.6 us (28%)
  waiting for transfers between devices  15.1 us (9%)
  other arithmetic  11.5 us (7%)
  local copies, waits for them, and re-layouts  4.79 us (3%)
    ppermute x28, starting transfers between devices, flip(): return lax.ppermute(array, axis, [(n, n ^ bits) for n in range(size)])  31 us
    pallas_call x2, Pallas kernels, column_call(): pl.pallas_call(kernel, grid=(cols // span,), in_specs=[three] if forward...  22.7 us
    all_to_all x4, starting transfers between devices, exchange(): lax.all_to_all(member, 'seq', split_axis=0, concat_axis=0, tiled=True)  15.6 us
    pallas_call x1, Pallas kernels, row_backward(): pl.pallas_call(row_backward_kernel, grid=(ROW_HEADS,), in_specs=[head] *...  14.1 us
    pallas_call x2, Pallas kernels, upstream_of(): pl.pallas_call(upstream_kernel, grid=(steps // block,), in_specs=[pl.Bloc...  13.8 us
    pallas_call x2, Pallas kernels, weight_part(): pl.pallas_call(functools.partial(weight_kernel, factor), grid=(model // b...  12.7 us
    ppermute x28, waiting for transfers between devices, flip(): return lax.ppermute(array, axis, [(n, n ^ bits) for n in range(size)])  11.3 us
    pallas_call x1, Pallas kernels, row_forward(): pl.pallas_call(row_forward_kernel, grid=(ROW_HEADS,), in_specs=[head] * 3...  9.99 us
  transfers between devices with their start and end apart: 32, of which 5 were waited for; matrix products, arithmetic and copies ran while one was open for 7% of the time, Pallas kernels for 47%

profile of v1, /device:TPU:0, one launch (start us, length us, event | category | flops | bytes accessed | tf_op | source)
XLA Modules:
  0.0 167.2 jit_solution(5739845770239838008)
XLA Ops:
  0.6 3.0 %collective-permute-start = (bf16[32,2048]{1,0:T(8,128)(2,1)}, bf16[32,2048]{1,0:T(8,128)(2,1)S(1)}, u32[]{:S(2)}, u32[]{:S(2)}) collective-permute-start(bf16[32,2048]{1,0:T(8,128)(2,1)} %param.8), channel_id=1, source_target_pairs={{0,8},{4,12},{8,0},{12,4},{16,24},{20,28},{24,16},{28,20},{1,9},{5... | collective-permute-start | bytes 393224 | tf_op jit(solution)/shard_map/ppermute | solution.py:371
  5.2 3.1 %pack.1 = bf16[8,3,128,512]{3,2,1,0:T(8,128)(2,1)} custom-call(bf16[1024,1024]{1,0:T(8,128)(2,1)} %bitcast.137, bf16[1024,1024]{1,0:T(8,128)(2,1)} %bitcast.140, bf16[1024,1024]{1,0:T(8,128)(2,1)} %bitcast.143), custom_call_target="tpu_custom_call" | custom-call | flops 690000000 | tf_op jit(solution)/shard_map/pack/pallas_call | solution.py:179
  8.3 3.3 %collective-permute-done.1 = bf16[32,2048]{1,0:T(8,128)(2,1)S(1)} collective-permute-done((bf16[32,2048]{1,0:T(8,128)(2,1)}, bf16[32,2048]{1,0:T(8,128)(2,1)S(1)}, u32[]{:S(2)}, u32[]{:S(2)}) %collective-permute-start.1) | collective-permute-done | bytes 131104 | tf_op jit(solution)/shard_map/ppermute | solution.py:371
  12.3 3.7 %all-to-all-start = ((bf16[8,3,128,512]{3,2,1,0:T(8,128)(2,1)}), bf16[8,3,128,512]{3,2,1,0:T(8,128)(2,1)S(1)}, u32[]{:S(2)}, u32[]{:S(2)}) async-start(bf16[8,3,128,512]{3,2,1,0:T(8,128)(2,1)} %pack.1), calls=%async_computation | async-start | bytes 6291456 | tf_op jit(solution)/shard_map/all_to_all | solution.py:450
  19.4 2.6 %collective-permute-start.4 = (bf16[2,32,2048]{2,1,0:T(8,128)(2,1)}, bf16[2,32,2048]{2,1,0:T(8,128)(2,1)}, u32[]{:S(2)}, u32[]{:S(2)}) collective-permute-start(bf16[2,32,2048]{2,1,0:T(8,128)(2,1)} %get-tuple-element.53.refs_0_), channel_id=1, source_target_pairs={{0,2},{1,3},{2,0},{3,1},{4,6},{5,7},{6,4},{7,5},{8,10},{9,11},{10,... | collective-permute-start | bytes 786440 | tf_op jit(solution)/shard_map/ppermute | solution.py:371
  22.2 10.0 %row_forward.1.attn_ref.row_ref = bf16[1024,512]{1,0:T(8,128)(2,1)} custom-call(bf16[1024,1024]{1,0:T(8,128)(2,1)} %bitcast.138, bf16[1024,1024]{1,0:T(8,128)(2,1)} %bitcast.141, bf16[1024,1024]{1,0:T(8,128)(2,1)} %bitcast.144), custom_call_target="tpu_custom_call" | custom-call | flops 1150000000 | tf_op jit(solution)/shard_map/row_forward/pallas_call | solution.py:134
  32.2 6.3 %weight_row.1 = (f32[2,128,2048]{2,1,0:T(8,128)}, bf16[2,128,2048]{2,1,0:T(8,128)(2,1)}) custom-call(s32[1]{0:T(128)} %bitcast.7.core_ref, bf16[1024,512]{1,0:T(8,128)(2,1)} %row_forward.1.attn_ref.row_ref, bf16[1024,2048]{1,0:T(8,128)(2,1)} %bitcast.133), custom_call_target="tpu_custom_call" | custom-call | flops 690000000 | tf_op jit(solution)/shard_map/weight_row/pallas_call | solution.py:351
  41.5 4.8 %collective-permute-start.10 = (bf16[2,32,2048]{2,1,0:T(8,128)(2,1)S(1)}, bf16[2,32,2048]{2,1,0:T(8,128)(2,1)}, u32[]{:S(2)}, u32[]{:S(2)}) collective-permute-start(bf16[2,32,2048]{2,1,0:T(8,128)(2,1)S(1)} %get-tuple-element.59.refs_0_), channel_id=1, source_target_pairs={{0,1},{1,0},{2,3},{3,2},{4,5},{5,4},{6,7},{7,6},{8,9},{9,8},{10,11... | collective-permute-start | bytes 786440 | tf_op jit(solution)/shard_map/ppermute | solution.py:371
  49.6 6.9 %upstream_col.1 = (bf16[1024,512]{1,0:T(8,128)(2,1)}, bf16[512,2048]{1,0:T(8,128)(2,1)}) custom-call(s32[16]{0:T(128)} %mul.26.place_ref, bf16[2,32,2048]{2,1,0:T(8,128)(2,1)} %get-tuple-element.53.refs_0_, bf16[2,32,2048]{2,1,0:T(8,128)(2,1)} %collective-permute-done.3.refs_1_, bf16[2,32,2048]{2,1,0:T(8,128)(2,1)} %collective-permute-done.4.refs_2_, ...), custom_call_target="tpu_custom_call" | custom-call | flops 805000000 | tf_op jit(solution)/shard_map/upstream_col/pallas_call | solution.py:291
  56.5 4.3 %all-to-all-start.1 = ((bf16[8,128,512]{2,1,0:T(8,128)(2,1)}), bf16[8,128,512]{2,1,0:T(8,128)(2,1)}, u32[]{:S(2)}, u32[]{:S(2)}) async-start(bf16[8,128,512]{2,1,0:T(8,128)(2,1)} %bitcast.156), calls=%async_computation.1 | async-start | bytes 2097152 | tf_op jit(solution)/shard_map/all_to_all | solution.py:450
  60.8 11.0 %column_forward.1 = bf16[8,128,512]{2,1,0:T(8,128)(2,1)} custom-call(bf16[8,3,128,512]{3,2,1,0:T(8,128)(2,1)} %copy-done.4), custom_call_target="tpu_custom_call" | custom-call | flops 126500003840 | tf_op jit(solution)/shard_map/column_forward/pallas_call | solution.py:258
  72.8 2.5 %fusion.16 = (bf16[2,32,2048]{2,1,0:T(8,128)(2,1)}, bf16[2,32,2048]{2,1,0:T(8,128)(2,1)S(1)}, bf16[2,32,2048]{2,1,0:T(8,128)(2,1)S(1)}) fusion(f32[2,4,32,2048]{3,2,1,0:T(8,128)} %bitcast.149, s32[]{:T(128)S(6)} %select_n.78, bf16[2,4,32,2048]{3,2,1,0:T(8,128)(2,1)} %bitcast.12, s32[]{:T(128)S(6)} %select_n.77, s32[]{:T(128)S(6)} %select_n.76), kind=kLoop, calls=%fused_computation.32 | loop fusion | flops 1179648 | bytes 3145740 | tf_op jit(solution)/shard_map/convert_element_type | solution.py:416
  75.3 3.1 %collective-permute-start.19 = (bf16[2,32,2048]{2,1,0:T(8,128)(2,1)S(1)}, bf16[2,32,2048]{2,1,0:T(8,128)(2,1)S(1)}, u32[]{:S(2)}, u32[]{:S(2)}) collective-permute-start(bf16[2,32,2048]{2,1,0:T(8,128)(2,1)S(1)} %get-tuple-element.70), channel_id=1, source_target_pairs={{0,2},{1,3},{2,0},{3,1},{4,6},{5,7},{6,4},{7,5},{8,10},{9,11},{10,... | collective-permute-start | bytes 786440 | tf_op jit(solution)/shard_map/ppermute | solution.py:371
  79.4 3.9 %all-to-all-start.2 = ((bf16[8,128,512]{2,1,0:T(8,128)(2,1)}), bf16[8,128,512]{2,1,0:T(8,128)(2,1)S(1)}, u32[]{:S(2)}, u32[]{:S(2)}) async-start(bf16[8,128,512]{2,1,0:T(8,128)(2,1)} %column_forward.1), calls=%async_computation.2 | async-start | bytes 2097152 | tf_op jit(solution)/shard_map/all_to_all | solution.py:450
  83.3 11.7 %column_backward.1 = bf16[8,3,128,512]{3,2,1,0:T(8,128)(2,1)} custom-call(bf16[8,3,128,512]{3,2,1,0:T(8,128)(2,1)} %copy-done.4, bf16[8,128,512]{2,1,0:T(8,128)(2,1)} %all-to-all-done.1.u_ref), custom_call_target="tpu_custom_call" | custom-call | flops 138000007168 | tf_op jit(solution)/shard_map/column_backward/pallas_call | solution.py:258
  95.0 3.7 %all-to-all-done.2 = bf16[8,128,512]{2,1,0:T(8,128)(2,1)S(1)} async-done(((bf16[8,128,512]{2,1,0:T(8,128)(2,1)}), bf16[8,128,512]{2,1,0:T(8,128)(2,1)S(1)}, u32[]{:S(2)}, u32[]{:S(2)}) %all-to-all-start.2) | async-done | bytes 1048608 | tf_op jit(solution)/shard_map/all_to_all | solution.py:450
  99.7 6.4 %weight_col.1 = (f32[2,128,2048]{2,1,0:T(8,128)}, bf16[2,128,2048]{2,1,0:T(8,128)(2,1)}) custom-call(s32[1]{0:T(128)} %bitcast.7.core_ref, bf16[1024,512]{1,0:T(8,128)(2,1)} %bitcast.146, bf16[1024,2048]{1,0:T(8,128)(2,1)} %bitcast.135), custom_call_target="tpu_custom_call" | custom-call | flops 690000000 | tf_op jit(solution)/shard_map/weight_col/pallas_call | solution.py:351
  106.2 3.8 %all-to-all-start.3 = ((bf16[8,3,128,512]{3,2,1,0:T(8,128)(2,1)}), bf16[8,3,128,512]{3,2,1,0:T(8,128)(2,1)S(1)}, u32[]{:S(2)}, u32[]{:S(2)}) async-start(bf16[8,3,128,512]{3,2,1,0:T(8,128)(2,1)} %column_backward.1), calls=%async_computation.3 | async-start | bytes 6291456 | tf_op jit(solution)/shard_map/all_to_all | solution.py:450
  117.8 6.9 %upstream_row.1 = (bf16[1024,512]{1,0:T(8,128)(2,1)}, bf16[512,2048]{1,0:T(8,128)(2,1)}) custom-call(s32[16]{0:T(128)} %mul.26.place_ref, bf16[2,32,2048]{2,1,0:T(8,128)(2,1)} %copy-done.5, bf16[2,32,2048]{2,1,0:T(8,128)(2,1)} %collective-permute-done.10.refs_1_, bf16[2,32,2048]{2,1,0:T(8,128)(2,1)} %collective-permute-done.11.refs_2_, ...), custom_call_target="tpu_custom_call" | custom-call | flops 805000000 | tf_op jit(solution)/shard_map/upstream_row/pallas_call | solution.py:291
  124.7 14.1 %row_backward.1 = (bf16[1024,1024]{1,0:T(8,128)(2,1)}, bf16[1024,1024]{1,0:T(8,128)(2,1)}, bf16[1024,1024]{1,0:T(8,128)(2,1)}) custom-call(bf16[1024,1024]{1,0:T(8,128)(2,1)} %bitcast.139, bf16[1024,1024]{1,0:T(8,128)(2,1)} %bitcast.142, bf16[1024,1024]{1,0:T(8,128)(2,1)} %bitcast.145, bf16[1024,512]{1,0:T(8,128)(2,1)} %get-tuple-element.75.u_ref), custom_call_target="tpu_custom_call" | custom-call | flops 1610000000 | tf_op jit(solution)/shard_map/row_backward/pallas_call | solution.py:149
  138.8 8.7 %layer_output.1 = bf16[1024,2048]{1,0:T(8,128)(2,1)} custom-call(bf16[1024,512]{1,0:T(8,128)(2,1)} %row_forward.1.attn_ref.row_ref, bf16[1024,512]{1,0:T(8,128)(2,1)} %bitcast.147, bf16[512,2048]{1,0:T(8,128)(2,1)} %get-tuple-element.78.w_row_ref, bf16[512,2048]{1,0:T(8,128)(2,1)} %get-tuple-element.79.w_col_ref), custom_call_target="tpu_custom_call" | custom-call | flops 1035000000 | tf_op jit(solution)/shard_map/layer_output/pallas_call | solution.py:323
  154.5 2.8 %collective-permute-done.25 = bf16[32,2048]{1,0:T(8,128)(2,1)S(1)} collective-permute-done((bf16[32,2048]{1,0:T(8,128)(2,1)}, bf16[32,2048]{1,0:T(8,128)(2,1)S(1)}, u32[]{:S(2)}, u32[]{:S(2)}) %collective-permute-start.25) | collective-permute-done | bytes 131104 | tf_op jit(solution)/shard_map/ppermute | solution.py:371
  157.3 3.2 %collective-permute-done.26 = bf16[32,2048]{1,0:T(8,128)(2,1)} collective-permute-done((bf16[32,2048]{1,0:T(8,128)(2,1)S(1)}, bf16[32,2048]{1,0:T(8,128)(2,1)}, u32[]{:S(2)}, u32[]{:S(2)}) %collective-permute-start.26) | collective-permute-done | bytes 131104 | tf_op jit(solution)/shard_map/ppermute | solution.py:371
  164.0 3.2 %unpack.1 = (bf16[1024,1024]{1,0:T(8,128)(2,1)}, bf16[1024,1024]{1,0:T(8,128)(2,1)}, bf16[1024,1024]{1,0:T(8,128)(2,1)}) custom-call(bf16[8,3,128,512]{3,2,1,0:T(8,128)(2,1)} %copy-done, bf16[1024,1024]{1,0:T(8,128)(2,1)} %get-tuple-element.76._q, ...), custom_call_target="tpu_custom_call", output_to_operand_aliasing={{0}: (1, {}), {1}: (2, {}), {2}: (3, {})} | custom-call | flops 690000000 | tf_op jit(solution)/shard_map/unpack/pallas_call | solution.py:200
  (99 shorter events, 33.3 us)
Async XLA Ops:
  0.6 7.7 %collective-permute-start = (bf16[32,2048]{1,0:T(8,128)(2,1)}, bf16[32,2048]{1,0:T(8,128)(2,1)S(1)}, u32[]{:S(2)}, u32[]{:S(2)}) collective-permute-start(bf16[32,2048]{1,0:T(8,128)(2,1)} %param.8), channel_id=1, source_target_pairs={{0,8},{4,12},{8,0},{12,4},{16,24},{20,28},{24,16},{28,20},{1,9},{5... | collective-permute-start | bytes 393224 | tf_op jit(solution)/shard_map/ppermute | solution.py:371
  3.6 8.0 %collective-permute-start.1 = (bf16[32,2048]{1,0:T(8,128)(2,1)}, bf16[32,2048]{1,0:T(8,128)(2,1)S(1)}, u32[]{:S(2)}, u32[]{:S(2)}) collective-permute-start(bf16[32,2048]{1,0:T(8,128)(2,1)} %param.8), channel_id=1, source_target_pairs={{0,16},{4,20},{8,24},{12,28},{16,0},{20,4},{24,8},{28,12},{1,17},{... | collective-permute-start | bytes 393224 | tf_op jit(solution)/shard_map/ppermute | solution.py:371
  12.3 44.2 %all-to-all-start = ((bf16[8,3,128,512]{3,2,1,0:T(8,128)(2,1)}), bf16[8,3,128,512]{3,2,1,0:T(8,128)(2,1)S(1)}, u32[]{:S(2)}, u32[]{:S(2)}) async-start(bf16[8,3,128,512]{3,2,1,0:T(8,128)(2,1)} %pack.1), calls=%async_computation | async-start | bytes 6291456 | tf_op jit(solution)/shard_map/all_to_all | solution.py:450
  17.8 20.8 %collective-permute-start.3 = (bf16[2,32,2048]{2,1,0:T(8,128)(2,1)}, bf16[2,32,2048]{2,1,0:T(8,128)(2,1)}, u32[]{:S(2)}, u32[]{:S(2)}) collective-permute-start(bf16[2,32,2048]{2,1,0:T(8,128)(2,1)} %get-tuple-element.53.refs_0_), channel_id=1, source_target_pairs={{0,1},{1,0},{2,3},{3,2},{4,5},{5,4},{6,7},{7,6},{8,9},{9,8},{10,11... | collective-permute-start | bytes 786440 | tf_op jit(solution)/shard_map/ppermute | solution.py:371
  19.4 21.7 %collective-permute-start.4 = (bf16[2,32,2048]{2,1,0:T(8,128)(2,1)}, bf16[2,32,2048]{2,1,0:T(8,128)(2,1)}, u32[]{:S(2)}, u32[]{:S(2)}) collective-permute-start(bf16[2,32,2048]{2,1,0:T(8,128)(2,1)} %get-tuple-element.53.refs_0_), channel_id=1, source_target_pairs={{0,2},{1,3},{2,0},{3,1},{4,6},{5,7},{6,4},{7,5},{8,10},{9,11},{10,... | collective-permute-start | bytes 786440 | tf_op jit(solution)/shard_map/ppermute | solution.py:371
  22.0 19.1 %collective-permute-start.5 = (bf16[2,32,2048]{2,1,0:T(8,128)(2,1)}, bf16[2,32,2048]{2,1,0:T(8,128)(2,1)}, u32[]{:S(2)}, u32[]{:S(2)}) collective-permute-start(bf16[2,32,2048]{2,1,0:T(8,128)(2,1)} %get-tuple-element.53.refs_0_), channel_id=1, source_target_pairs={{0,3},{1,2},{2,1},{3,0},{4,7},{5,6},{6,5},{7,4},{8,11},{9,10},{10,... | collective-permute-start | bytes 786440 | tf_op jit(solution)/shard_map/ppermute | solution.py:371
  38.5 8.5 %collective-permute-start.6 = (bf16[2,32,2048]{2,1,0:T(8,128)(2,1)}, bf16[2,32,2048]{2,1,0:T(8,128)(2,1)}, u32[]{:S(2)}, u32[]{:S(2)}) collective-permute-start(bf16[2,32,2048]{2,1,0:T(8,128)(2,1)} %get-tuple-element.53.refs_0_), channel_id=1, source_target_pairs={{0,4},{4,0},{8,12},{12,8},{16,20},{20,16},{24,28},{28,24},{1,5},{5... | collective-permute-start | bytes 786440 | tf_op jit(solution)/shard_map/ppermute | solution.py:371
  38.5 9.5 %collective-permute-start.7 = (bf16[2,32,2048]{2,1,0:T(8,128)(2,1)}, bf16[2,32,2048]{2,1,0:T(8,128)(2,1)}, u32[]{:S(2)}, u32[]{:S(2)}) collective-permute-start(bf16[2,32,2048]{2,1,0:T(8,128)(2,1)} %collective-permute-done.3.refs_1_), channel_id=1, source_target_pairs={{0,4},{4,0},{8,12},{12,8},{16,20},{20,16},{24,28},{28,24},{1,5},{5... | collective-permute-start | bytes 786440 | tf_op jit(solution)/shard_map/ppermute | solution.py:371
  41.0 8.5 %collective-permute-start.8 = (bf16[2,32,2048]{2,1,0:T(8,128)(2,1)}, bf16[2,32,2048]{2,1,0:T(8,128)(2,1)}, u32[]{:S(2)}, u32[]{:S(2)}) collective-permute-start(bf16[2,32,2048]{2,1,0:T(8,128)(2,1)} %collective-permute-done.4.refs_2_), channel_id=1, source_target_pairs={{0,4},{4,0},{8,12},{12,8},{16,20},{20,16},{24,28},{28,24},{1,5},{5... | collective-permute-start | bytes 786440 | tf_op jit(solution)/shard_map/ppermute | solution.py:371
  41.0 8.5 %collective-permute-start.9 = (bf16[2,32,2048]{2,1,0:T(8,128)(2,1)}, bf16[2,32,2048]{2,1,0:T(8,128)(2,1)}, u32[]{:S(2)}, u32[]{:S(2)}) collective-permute-start(bf16[2,32,2048]{2,1,0:T(8,128)(2,1)} %collective-permute-done.5.refs_3_), channel_id=1, source_target_pairs={{0,4},{4,0},{8,12},{12,8},{16,20},{20,16},{24,28},{28,24},{1,5},{5... | collective-permute-start | bytes 786440 | tf_op jit(solution)/shard_map/ppermute | solution.py:371
  41.5 19.3 %collective-permute-start.10 = (bf16[2,32,2048]{2,1,0:T(8,128)(2,1)S(1)}, bf16[2,32,2048]{2,1,0:T(8,128)(2,1)}, u32[]{:S(2)}, u32[]{:S(2)}) collective-permute-start(bf16[2,32,2048]{2,1,0:T(8,128)(2,1)S(1)} %get-tuple-element.59.refs_0_), channel_id=1, source_target_pairs={{0,1},{1,0},{2,3},{3,2},{4,5},{5,4},{6,7},{7,6},{8,9},{9,8},{10,11... | collective-permute-start | bytes 786440 | tf_op jit(solution)/shard_map/ppermute | solution.py:371
  47.0 25.2 %collective-permute-start.11 = (bf16[2,32,2048]{2,1,0:T(8,128)(2,1)S(1)}, bf16[2,32,2048]{2,1,0:T(8,128)(2,1)}, u32[]{:S(2)}, u32[]{:S(2)}) collective-permute-start(bf16[2,32,2048]{2,1,0:T(8,128)(2,1)S(1)} %get-tuple-element.59.refs_0_), channel_id=1, source_target_pairs={{0,2},{1,3},{2,0},{3,1},{4,6},{5,7},{6,4},{7,5},{8,10},{9,11},{10,... | collective-permute-start | bytes 786440 | tf_op jit(solution)/shard_map/ppermute | solution.py:371
  48.0 23.8 %collective-permute-start.12 = (bf16[2,32,2048]{2,1,0:T(8,128)(2,1)S(1)}, bf16[2,32,2048]{2,1,0:T(8,128)(2,1)}, u32[]{:S(2)}, u32[]{:S(2)}) collective-permute-start(bf16[2,32,2048]{2,1,0:T(8,128)(2,1)S(1)} %get-tuple-element.59.refs_0_), channel_id=1, source_target_pairs={{0,3},{1,2},{2,1},{3,0},{4,7},{5,6},{6,5},{7,4},{8,11},{9,10},{10,... | collective-permute-start | bytes 786440 | tf_op jit(solution)/shard_map/ppermute | solution.py:371
  49.6 23.3 %collective-permute-start.17 = (bf16[2,128,2048]{2,1,0:T(8,128)(2,1)}, bf16[2,128,2048]{2,1,0:T(8,128)(2,1)}, u32[]{:S(2)}, u32[]{:S(2)}) collective-permute-start(bf16[2,128,2048]{2,1,0:T(8,128)(2,1)} %get-tuple-element.66), channel_id=1, source_target_pairs={{0,4},{4,0},{8,12},{12,8},{16,20},{20,16},{24,28},{28,24},{1,5},{5... | collective-permute-start | bytes 3145736 | tf_op jit(solution)/shard_map/ppermute | solution.py:371
  56.5 22.0 %all-to-all-start.1 = ((bf16[8,128,512]{2,1,0:T(8,128)(2,1)}), bf16[8,128,512]{2,1,0:T(8,128)(2,1)}, u32[]{:S(2)}, u32[]{:S(2)}) async-start(bf16[8,128,512]{2,1,0:T(8,128)(2,1)} %bitcast.156), calls=%async_computation.1 | async-start | bytes 2097152 | tf_op jit(solution)/shard_map/all_to_all | solution.py:450
  75.3 23.4 %collective-permute-start.19 = (bf16[2,32,2048]{2,1,0:T(8,128)(2,1)S(1)}, bf16[2,32,2048]{2,1,0:T(8,128)(2,1)S(1)}, u32[]{:S(2)}, u32[]{:S(2)}) collective-permute-start(bf16[2,32,2048]{2,1,0:T(8,128)(2,1)S(1)} %get-tuple-element.70), channel_id=1, source_target_pairs={{0,2},{1,3},{2,0},{3,1},{4,6},{5,7},{6,4},{7,5},{8,10},{9,11},{10,... | collective-permute-start | bytes 786440 | tf_op jit(solution)/shard_map/ppermute | solution.py:371
  78.5 20.3 %collective-permute-start.18 = (bf16[2,32,2048]{2,1,0:T(8,128)(2,1)S(1)}, bf16[2,32,2048]{2,1,0:T(8,128)(2,1)S(1)}, u32[]{:S(2)}, u32[]{:S(2)}) collective-permute-start(bf16[2,32,2048]{2,1,0:T(8,128)(2,1)S(1)} %get-tuple-element.69), channel_id=1, source_target_pairs={{0,1},{1,0},{2,3},{3,2},{4,5},{5,4},{6,7},{7,6},{8,9},{9,8},{10,11... | collective-permute-start | bytes 786440 | tf_op jit(solution)/shard_map/ppermute | solution.py:371
  79.4 19.3 %all-to-all-start.2 = ((bf16[8,128,512]{2,1,0:T(8,128)(2,1)}), bf16[8,128,512]{2,1,0:T(8,128)(2,1)S(1)}, u32[]{:S(2)}, u32[]{:S(2)}) async-start(bf16[8,128,512]{2,1,0:T(8,128)(2,1)} %column_forward.1), calls=%async_computation.2 | async-start | bytes 2097152 | tf_op jit(solution)/shard_map/all_to_all | solution.py:450
  106.2 56.2 %all-to-all-start.3 = ((bf16[8,3,128,512]{3,2,1,0:T(8,128)(2,1)}), bf16[8,3,128,512]{3,2,1,0:T(8,128)(2,1)S(1)}, u32[]{:S(2)}, u32[]{:S(2)}) async-start(bf16[8,3,128,512]{3,2,1,0:T(8,128)(2,1)} %column_backward.1), calls=%async_computation.3 | async-start | bytes 6291456 | tf_op jit(solution)/shard_map/all_to_all | solution.py:450
  110.1 37.4 %collective-permute-start.21 = (bf16[2,32,2048]{2,1,0:T(8,128)(2,1)S(1)}, bf16[2,32,2048]{2,1,0:T(8,128)(2,1)S(1)}, u32[]{:S(2)}, u32[]{:S(2)}) collective-permute-start(bf16[2,32,2048]{2,1,0:T(8,128)(2,1)S(1)} %copy-done.12), channel_id=1, source_target_pairs={{0,3},{1,2},{2,1},{3,0},{4,7},{5,6},{6,5},{7,4},{8,11},{9,10},{10,... | collective-permute-start | bytes 786440 | tf_op jit(solution)/shard_map/ppermute | solution.py:371
  113.4 35.4 %collective-permute-start.22 = (bf16[2,32,2048]{2,1,0:T(8,128)(2,1)S(1)}, bf16[2,32,2048]{2,1,0:T(8,128)(2,1)S(1)}, u32[]{:S(2)}, u32[]{:S(2)}) collective-permute-start(bf16[2,32,2048]{2,1,0:T(8,128)(2,1)S(1)} %get-tuple-element.95), channel_id=1, source_target_pairs={{0,1},{1,0},{2,3},{3,2},{4,5},{5,4},{6,7},{7,6},{8,9},{9,8},{10,11... | collective-permute-start | bytes 786440 | tf_op jit(solution)/shard_map/ppermute | solution.py:371
  114.4 34.4 %collective-permute-start.23 = (bf16[2,32,2048]{2,1,0:T(8,128)(2,1)S(1)}, bf16[2,32,2048]{2,1,0:T(8,128)(2,1)S(1)}, u32[]{:S(2)}, u32[]{:S(2)}) collective-permute-start(bf16[2,32,2048]{2,1,0:T(8,128)(2,1)S(1)} %get-tuple-element.94), channel_id=1, source_target_pairs={{0,2},{1,3},{2,0},{3,1},{4,6},{5,7},{6,4},{7,5},{8,10},{9,11},{10,... | collective-permute-start | bytes 786440 | tf_op jit(solution)/shard_map/ppermute | solution.py:371
  116.4 32.4 %collective-permute-start.24 = (bf16[2,32,2048]{2,1,0:T(8,128)(2,1)S(1)}, bf16[2,32,2048]{2,1,0:T(8,128)(2,1)S(1)}, u32[]{:S(2)}, u32[]{:S(2)}) collective-permute-start(bf16[2,32,2048]{2,1,0:T(8,128)(2,1)S(1)} %get-tuple-element.93), channel_id=1, source_target_pairs={{0,3},{1,2},{2,1},{3,0},{4,7},{5,6},{6,5},{7,4},{8,11},{9,10},{10,... | collective-permute-start | bytes 786440 | tf_op jit(solution)/shard_map/ppermute | solution.py:371
  152.7 7.8 %collective-permute-start.26 = (bf16[32,2048]{1,0:T(8,128)(2,1)S(1)}, bf16[32,2048]{1,0:T(8,128)(2,1)}, u32[]{:S(2)}, u32[]{:S(2)}) collective-permute-start(bf16[32,2048]{1,0:T(8,128)(2,1)S(1)} %get-tuple-element.100), channel_id=1, source_target_pairs={{0,16},{4,20},{8,24},{12,28},{16,0},{20,4},{24,8},{28,12},{1,17},{... | collective-permute-start | bytes 393224 | tf_op jit(solution)/shard_map/ppermute | solution.py:371
  (26 other events, 163.7 us)

commit v2 on v1

v2 whole, which is shorter than its diff:
```python
import functools
import math

import jax
import jax.numpy as jnp
from jax import lax
from jax.experimental import pallas as pl
from jax.experimental.pallas import tpu as pltpu
from jax.sharding import PartitionSpec as P

ROW_HEADS = 4
COL_HEADS = 4
DH = 128
ROW_WIDTH = ROW_HEADS * DH
COL_WIDTH = COL_HEADS * DH
FACTOR = 1.0 / math.sqrt(DH)
EXP_SCALE = FACTOR * math.log2(math.e)
BLOCK = 256
COLUMN_SPAN = 16
SENT_FIRST = 2
LOW = -1e30
BF16 = jnp.bfloat16
F32 = jnp.float32
VMEM = 56 * 1024 * 1024
DECLARED = {
    "pack": 0.6, "unpack": 0.6, "row_forward": 100.0, "row_backward": 1.4, "column_forward": 110.0,
    "column_backward": 120.0, "upstream_col": 70.0, "upstream_row": 0.1, "weight_row": 0.6,
    "weight_col": 0.1, "layer_output": 0.9,
}
DECLARED_FLOPS = 1.15e9


def cost(name):
    return pl.CostEstimate(
        flops=int(DECLARED[name] * DECLARED_FLOPS), transcendentals=0, bytes_accessed=0
    )


def params():
    return pltpu.CompilerParams(vmem_limit_bytes=VMEM)


def dot(a, b, a_dim, b_dim):
    return lax.dot_general(a, b, (((a_dim,), (b_dim,)), ((), ())), preferred_element_type=F32)


def whole(shape):
    return pl.BlockSpec(shape, lambda *_: (0,) * len(shape))


def total_of(members):
    return functools.reduce(jnp.add, members)


def joined(parts):
    parts = [part.astype(BF16) for part in parts]
    return parts[0] if len(parts) == 1 else jnp.concatenate(parts, axis=0)


def softmax_units(units):
    peaks = [
        functools.reduce(jnp.maximum, [jnp.max(s, axis=0, keepdims=True) for s in parts])
        * EXP_SCALE
        for parts in units
    ]
    raised = [
        [jnp.exp2(s * EXP_SCALE - peak) for s in parts] for parts, peak in zip(units, peaks)
    ]
    inverses = [
        1.0 / total_of([jnp.sum(e, axis=0, keepdims=True) for e in parts]) for parts in raised
    ]
    return [[e * inverse for e in parts] for parts, inverse in zip(raised, inverses)]


def forward_units(units, values):
    shares = [joined(parts) for parts in softmax_units(units)]
    results = [dot(value, share, 0, 0) for value, share in zip(values, shares)]
    return [result.T.astype(BF16) for result in results]


def backward_units(units, share_grads, queries, keys, upstreams):
    shares = softmax_units(units)
    row_totals = [
        total_of([jnp.sum(p * g, axis=0, keepdims=True) for p, g in zip(parts, grads)])
        for parts, grads in zip(shares, share_grads)
    ]
    score_lows = [
        joined([p * (g - row_total) for p, g in zip(parts, grads)])
        for parts, grads, row_total in zip(shares, share_grads, row_totals)
    ]
    lows = [joined(parts) for parts in shares]
    query_grads = [dot(key, low, 0, 0).T * FACTOR for key, low in zip(keys, score_lows)]
    key_grads = [dot(low, query, 1, 0) for low, query in zip(score_lows, queries)]
    value_grads = [dot(low, upstream, 1, 0) for low, upstream in zip(lows, upstreams)]
    return query_grads, key_grads, value_grads


def causal_mask(block):
    return lax.broadcasted_iota(jnp.int32, (block, block), 0) <= lax.broadcasted_iota(
        jnp.int32, (block, block), 1
    )


def cut(scores, block):
    before = scores.shape[0] - block
    return [scores[:before], scores[before:]] if before else [scores]


def row_parts(key, query, block):
    parts = cut(dot(key, query, 1, 1), block)
    return parts[:-1] + [jnp.where(causal_mask(block), parts[-1], LOW)]


def head_span(h):
    return slice(h * DH, (h + 1) * DH)


def row_forward_kernel(q_ref, k_ref, v_ref, *refs):
    out_ref = refs[-1]
    steps, width = q_ref.shape
    block = min(BLOCK, steps)
    count = steps // block
    for first in range((count + 1) // 2):
        places = {first, count - 1 - first}
        units = [(i, head_span(h)) for i in sorted(places) for h in range(width // DH)]
        scores = [
            row_parts(
                k_ref[: (i + 1) * block, span], q_ref[i * block : (i + 1) * block, span], block
            )
            for i, span in units
        ]
        results = forward_units(scores, [v_ref[: (i + 1) * block, span] for i, span in units])
        for (i, span), result in zip(units, results):
            out_ref[i * block : (i + 1) * block, span] = result


def row_backward_kernel(q_ref, k_ref, v_ref, u_ref, dq_ref, dk_ref, dv_ref, dk_sum, dv_sum):
    steps = q_ref.shape[0]
    block = min(BLOCK, steps)
    count = steps // block
    order = range(count - 1, -1, -1)
    queries = [q_ref[i * block : (i + 1) * block, :] for i in order]
    upstreams = [u_ref[i * block : (i + 1) * block, :] for i in order]
    keys = [k_ref[: (i + 1) * block, :] for i in order]
    values = [v_ref[: (i + 1) * block, :] for i in order]
    scores = [row_parts(key, query, block) for key, query in zip(keys, queries)]
    share_grads = [
        cut(dot(value, upstream, 1, 1), block) for value, upstream in zip(values, upstreams)
    ]
    query_grads, key_grads, value_grads = backward_units(
        scores, share_grads, queries, keys, upstreams
    )
    for i, grad in zip(order, query_grads):
        dq_ref[i * block : (i + 1) * block, :] = grad.astype(BF16)
    for i, key_grad, value_grad in zip(order, key_grads, value_grads):
        rows = slice(0, (i + 1) * block)
        if i == count - 1:
            dk_sum[...] = key_grad
            dv_sum[...] = value_grad
        else:
            dk_sum[rows, :] += key_grad
            dv_sum[rows, :] += value_grad
    dk_ref[...] = (dk_sum[...] * FACTOR).astype(BF16)
    dv_ref[...] = dv_sum[...].astype(BF16)


def row_forward(queries, keys, values, *others):
    steps = queries.shape[0]
    head = pl.BlockSpec((steps, 2 * DH), lambda h: (0, h))
    return pl.pallas_call(
        row_forward_kernel,
        grid=(ROW_HEADS // 2,),
        in_specs=[head] * 3 + [pl.BlockSpec(memory_space=pl.ANY)] * len(others),
        out_specs=head,
        out_shape=jax.ShapeDtypeStruct((steps, ROW_WIDTH), BF16),
        compiler_params=params(),
        cost_estimate=cost("row_forward"),
        name="row_forward",
    )(queries, keys, values, *others)


def row_backward(queries, keys, values, upstream):
    steps = queries.shape[0]
    head = pl.BlockSpec((steps, DH), lambda h: (0, h))
    return pl.pallas_call(
        row_backward_kernel,
        grid=(ROW_HEADS,),
        in_specs=[head] * 4,
        out_specs=[head] * 3,
        out_shape=[jax.ShapeDtypeStruct(queries.shape, BF16)] * 3,
        scratch_shapes=[pltpu.VMEM((steps, DH), F32)] * 2,
        compiler_params=params(),
        cost_estimate=cost("row_backward"),
        name="row_backward",
    )(queries, keys, values, upstream)


def pack_kernel(q_ref, k_ref, v_ref, out_ref):
    group, _, cols, width = out_ref.shape
    for n, ref in enumerate((q_ref, k_ref, v_ref)):
        out_ref[:, n] = ref[...].reshape(group, cols, width)


def pack_specs(peers, cols):
    group = peers // 2
    return (
        pl.BlockSpec((group * cols, COL_WIDTH), lambda j: (j, ROW_WIDTH // COL_WIDTH)),
        pl.BlockSpec((group, 3, cols, COL_WIDTH), lambda j: (j, 0, 0, 0)),
    )


def pack(queries, keys, values, peers):
    cols = queries.shape[0] // peers
    apart, together = pack_specs(peers, cols)
    return pl.pallas_call(
        pack_kernel,
        grid=(2,),
        in_specs=[apart] * 3,
        out_specs=together,
        out_shape=jax.ShapeDtypeStruct((peers, 3, cols, COL_WIDTH), BF16),
        compiler_params=params(),
        cost_estimate=cost("pack"),
        name="pack",
    )(queries, keys, values)


def unpack_kernel(in_ref, _q, _k, _v, dq_ref, dk_ref, dv_ref):
    for n, ref in enumerate((dq_ref, dk_ref, dv_ref)):
        ref[...] = in_ref[:, n].reshape(ref.shape)


def unpack(packed, dq, dk, dv):
    peers, _, cols, _ = packed.shape
    apart, together = pack_specs(peers, cols)
    anywhere = pl.BlockSpec(memory_space=pl.ANY)
    return pl.pallas_call(
        unpack_kernel,
        grid=(2,),
        in_specs=[together] + [anywhere] * 3,
        out_specs=[apart] * 3,
        out_shape=[jax.ShapeDtypeStruct(dq.shape, BF16)] * 3,
        input_output_aliases={1: 0, 2: 1, 3: 2},
        compiler_params=params(),
        cost_estimate=cost("unpack"),
        name="unpack",
    )(packed, dq, dk, dv)


def column_mask(rows, cols):
    key = lax.broadcasted_iota(jnp.int32, (rows * cols, rows * cols), 0)
    query = lax.broadcasted_iota(jnp.int32, (rows * cols, rows * cols), 1)
    return (key <= query) & (key % cols == query % cols)


def head_tokens(ref, n, unit):
    cols, span = unit
    block = ref[:, cols, span] if n is None else ref[:, n, cols, span]
    return block.reshape(-1, DH)


def column_units(width, span):
    units = [
        (slice(c * span, (c + 1) * span), head_span(h))
        for c in range(width // span)
        for h in range(COL_HEADS)
    ]
    return [units[n : n + 8] for n in range(0, len(units), 8)]


def column_scores(in_ref, units, mask):
    return [
        [jnp.where(mask, dot(head_tokens(in_ref, 1, unit), head_tokens(in_ref, 0, unit), 1, 1), LOW)]
        for unit in units
    ]


def column_forward_kernel(in_ref, out_ref):
    rows, _, width, _ = in_ref.shape
    span = min(COLUMN_SPAN, width)
    mask = column_mask(rows, span)
    for units in column_units(width, span):
        scores = column_scores(in_ref, units, mask)
        results = forward_units(scores, [head_tokens(in_ref, 2, unit) for unit in units])
        for (cols, lanes), result in zip(units, results):
            out_ref[:, cols, lanes] = result.reshape(rows, span, DH)


def column_backward_kernel(in_ref, u_ref, out_ref):
    rows, _, width, _ = in_ref.shape
    span = min(COLUMN_SPAN, width)
    mask = column_mask(rows, span)
    for units in column_units(width, span):
        queries, keys, values = [
            [head_tokens(in_ref, n, unit) for unit in units] for n in range(3)
        ]
        upstreams = [head_tokens(u_ref, None, unit) for unit in units]
        scores = column_scores(in_ref, units, mask)
        share_grads = [[dot(v, u, 1, 1)] for v, u in zip(values, upstreams)]
        grads = backward_units(scores, share_grads, queries, keys, upstreams)
        for (cols, lanes), query_grad, key_grad, value_grad in zip(units, *grads):
            for n, grad in enumerate((query_grad, key_grad * FACTOR, value_grad)):
                out_ref[:, n, cols, lanes] = grad.astype(BF16).reshape(rows, span, DH)


def column_call(kernel, packed, upstream, parts, name):
    rows, _, cols, width = packed.shape
    span = max(min(COLUMN_SPAN, cols), cols // parts)
    three = pl.BlockSpec((rows, 3, span, width), lambda c: (0, 0, c, 0))
    one = pl.BlockSpec((rows, span, width), lambda c: (0, c, 0))
    forward = upstream is None
    return pl.pallas_call(
        kernel,
        grid=(cols // span,),
        in_specs=[three] if forward else [three, one],
        out_specs=one if forward else three,
        out_shape=jax.ShapeDtypeStruct(
            (rows, cols, width) if forward else (rows, 3, cols, width), BF16
        ),
        compiler_params=params(),
        cost_estimate=cost(name),
        name=name,
    )(*((packed,) if forward else (packed, upstream)))


def upstream_kernel(place_ref, *refs):
    *w_refs, cot_ref, up_ref, full_ref = refs
    each, rows, _ = w_refs[0].shape

    @pl.when(pl.program_id(0) == 0)
    def _():
        for n, w_ref in enumerate(w_refs):
            for m in range(each):
                at = pl.multiple_of(place_ref[n * each + m], rows)
                full_ref[pl.ds(at, rows), :] = w_ref[m]

    up_ref[...] = dot(cot_ref[...], full_ref[...], 1, 1).astype(BF16)


def upstream_of(place, pieces, cotangent, name):
    steps, model = cotangent.shape
    each, rows, _ = pieces[0].shape
    width = each * len(pieces) * rows
    block = min(2 * BLOCK, steps)
    return pl.pallas_call(
        upstream_kernel,
        grid=(steps // block,),
        in_specs=[
            pl.BlockSpec(memory_space=pltpu.SMEM),
            *[whole(piece.shape) for piece in pieces],
            pl.BlockSpec((block, model), lambda t: (t, 0)),
        ],
        out_specs=[pl.BlockSpec((block, width), lambda t: (t, 0)), whole((width, model))],
        out_shape=[
            jax.ShapeDtypeStruct((steps, width), BF16),
            jax.ShapeDtypeStruct((width, model), BF16),
        ],
        compiler_params=params(),
        cost_estimate=cost(name),
        name=name,
    )(place, *pieces, cotangent)


def layer_kernel(row_ref, col_ref, w_row_ref, w_col_ref, out_ref):
    out_ref[...] = (
        dot(row_ref[...], w_row_ref[...], 1, 0) + dot(col_ref[...], w_col_ref[...], 1, 0)
    ).astype(BF16)


def layer_output(attn_row, attn_col, w_row, w_col):
    steps, width = attn_row.shape
    model = w_row.shape[1]
    block = min(BLOCK, steps)
    return pl.pallas_call(
        layer_kernel,
        grid=(steps // block,),
        in_specs=[pl.BlockSpec((block, width), lambda t: (t, 0))] * 2 + [whole(w_row.shape)] * 2,
        out_specs=pl.BlockSpec((block, model), lambda t: (t, 0)),
        out_shape=jax.ShapeDtypeStruct((steps, model), BF16),
        compiler_params=params(),
        cost_estimate=cost("layer_output"),
        name="layer_output",
    )(attn_row, attn_col, w_row, w_col)


def weight_kernel(factor, core_ref, attn_ref, cot_ref, keep_ref, send_ref):
    depths, pairs, rows, _ = keep_ref.shape
    product = dot(attn_ref[...], cot_ref[...], 0, 0) * factor
    first = core_ref[0] == 0
    for n in range(pairs):
        for z in range(depths):
            even, odd = [
                product[head * DH + z * rows : head * DH + (z + 1) * rows]
                for head in (2 * n, 2 * n + 1)
            ]
            keep_ref[z, n] = jnp.where(first, even, odd)
            send_ref[z, n] = jnp.where(first, odd, even).astype(send_ref.dtype)


def weight_parts(core, attn, cotangent, factor, depths, dtype, name):
    steps, width = attn.shape
    model = cotangent.shape[1]
    block = min(512, model)
    shape = (depths, width // DH // 2, DH // depths, model)
    out = pl.BlockSpec(shape[:-1] + (block,), lambda n: (0, 0, 0, n))
    return pl.pallas_call(
        functools.partial(weight_kernel, factor),
        grid=(model // block,),
        in_specs=[
            pl.BlockSpec(memory_space=pltpu.SMEM),
            whole((steps, width)),
            pl.BlockSpec((steps, block), lambda n: (0, n)),
        ],
        out_specs=[out, out],
        out_shape=[jax.ShapeDtypeStruct(shape, F32), jax.ShapeDtypeStruct(shape, dtype)],
        compiler_params=params(),
        cost_estimate=cost(name),
        name=name,
    )(core, attn, cotangent)


def flip(array, axis, bits, size):
    return lax.ppermute(array, axis, [(n, n ^ bits) for n in range(size)])


def after(member, *others):
    return lax.optimization_barrier((member, *others))[0]


def over_dp(pieces, dp_size):
    return [flip(piece, "dp", e, dp_size) for e, piece in enumerate(pieces, 1)]


def over_core(member, seq_size):
    return flip(member, "seq", 1, seq_size)


def over_plane(pieces, seq_size):
    return [flip(piece, "seq", 2 * d, seq_size) for d, piece in enumerate(pieces, 1)]


def gather_plane(shard, seq_size):
    pairs = seq_size // 2
    near = [shard, *over_plane([shard] * (pairs - 1), seq_size)]
    close, far = jnp.stack(near[: pairs // 2]), jnp.stack(near[pairs // 2 :])
    upper = lax.axis_index("seq") // 2 >= pairs // 2
    return jnp.where(upper, close, far), jnp.where(upper, far, close)


def piece_places(rows, seq_size, dp_size):
    me = lax.axis_index("seq")
    half = seq_size // 4
    c = (jnp.arange(2) ^ (me % 2))[:, None, None]
    z = (jnp.arange(dp_size) ^ lax.axis_index("dp"))[None, :, None]
    pair = (jnp.arange(half) ^ (me // 2 % half))[None, None, :]
    return (((pair * 2 + c) * dp_size + z) * rows).reshape(-1).astype(jnp.int32)


def cut_up(addends, me):
    def part(n):
        return functools.reduce(
            jnp.add,
            [lax.dynamic_index_in_dim(a, me ^ n, 0, False).astype(F32) for a in addends],
        )

    return part(0), [part(n).astype(BF16) for n in range(1, addends[0].shape[0])]


def sum_up(own, arrived):
    return functools.reduce(jnp.add, [member.astype(F32) for member in arrived], own)


def body(queries, keys, values, out_weight, cotangent):
    seq_size, dp_size = lax.axis_size("seq"), lax.axis_size("dp")
    shape, cot_shape = queries.shape, cotangent.shape
    queries, keys, values, cotangent = [
        member.reshape(-1, member.shape[-1]) for member in (queries, keys, values, cotangent)
    ]
    steps = queries.shape[0]
    model = cotangent.shape[1]
    rows = out_weight.shape[0]
    factor = 1.0 / math.sqrt(steps * seq_size * dp_size)
    core = (lax.axis_index("seq") % 2).reshape(1).astype(jnp.int32)
    staged = seq_size == ROW_HEADS + COL_HEADS and rows % 16 == 0

    def exchange(member):
        return lax.all_to_all(member, "seq", split_axis=0, concat_axis=0, tiled=True)

    def weights(attn, name):
        return weight_parts(core, attn, cotangent, factor, dp_size, BF16, name)

    packed = pack(queries, keys, values, seq_size)
    arrived = exchange(packed)
    if staged:
        pair, depth = lax.axis_index("seq") // 2, lax.axis_index("dp")
        place = piece_places(rows, seq_size, dp_size)
        col_mine, row_mine = gather_plane(out_weight, seq_size)
        col_depth = [col_mine, *over_dp([col_mine] * (dp_size - 1), dp_size)]
        attn_row = row_forward(queries, keys, values, packed, col_mine)
        row_keep, row_send = weights(attn_row, "weight_row")
        col_depth = [after(member, row_keep) for member in col_depth]
        col_pieces = col_depth + [over_core(member, seq_size) for member in col_depth]
        row_received = over_core(after(row_send, *col_pieces), seq_size)
        row_mine = after(row_mine, *col_depth)
        row_depth = [row_mine, *over_dp([row_mine] * (dp_size - 1), dp_size)]
        arrived = after(arrived, row_keep)
        then = [row_depth[1]]
    else:
        place = jnp.zeros((1,), jnp.int32)
        full = lax.all_gather(out_weight, ("seq", "dp"), axis=0, tiled=True)
        row_pieces, col_pieces = [full[None, :ROW_WIDTH]], [full[None, ROW_WIDTH:]]
        attn_row = row_forward(queries, keys, values)
        then = []

    out_col = column_call(column_forward_kernel, arrived, None, 2, "column_forward")
    attn_col = exchange(out_col).reshape(steps, COL_WIDTH)
    up_col, w_col = upstream_of(
        place, col_pieces, after(cotangent, out_col, *then), "upstream_col"
    )
    then = []
    if staged:
        row_own, row_out = cut_up((row_keep, after(row_received, up_col)), depth)
        row_pieces = row_depth + [
            over_core(after(member, up_col), seq_size) for member in row_depth
        ]
        then = row_depth + row_out
    up_arrived = exchange(after(up_col, attn_col, *then).reshape(seq_size, -1, COL_WIDTH))
    then = []
    if staged:
        row_sent = over_dp([after(piece, *row_depth) for piece in row_out], dp_size)
        col_keep, col_send = weights(attn_col, "weight_col")
        col_received = over_core(col_send, seq_size)
        then = [col_keep]
    up_row, w_row = upstream_of(place, row_pieces, after(cotangent, *then), "upstream_row")
    then = [up_row, *row_sent[:SENT_FIRST]] if staged else [up_row]
    up_arrived = after(up_arrived, *then)
    grads_col = column_call(column_backward_kernel, arrived, up_arrived, 4, "column_backward")
    grads_arrived = exchange(grads_col)
    then = [grads_col]
    if staged:
        col_own, col_out = cut_up((after(col_keep, grads_col), col_received), depth)
        col_sent = over_dp(col_out, dp_size)
        then = col_out
    dq, dk, dv = row_backward(queries, keys, values, after(up_row, *then))
    layer_out = layer_output(after(attn_row, dq), attn_col, w_row, w_col)
    if staged:
        row_total = sum_up(row_own, [after(member, layer_out) for member in row_sent])
        col_total = sum_up(col_own, [after(member, layer_out) for member in col_sent])
        own, out = cut_up((jnp.concatenate([row_total, col_total]),), pair)
        sent = over_plane(out, seq_size)
        dq, dk, dv = unpack(after(grads_arrived, *out), dq, dk, dv)
        weight_grad = sum_up(own, [after(member, dq) for member in sent])
    else:
        local = []
        for member, name in ((attn_row, "weight_row"), (attn_col, "weight_col")):
            even, odd = weight_parts(
                jnp.zeros((1,), jnp.int32), member, cotangent, factor, 1, F32, name
            )
            local.append(jnp.stack([even[0], odd[0]], axis=1).reshape(-1, model))
        weight_grad = lax.psum_scatter(
            jnp.concatenate(local), ("seq", "dp"), scatter_dimension=0, tiled=True
        )
        dq, dk, dv = unpack(grads_arrived, dq, dk, dv)
    return (
        layer_out.reshape(cot_shape),
        dq.reshape(shape),
        dk.reshape(shape),
        dv.reshape(shape),
        weight_grad,
    )


def solution(mesh):
    tokens = P("dp", "seq", None, None)
    weights = P(("seq", "dp"), None)
    return jax.shard_map(
        body,
        mesh=mesh,
        in_specs=(tokens, tokens, tokens, weights, tokens),
        out_specs=(tokens, tokens, tokens, tokens, weights),
        check_vma=False,
    )
```

time: 168 us -> 161 us (0.958)
  Pallas kernels: 88.2 us -> 69.9 us
  waiting for transfers between devices: 15.1 us -> 28.1 us
  starting transfers between devices: 46.6 us -> 43.7 us
    pallas_call x2, Pallas kernels: 22.7 us -> 10.7 us  [column_call(): pl.pallas_call(kernel, grid=(cols // span,), in_specs=[three] if forward...]
    ppermute x28, waiting for transfers between devices: 11.3 us -> 20.6 us  [flip(): return lax.ppermute(array, axis, [(n, n ^ bits) for n in range(size)])]
    all_to_all x4, waiting for transfers between devices: 3.74 us -> 7.53 us  [exchange(): lax.all_to_all(member, 'seq', split_axis=0, concat_axis=0, tiled=True)]
    pallas_call x3, Pallas kernels: 22.7 us -> 19.5 us  [the longest x2 12.6 us: weight_parts(): pl.pallas_call(functools.partial(weight_kernel, factor), grid=(model // b...]
    ppermute x28, starting transfers between devices: 31 us -> 28.2 us  [flip(): return lax.ppermute(array, axis, [(n, n ^ bits) for n in range(size)])]
    pallas_call x1, Pallas kernels: 14.1 us -> 12.2 us  [row_backward(): pl.pallas_call(row_backward_kernel, grid=(ROW_HEADS,), in_specs=[head] *...]
    add x1 -> x0, other arithmetic: 1.83 us -> none  [scatter_over_seq(): total = total + flip(piece, 'seq', 2 * d, seq_size).astype(F32)]
    add x2 -> x3, other arithmetic: 2.69 us -> 4.27 us  [sum_up(): functools.reduce(jnp.add, [member.astype(F32) for member in arrived], own)]
  transfers between devices with their start and end apart: 32 -> 32, of which waited for: 5 -> 8; matrix products, arithmetic and copies ran while one was open for 7% -> 6% of each run, Pallas kernels for 47% -> 44%
where the time goes in v2:
time: 161 us; the launch traced here: 160 us
  Pallas kernels  69.9 us (43%)
  starting transfers between devices  43.7 us (27%)
  waiting for transfers between devices  28.1 us (17%)
  other arithmetic  10.8 us (7%)
  local copies, waits for them, and re-layouts  6.39 us (4%)
    ppermute x28, starting transfers between devices, flip(): return lax.ppermute(array, axis, [(n, n ^ bits) for n in range(size)])  28.2 us
    ppermute x28, waiting for transfers between devices, flip(): return lax.ppermute(array, axis, [(n, n ^ bits) for n in range(size)])  20.6 us
    all_to_all x4, starting transfers between devices, exchange(): lax.all_to_all(member, 'seq', split_axis=0, concat_axis=0, tiled=True)  15.6 us
    pallas_call x2, Pallas kernels, weight_parts(): pl.pallas_call(functools.partial(weight_kernel, factor), grid=(model // b...  12.6 us
    pallas_call x2, Pallas kernels, upstream_of(): pl.pallas_call(upstream_kernel, grid=(steps // block,), in_specs=[pl.Bloc...  12.5 us
    pallas_call x1, Pallas kernels, row_backward(): pl.pallas_call(row_backward_kernel, grid=(ROW_HEADS,), in_specs=[head] *...  12.2 us
    pallas_call x2, Pallas kernels, column_call(): pl.pallas_call(kernel, grid=(cols // span,), in_specs=[three] if forward...  10.7 us
    pallas_call x1, Pallas kernels, layer_output(): pl.pallas_call(layer_kernel, grid=(steps // block,), in_specs=[pl.BlockSp...  8.66 us
  transfers between devices with their start and end apart: 32, of which 8 were waited for; matrix products, arithmetic and copies ran while one was open for 6% of the time, Pallas kernels for 44%

profile of v2, /device:TPU:0, one launch (start us, length us, event | category | flops | bytes accessed | tf_op | source)
XLA Modules:
  0.0 159.8 jit_solution(4147516859646413035)
XLA Ops:
  0.6 3.0 %collective-permute-start = (bf16[32,2048]{1,0:T(8,128)(2,1)}, bf16[32,2048]{1,0:T(8,128)(2,1)S(1)}, u32[]{:S(2)}, u32[]{:S(2)}) collective-permute-start(bf16[32,2048]{1,0:T(8,128)(2,1)} %param.8), channel_id=1, source_target_pairs={{0,8},{4,12},{8,0},{12,4},{16,24},{20,28},{24,16},{28,20},{1,9},{5... | collective-permute-start | bytes 393224 | tf_op jit(solution)/shard_map/ppermute | solution.py:422
  5.2 3.1 %pack.1.refs_0_ = bf16[8,3,128,512]{3,2,1,0:T(8,128)(2,1)} custom-call(bf16[1024,1024]{1,0:T(8,128)(2,1)} %bitcast.59, bf16[1024,1024]{1,0:T(8,128)(2,1)} %bitcast.62, bf16[1024,1024]{1,0:T(8,128)(2,1)} %bitcast.65), custom_call_target="tpu_custom_call" | custom-call | flops 690000000 | tf_op jit(solution)/shard_map/pack/pallas_call | solution.py:215
  8.3 4.3 %all-to-all-start = ((bf16[8,3,128,512]{3,2,1,0:T(8,128)(2,1)}), bf16[8,3,128,512]{3,2,1,0:T(8,128)(2,1)S(1)}, u32[]{:S(2)}, u32[]{:S(2)}) async-start(bf16[8,3,128,512]{3,2,1,0:T(8,128)(2,1)} %pack.1.refs_0_), calls=%async_computation | async-start | bytes 6291456 | tf_op jit(solution)/shard_map/all_to_all | solution.py:486
  14.7 3.6 %collective-permute-start.5 = (bf16[2,32,2048]{2,1,0:T(8,128)(2,1)}, bf16[2,32,2048]{2,1,0:T(8,128)(2,1)}, u32[]{:S(2)}, u32[]{:S(2)}) collective-permute-start(bf16[2,32,2048]{2,1,0:T(8,128)(2,1)} %get-tuple-element.52.refs_1_.refs_0_), channel_id=1, source_target_pairs={{0,3},{1,2},{2,1},{3,0},{4,7},{5,6},{6,5},{7,4},{8,11},{9,10},{10,... | collective-permute-start | bytes 786440 | tf_op jit(solution)/shard_map/ppermute | solution.py:422
  19.1 6.9 %row_forward.1.attn_ref.row_ref = bf16[1024,512]{1,0:T(8,128)(2,1)} custom-call(bf16[1024,1024]{1,0:T(8,128)(2,1)} %bitcast.60, bf16[1024,1024]{1,0:T(8,128)(2,1)} %bitcast.63, bf16[1024,1024]{1,0:T(8,128)(2,1)} %bitcast.66, bf16[8,3,128,512]{3,2,1,0:T(8,128)(2,1)} %pack.1.refs_0_, bf16[2,32,2048]{2,1,0:T(8,128)(2,1)} %get-tuple-element.52.refs_1_.refs_0_), custom_call_target="tpu_custom_call" | custom-call | flops 115000000512 | tf_op jit(solution)/shard_map/row_forward/pallas_call | solution.py:170
  26.0 6.3 %weight_row.1 = (f32[4,2,32,2048]{3,2,1,0:T(8,128)}, bf16[4,2,32,2048]{3,2,1,0:T(8,128)(2,1)}) custom-call(s32[1]{0:T(128)} %bitcast.7.core_ref, bf16[1024,512]{1,0:T(8,128)(2,1)} %row_forward.1.attn_ref.row_ref, bf16[1024,2048]{1,0:T(8,128)(2,1)} %bitcast.53), custom_call_target="tpu_custom_call" | custom-call | flops 690000000 | tf_op jit(solution)/shard_map/weight_row/pallas_call | solution.py:405
  32.3 9.1 %collective-permute-done.4.refs_2_ = bf16[2,32,2048]{2,1,0:T(8,128)(2,1)} collective-permute-done((bf16[2,32,2048]{2,1,0:T(8,128)(2,1)}, bf16[2,32,2048]{2,1,0:T(8,128)(2,1)}, u32[]{:S(2)}, u32[]{:S(2)}) %collective-permute-start.4) | collective-permute-done | bytes 262176 | tf_op jit(solution)/shard_map/ppermute | solution.py:422
  47.1 3.4 %all-to-all-done.in_ref = bf16[8,3,128,512]{3,2,1,0:T(8,128)(2,1)S(1)} async-done(((bf16[8,3,128,512]{3,2,1,0:T(8,128)(2,1)}), bf16[8,3,128,512]{3,2,1,0:T(8,128)(2,1)S(1)}, u32[]{:S(2)}, u32[]{:S(2)}) %all-to-all-start) | async-done | bytes 3145760 | tf_op jit(solution)/shard_map/all_to_all | solution.py:486
  52.2 4.4 %column_forward.1 = bf16[8,128,512]{2,1,0:T(8,128)(2,1)} custom-call(bf16[8,3,128,512]{3,2,1,0:T(8,128)(2,1)} %copy-done.6), custom_call_target="tpu_custom_call" | custom-call | flops 126500003840 | tf_op jit(solution)/shard_map/column_forward/pallas_call | solution.py:311
  56.5 3.6 %all-to-all-start.1 = ((bf16[8,128,512]{2,1,0:T(8,128)(2,1)}), bf16[8,128,512]{2,1,0:T(8,128)(2,1)S(1)}, u32[]{:S(2)}, u32[]{:S(2)}) async-start(bf16[8,128,512]{2,1,0:T(8,128)(2,1)} %column_forward.1), calls=%async_computation.1 | async-start | bytes 2097152 | tf_op jit(solution)/shard_map/all_to_all | solution.py:486
  60.1 2.9 %collective-permute-done.6.refs_1_ = bf16[2,32,2048]{2,1,0:T(8,128)(2,1)S(1)} collective-permute-done((bf16[2,32,2048]{2,1,0:T(8,128)(2,1)}, bf16[2,32,2048]{2,1,0:T(8,128)(2,1)S(1)}, u32[]{:S(2)}, u32[]{:S(2)}) %collective-permute-start.6) | collective-permute-done | bytes 262176 | tf_op jit(solution)/shard_map/ppermute | solution.py:422
  63.0 6.3 %upstream_col.1 = (bf16[1024,512]{1,0:T(8,128)(2,1)}, bf16[512,2048]{1,0:T(8,128)(2,1)}) custom-call(s32[16]{0:T(128)} %mul.26.place_ref, bf16[2,32,2048]{2,1,0:T(8,128)(2,1)} %get-tuple-element.52.refs_1_.refs_0_, bf16[2,32,2048]{2,1,0:T(8,128)(2,1)} %copy-done.20, bf16[2,32,2048]{2,1,0:T(8,128)(2,1)} %collective-permute-done.4.refs_2_, ...), custom_call_target="tpu_custom_call" | custom-call | flops 80499998720 | tf_op jit(solution)/shard_map/upstream_col/pallas_call | solution.py:344
  71.3 4.1 %all-to-all-done.1 = bf16[8,128,512]{2,1,0:T(8,128)(2,1)S(1)} async-done(((bf16[8,128,512]{2,1,0:T(8,128)(2,1)}), bf16[8,128,512]{2,1,0:T(8,128)(2,1)S(1)}, u32[]{:S(2)}, u32[]{:S(2)}) %all-to-all-start.1) | async-done | bytes 1048608 | tf_op jit(solution)/shard_map/all_to_all | solution.py:486
  75.4 3.6 %all-to-all-start.2 = ((bf16[8,128,512]{2,1,0:T(8,128)(2,1)}), bf16[8,128,512]{2,1,0:T(8,128)(2,1)S(1)}, u32[]{:S(2)}, u32[]{:S(2)}) async-start(bf16[8,128,512]{2,1,0:T(8,128)(2,1)} %bitcast.13), calls=%async_computation.2 | async-start | bytes 2097152 | tf_op jit(solution)/shard_map/all_to_all | solution.py:486
  81.7 2.6 %collective-permute-start.19 = (bf16[2,32,2048]{2,1,0:T(8,128)(2,1)S(1)}, bf16[2,32,2048]{2,1,0:T(8,128)(2,1)S(1)}, u32[]{:S(2)}, u32[]{:S(2)}) collective-permute-start(bf16[2,32,2048]{2,1,0:T(8,128)(2,1)S(1)} %get-tuple-element.72), channel_id=1, source_target_pairs={{0,2},{1,3},{2,0},{3,1},{4,6},{5,7},{6,4},{7,5},{8,10},{9,11},{10,... | collective-permute-start | bytes 786440 | tf_op jit(solution)/shard_map/ppermute | solution.py:422
  84.3 6.3 %weight_col.1 = (f32[4,2,32,2048]{3,2,1,0:T(8,128)}, bf16[4,2,32,2048]{3,2,1,0:T(8,128)(2,1)}) custom-call(s32[1]{0:T(128)} %bitcast.7.core_ref, bf16[1024,512]{1,0:T(8,128)(2,1)} %bitcast.57, bf16[1024,2048]{1,0:T(8,128)(2,1)} %bitcast.55), custom_call_target="tpu_custom_call" | custom-call | flops 115000000 | tf_op jit(solution)/shard_map/weight_col/pallas_call | solution.py:405
  92.1 6.2 %upstream_row.1 = (bf16[1024,512]{1,0:T(8,128)(2,1)}, bf16[512,2048]{1,0:T(8,128)(2,1)}) custom-call(s32[16]{0:T(128)} %mul.26.place_ref, bf16[2,32,2048]{2,1,0:T(8,128)(2,1)} %get-tuple-element.60.refs_0_, bf16[2,32,2048]{2,1,0:T(8,128)(2,1)} %copy-done.13, bf16[2,32,2048]{2,1,0:T(8,128)(2,1)} %collective-permute-done.7.refs_2_, ...), custom_call_target="tpu_custom_call" | custom-call | flops 115000000 | tf_op jit(solution)/shard_map/upstream_row/pallas_call | solution.py:344
  99.3 6.3 %column_backward.1 = bf16[8,3,128,512]{3,2,1,0:T(8,128)(2,1)} custom-call(bf16[8,3,128,512]{3,2,1,0:T(8,128)(2,1)} %copy-done.6, bf16[8,128,512]{2,1,0:T(8,128)(2,1)} %copy-done.8), custom_call_target="tpu_custom_call" | custom-call | flops 138000007168 | tf_op jit(solution)/shard_map/column_backward/pallas_call | solution.py:311
  105.7 4.2 %all-to-all-start.3 = ((bf16[8,3,128,512]{3,2,1,0:T(8,128)(2,1)}), bf16[8,3,128,512]{3,2,1,0:T(8,128)(2,1)S(1)}, u32[]{:S(2)}, u32[]{:S(2)}) async-start(bf16[8,3,128,512]{3,2,1,0:T(8,128)(2,1)} %column_backward.1), calls=%async_computation.3 | async-start | bytes 6291456 | tf_op jit(solution)/shard_map/all_to_all | solution.py:486
  112.6 2.9 %collective-permute-start.24 = (bf16[2,32,2048]{2,1,0:T(8,128)(2,1)S(1)}, bf16[2,32,2048]{2,1,0:T(8,128)(2,1)S(1)}, u32[]{:S(2)}, u32[]{:S(2)}) collective-permute-start(bf16[2,32,2048]{2,1,0:T(8,128)(2,1)S(1)} %get-tuple-element.97), channel_id=1, source_target_pairs={{0,3},{1,2},{2,1},{3,0},{4,7},{5,6},{6,5},{7,4},{8,11},{9,10},{10,... | collective-permute-start | bytes 786440 | tf_op jit(solution)/shard_map/ppermute | solution.py:422
  117.1 12.2 %row_backward.1 = (bf16[1024,1024]{1,0:T(8,128)(2,1)}, bf16[1024,1024]{1,0:T(8,128)(2,1)}, bf16[1024,1024]{1,0:T(8,128)(2,1)}) custom-call(bf16[1024,1024]{1,0:T(8,128)(2,1)} %bitcast.61, bf16[1024,1024]{1,0:T(8,128)(2,1)} %bitcast.64, bf16[1024,1024]{1,0:T(8,128)(2,1)} %bitcast.67, bf16[1024,512]{1,0:T(8,128)(2,1)} %get-tuple-element.76.u_ref), custom_call_target="tpu_custom_call" | custom-call | flops 1610000000 | tf_op jit(solution)/shard_map/row_backward/pallas_call | solution.py:185
  129.3 8.7 %layer_output.1 = bf16[1024,2048]{1,0:T(8,128)(2,1)} custom-call(bf16[1024,512]{1,0:T(8,128)(2,1)} %row_forward.1.attn_ref.row_ref, bf16[1024,512]{1,0:T(8,128)(2,1)} %bitcast.58, bf16[512,2048]{1,0:T(8,128)(2,1)} %get-tuple-element.79.w_row_ref, bf16[512,2048]{1,0:T(8,128)(2,1)} %get-tuple-element.80.w_col_ref), custom_call_target="tpu_custom_call" | custom-call | flops 1035000000 | tf_op jit(solution)/shard_map/layer_output/pallas_call | solution.py:373
  139.2 7.6 %collective-permute-done.23 = bf16[2,32,2048]{2,1,0:T(8,128)(2,1)S(1)} collective-permute-done((bf16[2,32,2048]{2,1,0:T(8,128)(2,1)S(1)}, bf16[2,32,2048]{2,1,0:T(8,128)(2,1)S(1)}, u32[]{:S(2)}, u32[]{:S(2)}) %collective-permute-start.23) | collective-permute-done | bytes 262176 | tf_op jit(solution)/shard_map/ppermute | solution.py:422
  154.0 3.3 %unpack.1 = (bf16[1024,1024]{1,0:T(8,128)(2,1)}, bf16[1024,1024]{1,0:T(8,128)(2,1)}, bf16[1024,1024]{1,0:T(8,128)(2,1)}) custom-call(bf16[8,3,128,512]{3,2,1,0:T(8,128)(2,1)} %copy-done, bf16[1024,1024]{1,0:T(8,128)(2,1)} %get-tuple-element.77._q, ...), custom_call_target="tpu_custom_call", output_to_operand_aliasing={{0}: (1, {}), {1}: (2, {}), {2}: (3, {})} | custom-call | flops 690000000 | tf_op jit(solution)/shard_map/unpack/pallas_call | solution.py:236
  (105 shorter events, 34.3 us)
Async XLA Ops:
  0.6 12.1 %collective-permute-start = (bf16[32,2048]{1,0:T(8,128)(2,1)}, bf16[32,2048]{1,0:T(8,128)(2,1)S(1)}, u32[]{:S(2)}, u32[]{:S(2)}) collective-permute-start(bf16[32,2048]{1,0:T(8,128)(2,1)} %param.8), channel_id=1, source_target_pairs={{0,8},{4,12},{8,0},{12,4},{16,24},{20,28},{24,16},{28,20},{1,9},{5... | collective-permute-start | bytes 393224 | tf_op jit(solution)/shard_map/ppermute | solution.py:422
  3.6 9.1 %collective-permute-start.2 = (bf16[32,2048]{1,0:T(8,128)(2,1)}, bf16[32,2048]{1,0:T(8,128)(2,1)S(1)}, u32[]{:S(2)}, u32[]{:S(2)}) collective-permute-start(bf16[32,2048]{1,0:T(8,128)(2,1)} %param.8), channel_id=1, source_target_pairs={{0,24},{4,28},{8,16},{12,20},{16,8},{20,12},{24,0},{28,4},{1,25},{... | collective-permute-start | bytes 393224 | tf_op jit(solution)/shard_map/ppermute | solution.py:422
  8.3 42.2 %all-to-all-start = ((bf16[8,3,128,512]{3,2,1,0:T(8,128)(2,1)}), bf16[8,3,128,512]{3,2,1,0:T(8,128)(2,1)S(1)}, u32[]{:S(2)}, u32[]{:S(2)}) async-start(bf16[8,3,128,512]{3,2,1,0:T(8,128)(2,1)} %pack.1.refs_0_), calls=%async_computation | async-start | bytes 6291456 | tf_op jit(solution)/shard_map/all_to_all | solution.py:486
  14.7 17.6 %collective-permute-start.5 = (bf16[2,32,2048]{2,1,0:T(8,128)(2,1)}, bf16[2,32,2048]{2,1,0:T(8,128)(2,1)}, u32[]{:S(2)}, u32[]{:S(2)}) collective-permute-start(bf16[2,32,2048]{2,1,0:T(8,128)(2,1)} %get-tuple-element.52.refs_1_.refs_0_), channel_id=1, source_target_pairs={{0,3},{1,2},{2,1},{3,0},{4,7},{5,6},{6,5},{7,4},{8,11},{9,10},{10,... | collective-permute-start | bytes 786440 | tf_op jit(solution)/shard_map/ppermute | solution.py:422
  18.3 23.1 %collective-permute-start.4 = (bf16[2,32,2048]{2,1,0:T(8,128)(2,1)}, bf16[2,32,2048]{2,1,0:T(8,128)(2,1)}, u32[]{:S(2)}, u32[]{:S(2)}) collective-permute-start(bf16[2,32,2048]{2,1,0:T(8,128)(2,1)} %get-tuple-element.52.refs_1_.refs_0_), channel_id=1, source_target_pairs={{0,2},{1,3},{2,0},{3,1},{4,6},{5,7},{6,4},{7,5},{8,10},{9,11},{10,... | collective-permute-start | bytes 786440 | tf_op jit(solution)/shard_map/ppermute | solution.py:422
  18.3 23.1 %collective-permute-start.3 = (bf16[2,32,2048]{2,1,0:T(8,128)(2,1)}, bf16[2,32,2048]{2,1,0:T(8,128)(2,1)S(1)}, u32[]{:S(2)}, u32[]{:S(2)}) collective-permute-start(bf16[2,32,2048]{2,1,0:T(8,128)(2,1)} %get-tuple-element.52.refs_1_.refs_0_), channel_id=1, source_target_pairs={{0,1},{1,0},{2,3},{3,2},{4,5},{5,4},{6,7},{7,6},{8,9},{9,8},{10,11... | collective-permute-start | bytes 786440 | tf_op jit(solution)/shard_map/ppermute | solution.py:422
  32.3 12.9 %collective-permute-start.9 = (bf16[2,32,2048]{2,1,0:T(8,128)(2,1)}, bf16[2,32,2048]{2,1,0:T(8,128)(2,1)}, u32[]{:S(2)}, u32[]{:S(2)}) collective-permute-start(bf16[2,32,2048]{2,1,0:T(8,128)(2,1)} %get-tuple-element.52.refs_1_.refs_0_), channel_id=1, source_target_pairs={{0,4},{4,0},{8,12},{12,8},{16,20},{20,16},{24,28},{28,24},{1,5},{5... | collective-permute-start | bytes 786440 | tf_op jit(solution)/shard_map/ppermute | solution.py:422
  42.7 28.6 %collective-permute-start.8 = (bf16[2,32,2048]{2,1,0:T(8,128)(2,1)}, bf16[2,32,2048]{2,1,0:T(8,128)(2,1)}, u32[]{:S(2)}, u32[]{:S(2)}) collective-permute-start(bf16[2,32,2048]{2,1,0:T(8,128)(2,1)} %get-tuple-element.60.refs_0_), channel_id=1, source_target_pairs={{0,3},{1,2},{2,1},{3,0},{4,7},{5,6},{6,5},{7,4},{8,11},{9,10},{10,... | collective-permute-start | bytes 786440 | tf_op jit(solution)/shard_map/ppermute | solution.py:422
  45.2 26.2 %collective-permute-start.7 = (bf16[2,32,2048]{2,1,0:T(8,128)(2,1)}, bf16[2,32,2048]{2,1,0:T(8,128)(2,1)}, u32[]{:S(2)}, u32[]{:S(2)}) collective-permute-start(bf16[2,32,2048]{2,1,0:T(8,128)(2,1)} %get-tuple-element.60.refs_0_), channel_id=1, source_target_pairs={{0,2},{1,3},{2,0},{3,1},{4,6},{5,7},{6,4},{7,5},{8,10},{9,11},{10,... | collective-permute-start | bytes 786440 | tf_op jit(solution)/shard_map/ppermute | solution.py:422
  45.2 17.8 %collective-permute-start.6 = (bf16[2,32,2048]{2,1,0:T(8,128)(2,1)}, bf16[2,32,2048]{2,1,0:T(8,128)(2,1)S(1)}, u32[]{:S(2)}, u32[]{:S(2)}) collective-permute-start(bf16[2,32,2048]{2,1,0:T(8,128)(2,1)} %get-tuple-element.60.refs_0_), channel_id=1, source_target_pairs={{0,1},{1,0},{2,3},{3,2},{4,5},{5,4},{6,7},{7,6},{8,9},{9,8},{10,11... | collective-permute-start | bytes 786440 | tf_op jit(solution)/shard_map/ppermute | solution.py:422
  47.1 22.2 %collective-permute-start.17 = (bf16[4,2,32,2048]{3,2,1,0:T(8,128)(2,1)}, bf16[4,2,32,2048]{3,2,1,0:T(8,128)(2,1)}, u32[]{:S(2)}, u32[]{:S(2)}) collective-permute-start(bf16[4,2,32,2048]{3,2,1,0:T(8,128)(2,1)} %get-tuple-element.68), channel_id=1, source_target_pairs={{0,4},{4,0},{8,12},{12,8},{16,20},{20,16},{24,28},{28,24},{1,5},{5... | collective-permute-start | bytes 3145736 | tf_op jit(solution)/shard_map/ppermute | solution.py:422
  56.5 18.9 %all-to-all-start.1 = ((bf16[8,128,512]{2,1,0:T(8,128)(2,1)}), bf16[8,128,512]{2,1,0:T(8,128)(2,1)S(1)}, u32[]{:S(2)}, u32[]{:S(2)}) async-start(bf16[8,128,512]{2,1,0:T(8,128)(2,1)} %column_forward.1), calls=%async_computation.1 | async-start | bytes 2097152 | tf_op jit(solution)/shard_map/all_to_all | solution.py:486
  75.4 22.9 %all-to-all-start.2 = ((bf16[8,128,512]{2,1,0:T(8,128)(2,1)}), bf16[8,128,512]{2,1,0:T(8,128)(2,1)S(1)}, u32[]{:S(2)}, u32[]{:S(2)}) async-start(bf16[8,128,512]{2,1,0:T(8,128)(2,1)} %bitcast.13), calls=%async_computation.2 | async-start | bytes 2097152 | tf_op jit(solution)/shard_map/all_to_all | solution.py:486
  79.4 11.2 %collective-permute-start.14 = (bf16[2,32,2048]{2,1,0:T(8,128)(2,1)S(1)}, bf16[2,32,2048]{2,1,0:T(8,128)(2,1)S(1)}, u32[]{:S(2)}, u32[]{:S(2)}) collective-permute-start(bf16[2,32,2048]{2,1,0:T(8,128)(2,1)S(1)} %copy-done.14), channel_id=1, source_target_pairs={{0,4},{4,0},{8,12},{12,8},{16,20},{20,16},{24,28},{28,24},{1,5},{5... | collective-permute-start | bytes 786440 | tf_op jit(solution)/shard_map/ppermute | solution.py:422
  79.6 11.1 %collective-permute-start.15 = (bf16[2,32,2048]{2,1,0:T(8,128)(2,1)}, bf16[2,32,2048]{2,1,0:T(8,128)(2,1)S(1)}, u32[]{:S(2)}, u32[]{:S(2)}) collective-permute-start(bf16[2,32,2048]{2,1,0:T(8,128)(2,1)} %collective-permute-done.7.refs_2_), channel_id=1, source_target_pairs={{0,4},{4,0},{8,12},{12,8},{16,20},{20,16},{24,28},{28,24},{1,5},{5... | collective-permute-start | bytes 786440 | tf_op jit(solution)/shard_map/ppermute | solution.py:422
  79.9 10.8 %collective-permute-start.16 = (bf16[2,32,2048]{2,1,0:T(8,128)(2,1)}, bf16[2,32,2048]{2,1,0:T(8,128)(2,1)S(1)}, u32[]{:S(2)}, u32[]{:S(2)}) collective-permute-start(bf16[2,32,2048]{2,1,0:T(8,128)(2,1)} %collective-permute-done.8.refs_3_), channel_id=1, source_target_pairs={{0,4},{4,0},{8,12},{12,8},{16,20},{20,16},{24,28},{28,24},{1,5},{5... | collective-permute-start | bytes 786440 | tf_op jit(solution)/shard_map/ppermute | solution.py:422
  80.1 18.2 %collective-permute-start.18 = (bf16[2,32,2048]{2,1,0:T(8,128)(2,1)}, bf16[2,32,2048]{2,1,0:T(8,128)(2,1)S(1)}, u32[]{:S(2)}, u32[]{:S(2)}) collective-permute-start(bf16[2,32,2048]{2,1,0:T(8,128)(2,1)} %get-tuple-element.71), channel_id=1, source_target_pairs={{0,1},{1,0},{2,3},{3,2},{4,5},{5,4},{6,7},{7,6},{8,9},{9,8},{10,11... | collective-permute-start | bytes 786440 | tf_op jit(solution)/shard_map/ppermute | solution.py:422
  81.7 16.6 %collective-permute-start.19 = (bf16[2,32,2048]{2,1,0:T(8,128)(2,1)S(1)}, bf16[2,32,2048]{2,1,0:T(8,128)(2,1)S(1)}, u32[]{:S(2)}, u32[]{:S(2)}) collective-permute-start(bf16[2,32,2048]{2,1,0:T(8,128)(2,1)S(1)} %get-tuple-element.72), channel_id=1, source_target_pairs={{0,2},{1,3},{2,0},{3,1},{4,6},{5,7},{6,4},{7,5},{8,10},{9,11},{10,... | collective-permute-start | bytes 786440 | tf_op jit(solution)/shard_map/ppermute | solution.py:422
  90.6 20.3 %collective-permute-start.20 = (bf16[4,2,32,2048]{3,2,1,0:T(8,128)(2,1)}, bf16[4,2,32,2048]{3,2,1,0:T(8,128)(2,1)}, u32[]{:S(2)}, u32[]{:S(2)}) collective-permute-start(bf16[4,2,32,2048]{3,2,1,0:T(8,128)(2,1)} %get-tuple-element.75), channel_id=1, source_target_pairs={{0,4},{4,0},{8,12},{12,8},{16,20},{20,16},{24,28},{28,24},{1,5},{5... | collective-permute-start | bytes 3145736 | tf_op jit(solution)/shard_map/ppermute | solution.py:422
  105.7 46.7 %all-to-all-start.3 = ((bf16[8,3,128,512]{3,2,1,0:T(8,128)(2,1)}), bf16[8,3,128,512]{3,2,1,0:T(8,128)(2,1)S(1)}, u32[]{:S(2)}, u32[]{:S(2)}) async-start(bf16[8,3,128,512]{3,2,1,0:T(8,128)(2,1)} %column_backward.1), calls=%async_computation.3 | async-start | bytes 6291456 | tf_op jit(solution)/shard_map/all_to_all | solution.py:486
  109.8 28.1 %collective-permute-start.21 = (bf16[2,32,2048]{2,1,0:T(8,128)(2,1)S(1)}, bf16[2,32,2048]{2,1,0:T(8,128)(2,1)S(1)}, u32[]{:S(2)}, u32[]{:S(2)}) collective-permute-start(bf16[2,32,2048]{2,1,0:T(8,128)(2,1)S(1)} %get-tuple-element.83), channel_id=1, source_target_pairs={{0,3},{1,2},{2,1},{3,0},{4,7},{5,6},{6,5},{7,4},{8,11},{9,10},{10,... | collective-permute-start | bytes 786440 | tf_op jit(solution)/shard_map/ppermute | solution.py:422
  112.6 26.6 %collective-permute-start.24 = (bf16[2,32,2048]{2,1,0:T(8,128)(2,1)S(1)}, bf16[2,32,2048]{2,1,0:T(8,128)(2,1)S(1)}, u32[]{:S(2)}, u32[]{:S(2)}) collective-permute-start(bf16[2,32,2048]{2,1,0:T(8,128)(2,1)S(1)} %get-tuple-element.97), channel_id=1, source_target_pairs={{0,3},{1,2},{2,1},{3,0},{4,7},{5,6},{6,5},{7,4},{8,11},{9,10},{10,... | collective-permute-start | bytes 786440 | tf_op jit(solution)/shard_map/ppermute | solution.py:422
  115.5 31.3 %collective-permute-start.23 = (bf16[2,32,2048]{2,1,0:T(8,128)(2,1)S(1)}, bf16[2,32,2048]{2,1,0:T(8,128)(2,1)S(1)}, u32[]{:S(2)}, u32[]{:S(2)}) collective-permute-start(bf16[2,32,2048]{2,1,0:T(8,128)(2,1)S(1)} %get-tuple-element.98), channel_id=1, source_target_pairs={{0,2},{1,3},{2,0},{3,1},{4,6},{5,7},{6,4},{7,5},{8,10},{9,11},{10,... | collective-permute-start | bytes 786440 | tf_op jit(solution)/shard_map/ppermute | solution.py:422
  115.5 31.3 %collective-permute-start.22 = (bf16[2,32,2048]{2,1,0:T(8,128)(2,1)S(1)}, bf16[2,32,2048]{2,1,0:T(8,128)(2,1)S(1)}, u32[]{:S(2)}, u32[]{:S(2)}) collective-permute-start(bf16[2,32,2048]{2,1,0:T(8,128)(2,1)S(1)} %get-tuple-element.99), channel_id=1, source_target_pairs={{0,1},{1,0},{2,3},{3,2},{4,5},{5,4},{6,7},{7,6},{8,9},{9,8},{10,11... | collective-permute-start | bytes 786440 | tf_op jit(solution)/shard_map/ppermute | solution.py:422
  (29 other events, 154.0 us)

commit v3 on v2

--- a/solution.py
+++ b/solution.py
@@ -17,6 +17,7 @@
 EXP_SCALE = FACTOR * math.log2(math.e)
 BLOCK = 256
 COLUMN_SPAN = 16
+COLUMN_OUT = jax.ShapeDtypeStruct
 SENT_FIRST = 2
 LOW = -1e30
 BF16 = jnp.bfloat16
@@ -25,7 +26,7 @@
 DECLARED = {
     "pack": 0.6, "unpack": 0.6, "row_forward": 100.0, "row_backward": 1.4, "column_forward": 110.0,
     "column_backward": 120.0, "upstream_col": 70.0, "upstream_row": 0.1, "weight_row": 0.6,
-    "weight_col": 0.1, "layer_output": 0.9,
+    "weight_col": 0.1, "layer_output": 0.9, "plane_pieces": 0.1,
 }
 DECLARED_FLOPS = 1.15e9
 
@@ -38,6 +39,13 @@
 
 def params():
     return pltpu.CompilerParams(vmem_limit_bytes=VMEM)
+
+
+def resident(array):
+    return pltpu.with_memory_space_constraint(array, pltpu.VMEM)
+
+
+RESIDENT = pl.BlockSpec(memory_space=pltpu.VMEM)
 
 
 def dot(a, b, a_dim, b_dim):
@@ -225,25 +233,27 @@
 
 
 def unpack_kernel(in_ref, _q, _k, _v, dq_ref, dk_ref, dv_ref):
+    group = in_ref.shape[0] // pl.num_programs(0)
+    peers = pl.ds(pl.program_id(0) * group, group)
     for n, ref in enumerate((dq_ref, dk_ref, dv_ref)):
-        ref[...] = in_ref[:, n].reshape(ref.shape)
+        ref[...] = in_ref[peers, n].reshape(ref.shape)
 
 
 def unpack(packed, dq, dk, dv):
     peers, _, cols, _ = packed.shape
-    apart, together = pack_specs(peers, cols)
+    apart, _ = pack_specs(peers, cols)
     anywhere = pl.BlockSpec(memory_space=pl.ANY)
     return pl.pallas_call(
         unpack_kernel,
         grid=(2,),
-        in_specs=[together] + [anywhere] * 3,
+        in_specs=[RESIDENT] + [anywhere] * 3,
         out_specs=[apart] * 3,
         out_shape=[jax.ShapeDtypeStruct(dq.shape, BF16)] * 3,
         input_output_aliases={1: 0, 2: 1, 3: 2},
         compiler_params=params(),
         cost_estimate=cost("unpack"),
         name="unpack",
-    )(packed, dq, dk, dv)
+    )(resident(packed), dq, dk, dv)
 
 
 def column_mask(rows, cols):
@@ -258,13 +268,14 @@
     return block.reshape(-1, DH)
 
 
-def column_units(width, span):
+def column_units(rows, width, span):
+    together = max(1, 8 * 128**2 // (rows * span) ** 2)
     units = [
         (slice(c * span, (c + 1) * span), head_span(h))
         for c in range(width // span)
         for h in range(COL_HEADS)
     ]
-    return [units[n : n + 8] for n in range(0, len(units), 8)]
+    return [units[n : n + together] for n in range(0, len(units), together)]
 
 
 def column_scores(in_ref, units, mask):
@@ -278,7 +289,7 @@
     rows, _, width, _ = in_ref.shape
     span = min(COLUMN_SPAN, width)
     mask = column_mask(rows, span)
-    for units in column_units(width, span):
+    for units in column_units(rows, width, span):
         scores = column_scores(in_ref, units, mask)
         results = forward_units(scores, [head_tokens(in_ref, 2, unit) for unit in units])
         for (cols, lanes), result in zip(units, results):
@@ -289,7 +300,7 @@
     rows, _, width, _ = in_ref.shape
     span = min(COLUMN_SPAN, width)
     mask = column_mask(rows, span)
-    for units in column_units(width, span):
+    for units in column_units(rows, width, span):
         queries, keys, values = [
             [head_tokens(in_ref, n, unit) for unit in units] for n in range(3)
         ]
@@ -302,24 +313,20 @@
                 out_ref[:, n, cols, lanes] = grad.astype(BF16).reshape(rows, span, DH)
 
 
-def column_call(kernel, packed, upstream, parts, name):
+def column_call(kernel, packed, upstream, name):
     rows, _, cols, width = packed.shape
-    span = max(min(COLUMN_SPAN, cols), cols // parts)
-    three = pl.BlockSpec((rows, 3, span, width), lambda c: (0, 0, c, 0))
-    one = pl.BlockSpec((rows, span, width), lambda c: (0, c, 0))
     forward = upstream is None
+    shape = (rows, cols, width) if forward else (rows, 3, cols, width)
+    operands = (packed,) if forward else (packed, upstream)
     return pl.pallas_call(
         kernel,
-        grid=(cols // span,),
-        in_specs=[three] if forward else [three, one],
-        out_specs=one if forward else three,
-        out_shape=jax.ShapeDtypeStruct(
-            (rows, cols, width) if forward else (rows, 3, cols, width), BF16
-        ),
+        in_specs=[RESIDENT] * len(operands),
+        out_specs=RESIDENT,
+        out_shape=COLUMN_OUT(shape, BF16),
         compiler_params=params(),
         cost_estimate=cost(name),
         name=name,
-    )(*((packed,) if forward else (packed, upstream)))
+    )(*map(resident, operands))
 
 
 def upstream_kernel(place_ref, *refs):
@@ -467,6 +474,37 @@
 
 def sum_up(own, arrived):
     return functools.reduce(jnp.add, [member.astype(F32) for member in arrived], own)
+
+
+def plane_kernel(pair_ref, *refs):
+    *in_refs, own_ref, out_ref, total_ref = refs
+    half, others = len(in_refs) // 2, out_ref.shape[0]
+    for n in range(2):
+        own, *arrived = in_refs[n * half : (n + 1) * half]
+        rows = slice(n * own.shape[0], (n + 1) * own.shape[0])
+        total_ref[rows] = sum_up(own[...], [ref[...] for ref in arrived])
+    own_ref[...] = total_ref[pair_ref[0]]
+    for d in range(others):
+        out_ref[d] = total_ref[pair_ref[0] ^ (d + 1)].astype(BF16)
+
+
+def plane_pieces(pair, row_own, row_sent, col_own, col_sent):
+    operands = [row_own, *row_sent, col_own, *col_sent]
+    pairs, rows, model = row_own.shape
+    own, out = pl.pallas_call(
+        plane_kernel,
+        in_specs=[pl.BlockSpec(memory_space=pltpu.SMEM)] + [RESIDENT] * len(operands),
+        out_specs=[RESIDENT] * 2,
+        out_shape=[
+            pltpu.VMEM((rows, model), F32),
+            pltpu.VMEM((2 * pairs - 1, rows, model), BF16),
+        ],
+        scratch_shapes=[pltpu.VMEM((2 * pairs, rows, model), F32)],
+        compiler_params=params(),
+        cost_estimate=cost("plane_pieces"),
+        name="plane_pieces",
+    )(pair.reshape(1).astype(jnp.int32), *map(resident, operands))
+    return own, [out[d] for d in range(out.shape[0])]
 
 
 def body(queries, keys, values, out_weight, cotangent):
@@ -511,7 +549,7 @@
         attn_row = row_forward(queries, keys, values)
         then = []
 
-    out_col = column_call(column_forward_kernel, arrived, None, 2, "column_forward")
+    out_col = column_call(column_forward_kernel, arrived, None, "column_forward")
     attn_col = exchange(out_col).reshape(steps, COL_WIDTH)
     up_col, w_col = upstream_of(
         place, col_pieces, after(cotangent, out_col, *then), "upstream_col"
@@ -529,23 +567,28 @@
         row_sent = over_dp([after(piece, *row_depth) for piece in row_out], dp_size)
         col_keep, col_send = weights(attn_col, "weight_col")
         col_received = over_core(col_send, seq_size)
-        then = [col_keep]
-    up_row, w_row = upstream_of(place, row_pieces, after(cotangent, *then), "upstream_row")
-    then = [up_row, *row_sent[:SENT_FIRST]] if staged else [up_row]
+        then = [col_keep, *row_pieces, *row_sent[:SENT_FIRST]]
     up_arrived = after(up_arrived, *then)
-    grads_col = column_call(column_backward_kernel, arrived, up_arrived, 4, "column_backward")
+    grads_col = column_call(column_backward_kernel, arrived, up_arrived, "column_backward")
+    if staged:
+        grads_col = after(grads_col, col_received)
     grads_arrived = exchange(grads_col)
     then = [grads_col]
     if staged:
         col_own, col_out = cut_up((after(col_keep, grads_col), col_received), depth)
         col_sent = over_dp(col_out, dp_size)
         then = col_out
-    dq, dk, dv = row_backward(queries, keys, values, after(up_row, *then))
+    up_row, w_row = upstream_of(place, row_pieces, after(cotangent, *then), "upstream_row")
+    dq, dk, dv = row_backward(queries, keys, values, up_row)
     layer_out = layer_output(after(attn_row, dq), attn_col, w_row, w_col)
     if staged:
-        row_total = sum_up(row_own, [after(member, layer_out) for member in row_sent])
-        col_total = sum_up(col_own, [after(member, layer_out) for member in col_sent])
-        own, out = cut_up((jnp.concatenate([row_total, col_total]),), pair)
+        own, out = plane_pieces(
+            pair,
+            row_own,
+            row_sent,
+            col_own,
+            [after(member, layer_out) for member in col_sent],
+        )
         sent = over_plane(out, seq_size)
         dq, dk, dv = unpack(after(grads_arrived, *out), dq, dk, dv)
         weight_grad = sum_up(own, [after(member, dq) for member in sent])

time: 161 us -> 155 us (0.963)
  local copies, waits for them, and re-layouts: 6.39 us -> 2.84 us
  starting transfers between devices: 43.7 us -> 47 us
  Pallas kernels: 69.9 us -> 67 us
  other arithmetic: 10.8 us -> 8.16 us
    convert_element_type x3 -> x0, other arithmetic: 4.62 us -> none  [cut_up(): part(n).astype(BF16)]
    add x0 -> x2, other arithmetic: none -> 4.51 us  [part(): functools.reduce(jnp.add, [lax.dynamic_index_in_dim(a, me ^ n, 0, False)....]
    unnamed x42 -> x26, local copies, waits for them, and re-layouts: 5.74 us -> 1.44 us
    ppermute x28, waiting for transfers between devices: 20.6 us -> 23.8 us  [flip(): return lax.ppermute(array, axis, [(n, n ^ bits) for n in range(size)])]
    pallas_call x3 -> x4, Pallas kernels: 14 us -> 11.1 us  [the longest x2 8.88 us: column_call(): pl.pallas_call(kernel, in_specs=[RESIDENT] * len(operands), out_specs=RES...]
    all_to_all x4, waiting for transfers between devices: 7.53 us -> 4.76 us  [exchange(): lax.all_to_all(member, 'seq', split_axis=0, concat_axis=0, tiled=True)]
    add x3 -> x1, other arithmetic: 4.27 us -> 1.72 us  [sum_up(): functools.reduce(jnp.add, [member.astype(F32) for member in arrived], own)]
    ppermute x28, starting transfers between devices: 28.2 us -> 30.3 us  [flip(): return lax.ppermute(array, axis, [(n, n ^ bits) for n in range(size)])]
  transfers between devices with their start and end apart: 32 -> 32, of which waited for: 8 -> 10; matrix products, arithmetic and copies ran while one was open for 6% -> 5% of each run, Pallas kernels for 44% -> 43%
where the time goes in v3:
time: 155 us; the launch traced here: 154 us
  Pallas kernels  67 us (43%)
  starting transfers between devices  47 us (30%)
  waiting for transfers between devices  28.6 us (18%)
  other arithmetic  8.16 us (5%)
  local copies, waits for them, and re-layouts  2.84 us (2%)
    ppermute x28, starting transfers between devices, flip(): return lax.ppermute(array, axis, [(n, n ^ bits) for n in range(size)])  30.3 us
    ppermute x28, waiting for transfers between devices, flip(): return lax.ppermute(array, axis, [(n, n ^ bits) for n in range(size)])  23.8 us
    all_to_all x4, starting transfers between devices, exchange(): lax.all_to_all(member, 'seq', split_axis=0, concat_axis=0, tiled=True)  16.7 us
    pallas_call x2, Pallas kernels, weight_parts(): pl.pallas_call(functools.partial(weight_kernel, factor), grid=(model // b...  12.6 us
    pallas_call x2, Pallas kernels, upstream_of(): pl.pallas_call(upstream_kernel, grid=(steps // block,), in_specs=[pl.Bloc...  12.4 us
    pallas_call x1, Pallas kernels, row_backward(): pl.pallas_call(row_backward_kernel, grid=(ROW_HEADS,), in_specs=[head] *...  12.2 us
    pallas_call x2, Pallas kernels, column_call(): pl.pallas_call(kernel, in_specs=[RESIDENT] * len(operands), out_specs=RES...  8.88 us
    pallas_call x1, Pallas kernels, layer_output(): pl.pallas_call(layer_kernel, grid=(steps // block,), in_specs=[pl.BlockSp...  8.69 us
  transfers between devices with their start and end apart: 32, of which 10 were waited for; matrix products, arithmetic and copies ran while one was open for 5% of the time, Pallas kernels for 43%

profile of v3, /device:TPU:0, one launch (start us, length us, event | category | flops | bytes accessed | tf_op | source)
XLA Modules:
  0.0 154.5 jit_solution(7446701548692189890)
XLA Ops:
  0.6 3.0 %collective-permute-start = (bf16[32,2048]{1,0:T(8,128)(2,1)}, bf16[32,2048]{1,0:T(8,128)(2,1)S(1)}, u32[]{:S(2)}, u32[]{:S(2)}) collective-permute-start(bf16[32,2048]{1,0:T(8,128)(2,1)} %param.8), channel_id=1, source_target_pairs={{0,8},{4,12},{8,0},{12,4},{16,24},{20,28},{24,16},{28,20},{1,9},{5... | collective-permute-start | bytes 393224 | tf_op jit(solution)/shard_map/ppermute | solution.py:429
  5.2 3.1 %pack.1.refs_0_ = bf16[8,3,128,512]{3,2,1,0:T(8,128)(2,1)} custom-call(bf16[1024,1024]{1,0:T(8,128)(2,1)} %bitcast.42, bf16[1024,1024]{1,0:T(8,128)(2,1)} %bitcast.45, bf16[1024,1024]{1,0:T(8,128)(2,1)} %bitcast.48), custom_call_target="tpu_custom_call" | custom-call | flops 690000000 | tf_op jit(solution)/shard_map/pack/pallas_call | solution.py:223
  8.3 4.3 %all-to-all-start = ((bf16[8,3,128,512]{3,2,1,0:T(8,128)(2,1)}), bf16[8,3,128,512]{3,2,1,0:T(8,128)(2,1)S(1)}, u32[]{:S(2)}, u32[]{:S(2)}) async-start(bf16[8,3,128,512]{3,2,1,0:T(8,128)(2,1)} %pack.1.refs_0_), calls=%async_computation | async-start | bytes 6291456 | tf_op jit(solution)/shard_map/all_to_all | solution.py:524
  14.7 3.6 %collective-permute-start.5 = (bf16[2,32,2048]{2,1,0:T(8,128)(2,1)}, bf16[2,32,2048]{2,1,0:T(8,128)(2,1)}, u32[]{:S(2)}, u32[]{:S(2)}) collective-permute-start(bf16[2,32,2048]{2,1,0:T(8,128)(2,1)} %get-tuple-element.51.refs_1_.refs_0_), channel_id=1, source_target_pairs={{0,3},{1,2},{2,1},{3,0},{4,7},{5,6},{6,5},{7,4},{8,11},{9,10},{10,... | collective-permute-start | bytes 786440 | tf_op jit(solution)/shard_map/ppermute | solution.py:429
  19.1 6.9 %row_forward.1.attn_ref.row_ref = bf16[1024,512]{1,0:T(8,128)(2,1)} custom-call(bf16[1024,1024]{1,0:T(8,128)(2,1)} %bitcast.43, bf16[1024,1024]{1,0:T(8,128)(2,1)} %bitcast.46, bf16[1024,1024]{1,0:T(8,128)(2,1)} %bitcast.49, bf16[8,3,128,512]{3,2,1,0:T(8,128)(2,1)} %pack.1.refs_0_, bf16[2,32,2048]{2,1,0:T(8,128)(2,1)} %get-tuple-element.51.refs_1_.refs_0_), custom_call_target="tpu_custom_call" | custom-call | flops 115000000512 | tf_op jit(solution)/shard_map/row_forward/pallas_call | solution.py:178
  25.9 6.3 %weight_row.1 = (f32[4,2,32,2048]{3,2,1,0:T(8,128)}, bf16[4,2,32,2048]{3,2,1,0:T(8,128)(2,1)}) custom-call(s32[1]{0:T(128)} %bitcast.7.core_ref, bf16[1024,512]{1,0:T(8,128)(2,1)} %row_forward.1.attn_ref.row_ref, bf16[1024,2048]{1,0:T(8,128)(2,1)} %bitcast.38), custom_call_target="tpu_custom_call" | custom-call | flops 690000000 | tf_op jit(solution)/shard_map/weight_row/pallas_call | solution.py:412
  32.3 9.1 %collective-permute-done.4.refs_2_ = bf16[2,32,2048]{2,1,0:T(8,128)(2,1)} collective-permute-done((bf16[2,32,2048]{2,1,0:T(8,128)(2,1)}, bf16[2,32,2048]{2,1,0:T(8,128)(2,1)}, u32[]{:S(2)}, u32[]{:S(2)}) %collective-permute-start.4) | collective-permute-done | bytes 262176 | tf_op jit(solution)/shard_map/ppermute | solution.py:429
  47.1 3.4 %all-to-all-done.in_ref = bf16[8,3,128,512]{3,2,1,0:T(8,128)(2,1)S(1)} async-done(((bf16[8,3,128,512]{3,2,1,0:T(8,128)(2,1)}), bf16[8,3,128,512]{3,2,1,0:T(8,128)(2,1)S(1)}, u32[]{:S(2)}, u32[]{:S(2)}) %all-to-all-start) | async-done | bytes 3145760 | tf_op jit(solution)/shard_map/all_to_all | solution.py:524
  50.5 2.9 %column_forward.1 = bf16[8,128,512]{2,1,0:T(8,128)(2,1)} custom-call(bf16[8,3,128,512]{3,2,1,0:T(8,128)(2,1)S(1)} %all-to-all-done.in_ref), custom_call_target="tpu_custom_call" | custom-call | flops 126500003840 | tf_op jit(solution)/shard_map/column_forward/pallas_call | solution.py:321
  53.4 4.2 %all-to-all-start.1 = ((bf16[8,128,512]{2,1,0:T(8,128)(2,1)}), bf16[8,128,512]{2,1,0:T(8,128)(2,1)}, u32[]{:S(2)}, u32[]{:S(2)}) async-start(bf16[8,128,512]{2,1,0:T(8,128)(2,1)} %column_forward.1), calls=%async_computation.1 | async-start | bytes 2097152 | tf_op jit(solution)/shard_map/all_to_all | solution.py:524
  57.7 5.3 %collective-permute-done.6.refs_1_ = bf16[2,32,2048]{2,1,0:T(8,128)(2,1)S(1)} collective-permute-done((bf16[2,32,2048]{2,1,0:T(8,128)(2,1)}, bf16[2,32,2048]{2,1,0:T(8,128)(2,1)S(1)}, u32[]{:S(2)}, u32[]{:S(2)}) %collective-permute-start.6) | collective-permute-done | bytes 262176 | tf_op jit(solution)/shard_map/ppermute | solution.py:429
  63.0 6.3 %upstream_col.1 = (bf16[1024,512]{1,0:T(8,128)(2,1)}, bf16[512,2048]{1,0:T(8,128)(2,1)}) custom-call(s32[16]{0:T(128)} %mul.26.place_ref, bf16[2,32,2048]{2,1,0:T(8,128)(2,1)} %get-tuple-element.51.refs_1_.refs_0_, bf16[2,32,2048]{2,1,0:T(8,128)(2,1)} %copy-done.12, bf16[2,32,2048]{2,1,0:T(8,128)(2,1)} %collective-permute-done.4.refs_2_, ...), custom_call_target="tpu_custom_call" | custom-call | flops 80499998720 | tf_op jit(solution)/shard_map/upstream_col/pallas_call | solution.py:351
  73.1 4.3 %all-to-all-start.2 = ((bf16[8,128,512]{2,1,0:T(8,128)(2,1)}), bf16[8,128,512]{2,1,0:T(8,128)(2,1)}, u32[]{:S(2)}, u32[]{:S(2)}) async-start(bf16[8,128,512]{2,1,0:T(8,128)(2,1)} %bitcast.55), calls=%async_computation.2 | async-start | bytes 2097152 | tf_op jit(solution)/shard_map/all_to_all | solution.py:524
  80.0 2.6 %collective-permute-start.19 = (bf16[2,32,2048]{2,1,0:T(8,128)(2,1)}, bf16[2,32,2048]{2,1,0:T(8,128)(2,1)S(1)}, u32[]{:S(2)}, u32[]{:S(2)}) collective-permute-start(bf16[2,32,2048]{2,1,0:T(8,128)(2,1)} %get-tuple-element.69), channel_id=1, source_target_pairs={{0,2},{1,3},{2,0},{3,1},{4,6},{5,7},{6,4},{7,5},{8,10},{9,11},{10,... | collective-permute-start | bytes 786440 | tf_op jit(solution)/shard_map/ppermute | solution.py:429
  82.6 6.3 %weight_col.1 = (f32[4,2,32,2048]{3,2,1,0:T(8,128)}, bf16[4,2,32,2048]{3,2,1,0:T(8,128)(2,1)}) custom-call(s32[1]{0:T(128)} %bitcast.7.core_ref, bf16[1024,512]{1,0:T(8,128)(2,1)} %bitcast.9.attn_ref.col_ref, bf16[1024,2048]{1,0:T(8,128)(2,1)} %bitcast.40), custom_call_target="tpu_custom_call" | custom-call | flops 115000000 | tf_op jit(solution)/shard_map/weight_col/pallas_call | solution.py:412
  89.0 3.6 %collective-permute-done.18.refs_1_ = bf16[2,32,2048]{2,1,0:T(8,128)(2,1)S(1)} collective-permute-done((bf16[2,32,2048]{2,1,0:T(8,128)(2,1)}, bf16[2,32,2048]{2,1,0:T(8,128)(2,1)S(1)}, u32[]{:S(2)}, u32[]{:S(2)}) %collective-permute-start.18) | collective-permute-done | bytes 262176 | tf_op jit(solution)/shard_map/ppermute | solution.py:429
  95.7 6.0 %column_backward.1 = bf16[8,3,128,512]{3,2,1,0:T(8,128)(2,1)} custom-call(bf16[8,3,128,512]{3,2,1,0:T(8,128)(2,1)S(1)} %all-to-all-done.in_ref, bf16[8,128,512]{2,1,0:T(8,128)(2,1)} %all-to-all-done.2.u_ref), custom_call_target="tpu_custom_call" | custom-call | flops 138000007168 | tf_op jit(solution)/shard_map/column_backward/pallas_call | solution.py:321
  101.7 3.9 %all-to-all-start.3 = ((bf16[8,3,128,512]{3,2,1,0:T(8,128)(2,1)}), bf16[8,3,128,512]{3,2,1,0:T(8,128)(2,1)S(1)}, u32[]{:S(2)}, u32[]{:S(2)}) async-start(bf16[8,3,128,512]{3,2,1,0:T(8,128)(2,1)} %column_backward.1), calls=%async_computation.3 | async-start | bytes 6291456 | tf_op jit(solution)/shard_map/all_to_all | solution.py:524
  107.7 3.3 %collective-permute-start.24 = (bf16[2,32,2048]{2,1,0:T(8,128)(2,1)S(1)}, bf16[2,32,2048]{2,1,0:T(8,128)(2,1)S(1)}, u32[]{:S(2)}, u32[]{:S(2)}) collective-permute-start(bf16[2,32,2048]{2,1,0:T(8,128)(2,1)S(1)} %get-tuple-element.96), channel_id=1, source_target_pairs={{0,3},{1,2},{2,1},{3,0},{4,7},{5,6},{6,5},{7,4},{8,11},{9,10},{10,... | collective-permute-start | bytes 786440 | tf_op jit(solution)/shard_map/ppermute | solution.py:429
  112.2 3.2 %collective-permute-start.21 = (bf16[2,32,2048]{2,1,0:T(8,128)(2,1)S(1)}, bf16[2,32,2048]{2,1,0:T(8,128)(2,1)S(1)}, u32[]{:S(2)}, u32[]{:S(2)}) collective-permute-start(bf16[2,32,2048]{2,1,0:T(8,128)(2,1)S(1)} %copy-done.7), channel_id=1, source_target_pairs={{0,3},{1,2},{2,1},{3,0},{4,7},{5,6},{6,5},{7,4},{8,11},{9,10},{10,... | collective-permute-start | bytes 786440 | tf_op jit(solution)/shard_map/ppermute | solution.py:429
  115.4 6.2 %upstream_row.1 = (bf16[1024,512]{1,0:T(8,128)(2,1)}, bf16[512,2048]{1,0:T(8,128)(2,1)}) custom-call(s32[16]{0:T(128)} %mul.26.place_ref, bf16[2,32,2048]{2,1,0:T(8,128)(2,1)} %get-tuple-element.59.refs_0_, bf16[2,32,2048]{2,1,0:T(8,128)(2,1)} %copy-done.6, bf16[2,32,2048]{2,1,0:T(8,128)(2,1)} %collective-permute-done.7.refs_2_, ...), custom_call_target="tpu_custom_call" | custom-call | flops 115000000 | tf_op jit(solution)/shard_map/upstream_row/pallas_call | solution.py:351
  121.5 12.2 %row_backward.1 = (bf16[1024,1024]{1,0:T(8,128)(2,1)}, bf16[1024,1024]{1,0:T(8,128)(2,1)}, bf16[1024,1024]{1,0:T(8,128)(2,1)}) custom-call(bf16[1024,1024]{1,0:T(8,128)(2,1)} %bitcast.44, bf16[1024,1024]{1,0:T(8,128)(2,1)} %bitcast.47, bf16[1024,1024]{1,0:T(8,128)(2,1)} %bitcast.50, bf16[1024,512]{1,0:T(8,128)(2,1)} %get-tuple-element.75.u_ref), custom_call_target="tpu_custom_call" | custom-call | flops 1610000000 | tf_op jit(solution)/shard_map/row_backward/pallas_call | solution.py:193
  133.8 8.7 %layer_output.1 = bf16[1024,2048]{1,0:T(8,128)(2,1)} custom-call(bf16[1024,512]{1,0:T(8,128)(2,1)} %row_forward.1.attn_ref.row_ref, bf16[1024,512]{1,0:T(8,128)(2,1)} %bitcast.9.attn_ref.col_ref, bf16[512,2048]{1,0:T(8,128)(2,1)} %get-tuple-element.78.w_row_ref, bf16[512,2048]{1,0:T(8,128)(2,1)} %get-tuple-element.79.w_col_ref), custom_call_target="tpu_custom_call" | custom-call | flops 1035000000 | tf_op jit(solution)/shard_map/layer_output/pallas_call | solution.py:380
  143.7 2.9 %collective-permute-start.27 = (bf16[32,2048]{1,0:T(8,128)(2,1)}, bf16[32,2048]{1,0:T(8,128)(2,1)S(1)}, u32[]{:S(2)}, u32[]{:S(2)}) collective-permute-start(bf16[32,2048]{1,0:T(8,128)(2,1)} %get-tuple-element.105), channel_id=1, source_target_pairs={{0,24},{4,28},{8,16},{12,20},{16,8},{20,12},{24,0},{28,4},{1,25},{... | collective-permute-start | bytes 393224 | tf_op jit(solution)/shard_map/ppermute | solution.py:429
  (88 shorter events, 32.1 us)
Async XLA Ops:
  0.6 12.1 %collective-permute-start = (bf16[32,2048]{1,0:T(8,128)(2,1)}, bf16[32,2048]{1,0:T(8,128)(2,1)S(1)}, u32[]{:S(2)}, u32[]{:S(2)}) collective-permute-start(bf16[32,2048]{1,0:T(8,128)(2,1)} %param.8), channel_id=1, source_target_pairs={{0,8},{4,12},{8,0},{12,4},{16,24},{20,28},{24,16},{28,20},{1,9},{5... | collective-permute-start | bytes 393224 | tf_op jit(solution)/shard_map/ppermute | solution.py:429
  3.6 9.1 %collective-permute-start.2 = (bf16[32,2048]{1,0:T(8,128)(2,1)}, bf16[32,2048]{1,0:T(8,128)(2,1)S(1)}, u32[]{:S(2)}, u32[]{:S(2)}) collective-permute-start(bf16[32,2048]{1,0:T(8,128)(2,1)} %param.8), channel_id=1, source_target_pairs={{0,24},{4,28},{8,16},{12,20},{16,8},{20,12},{24,0},{28,4},{1,25},{... | collective-permute-start | bytes 393224 | tf_op jit(solution)/shard_map/ppermute | solution.py:429
  8.3 42.2 %all-to-all-start = ((bf16[8,3,128,512]{3,2,1,0:T(8,128)(2,1)}), bf16[8,3,128,512]{3,2,1,0:T(8,128)(2,1)S(1)}, u32[]{:S(2)}, u32[]{:S(2)}) async-start(bf16[8,3,128,512]{3,2,1,0:T(8,128)(2,1)} %pack.1.refs_0_), calls=%async_computation | async-start | bytes 6291456 | tf_op jit(solution)/shard_map/all_to_all | solution.py:524
  14.7 17.6 %collective-permute-start.5 = (bf16[2,32,2048]{2,1,0:T(8,128)(2,1)}, bf16[2,32,2048]{2,1,0:T(8,128)(2,1)}, u32[]{:S(2)}, u32[]{:S(2)}) collective-permute-start(bf16[2,32,2048]{2,1,0:T(8,128)(2,1)} %get-tuple-element.51.refs_1_.refs_0_), channel_id=1, source_target_pairs={{0,3},{1,2},{2,1},{3,0},{4,7},{5,6},{6,5},{7,4},{8,11},{9,10},{10,... | collective-permute-start | bytes 786440 | tf_op jit(solution)/shard_map/ppermute | solution.py:429
  18.3 23.1 %collective-permute-start.4 = (bf16[2,32,2048]{2,1,0:T(8,128)(2,1)}, bf16[2,32,2048]{2,1,0:T(8,128)(2,1)}, u32[]{:S(2)}, u32[]{:S(2)}) collective-permute-start(bf16[2,32,2048]{2,1,0:T(8,128)(2,1)} %get-tuple-element.51.refs_1_.refs_0_), channel_id=1, source_target_pairs={{0,2},{1,3},{2,0},{3,1},{4,6},{5,7},{6,4},{7,5},{8,10},{9,11},{10,... | collective-permute-start | bytes 786440 | tf_op jit(solution)/shard_map/ppermute | solution.py:429
  18.3 23.1 %collective-permute-start.3 = (bf16[2,32,2048]{2,1,0:T(8,128)(2,1)}, bf16[2,32,2048]{2,1,0:T(8,128)(2,1)S(1)}, u32[]{:S(2)}, u32[]{:S(2)}) collective-permute-start(bf16[2,32,2048]{2,1,0:T(8,128)(2,1)} %get-tuple-element.51.refs_1_.refs_0_), channel_id=1, source_target_pairs={{0,1},{1,0},{2,3},{3,2},{4,5},{5,4},{6,7},{7,6},{8,9},{9,8},{10,11... | collective-permute-start | bytes 786440 | tf_op jit(solution)/shard_map/ppermute | solution.py:429
  32.3 12.9 %collective-permute-start.9 = (bf16[2,32,2048]{2,1,0:T(8,128)(2,1)}, bf16[2,32,2048]{2,1,0:T(8,128)(2,1)}, u32[]{:S(2)}, u32[]{:S(2)}) collective-permute-start(bf16[2,32,2048]{2,1,0:T(8,128)(2,1)} %get-tuple-element.51.refs_1_.refs_0_), channel_id=1, source_target_pairs={{0,4},{4,0},{8,12},{12,8},{16,20},{20,16},{24,28},{28,24},{1,5},{5... | collective-permute-start | bytes 786440 | tf_op jit(solution)/shard_map/ppermute | solution.py:429
  42.7 28.9 %collective-permute-start.8 = (bf16[2,32,2048]{2,1,0:T(8,128)(2,1)}, bf16[2,32,2048]{2,1,0:T(8,128)(2,1)}, u32[]{:S(2)}, u32[]{:S(2)}) collective-permute-start(bf16[2,32,2048]{2,1,0:T(8,128)(2,1)} %get-tuple-element.59.refs_0_), channel_id=1, source_target_pairs={{0,3},{1,2},{2,1},{3,0},{4,7},{5,6},{6,5},{7,4},{8,11},{9,10},{10,... | collective-permute-start | bytes 786440 | tf_op jit(solution)/shard_map/ppermute | solution.py:429
  45.2 26.5 %collective-permute-start.7 = (bf16[2,32,2048]{2,1,0:T(8,128)(2,1)}, bf16[2,32,2048]{2,1,0:T(8,128)(2,1)}, u32[]{:S(2)}, u32[]{:S(2)}) collective-permute-start(bf16[2,32,2048]{2,1,0:T(8,128)(2,1)} %get-tuple-element.59.refs_0_), channel_id=1, source_target_pairs={{0,2},{1,3},{2,0},{3,1},{4,6},{5,7},{6,4},{7,5},{8,10},{9,11},{10,... | collective-permute-start | bytes 786440 | tf_op jit(solution)/shard_map/ppermute | solution.py:429
  45.2 17.8 %collective-permute-start.6 = (bf16[2,32,2048]{2,1,0:T(8,128)(2,1)}, bf16[2,32,2048]{2,1,0:T(8,128)(2,1)S(1)}, u32[]{:S(2)}, u32[]{:S(2)}) collective-permute-start(bf16[2,32,2048]{2,1,0:T(8,128)(2,1)} %get-tuple-element.59.refs_0_), channel_id=1, source_target_pairs={{0,1},{1,0},{2,3},{3,2},{4,5},{5,4},{6,7},{7,6},{8,9},{9,8},{10,11... | collective-permute-start | bytes 786440 | tf_op jit(solution)/shard_map/ppermute | solution.py:429
  47.1 22.2 %collective-permute-start.17 = (bf16[4,2,32,2048]{3,2,1,0:T(8,128)(2,1)}, bf16[4,2,32,2048]{3,2,1,0:T(8,128)(2,1)}, u32[]{:S(2)}, u32[]{:S(2)}) collective-permute-start(bf16[4,2,32,2048]{3,2,1,0:T(8,128)(2,1)} %get-tuple-element.65), channel_id=1, source_target_pairs={{0,4},{4,0},{8,12},{12,8},{16,20},{20,16},{24,28},{28,24},{1,5},{5... | collective-permute-start | bytes 3145736 | tf_op jit(solution)/shard_map/ppermute | solution.py:429
  53.4 19.7 %all-to-all-start.1 = ((bf16[8,128,512]{2,1,0:T(8,128)(2,1)}), bf16[8,128,512]{2,1,0:T(8,128)(2,1)}, u32[]{:S(2)}, u32[]{:S(2)}) async-start(bf16[8,128,512]{2,1,0:T(8,128)(2,1)} %column_forward.1), calls=%async_computation.1 | async-start | bytes 2097152 | tf_op jit(solution)/shard_map/all_to_all | solution.py:524
  73.1 22.6 %all-to-all-start.2 = ((bf16[8,128,512]{2,1,0:T(8,128)(2,1)}), bf16[8,128,512]{2,1,0:T(8,128)(2,1)}, u32[]{:S(2)}, u32[]{:S(2)}) async-start(bf16[8,128,512]{2,1,0:T(8,128)(2,1)} %bitcast.55), calls=%async_computation.2 | async-start | bytes 2097152 | tf_op jit(solution)/shard_map/all_to_all | solution.py:524
  77.7 11.2 %collective-permute-start.14 = (bf16[2,32,2048]{2,1,0:T(8,128)(2,1)S(1)}, bf16[2,32,2048]{2,1,0:T(8,128)(2,1)S(1)}, u32[]{:S(2)}, u32[]{:S(2)}) collective-permute-start(bf16[2,32,2048]{2,1,0:T(8,128)(2,1)S(1)} %collective-permute-done.6.refs_1_), channel_id=1, source_target_pairs={{0,4},{4,0},{8,12},{12,8},{16,20},{20,16},{24,28},{28,24},{1,5},{5... | collective-permute-start | bytes 786440 | tf_op jit(solution)/shard_map/ppermute | solution.py:429
  77.9 11.1 %collective-permute-start.15 = (bf16[2,32,2048]{2,1,0:T(8,128)(2,1)}, bf16[2,32,2048]{2,1,0:T(8,128)(2,1)S(1)}, u32[]{:S(2)}, u32[]{:S(2)}) collective-permute-start(bf16[2,32,2048]{2,1,0:T(8,128)(2,1)} %collective-permute-done.7.refs_2_), channel_id=1, source_target_pairs={{0,4},{4,0},{8,12},{12,8},{16,20},{20,16},{24,28},{28,24},{1,5},{5... | collective-permute-start | bytes 786440 | tf_op jit(solution)/shard_map/ppermute | solution.py:429
  78.2 10.8 %collective-permute-start.16 = (bf16[2,32,2048]{2,1,0:T(8,128)(2,1)}, bf16[2,32,2048]{2,1,0:T(8,128)(2,1)S(1)}, u32[]{:S(2)}, u32[]{:S(2)}) collective-permute-start(bf16[2,32,2048]{2,1,0:T(8,128)(2,1)} %collective-permute-done.8.refs_3_), channel_id=1, source_target_pairs={{0,4},{4,0},{8,12},{12,8},{16,20},{20,16},{24,28},{28,24},{1,5},{5... | collective-permute-start | bytes 786440 | tf_op jit(solution)/shard_map/ppermute | solution.py:429
  78.4 14.2 %collective-permute-start.18 = (bf16[2,32,2048]{2,1,0:T(8,128)(2,1)}, bf16[2,32,2048]{2,1,0:T(8,128)(2,1)S(1)}, u32[]{:S(2)}, u32[]{:S(2)}) collective-permute-start(bf16[2,32,2048]{2,1,0:T(8,128)(2,1)} %get-tuple-element.68), channel_id=1, source_target_pairs={{0,1},{1,0},{2,3},{3,2},{4,5},{5,4},{6,7},{7,6},{8,9},{9,8},{10,11... | collective-permute-start | bytes 786440 | tf_op jit(solution)/shard_map/ppermute | solution.py:429
  80.0 15.0 %collective-permute-start.19 = (bf16[2,32,2048]{2,1,0:T(8,128)(2,1)}, bf16[2,32,2048]{2,1,0:T(8,128)(2,1)S(1)}, u32[]{:S(2)}, u32[]{:S(2)}) collective-permute-start(bf16[2,32,2048]{2,1,0:T(8,128)(2,1)} %get-tuple-element.69), channel_id=1, source_target_pairs={{0,2},{1,3},{2,0},{3,1},{4,6},{5,7},{6,4},{7,5},{8,10},{9,11},{10,... | collective-permute-start | bytes 786440 | tf_op jit(solution)/shard_map/ppermute | solution.py:429
  88.9 12.8 %collective-permute-start.20 = (bf16[4,2,32,2048]{3,2,1,0:T(8,128)(2,1)}, bf16[4,2,32,2048]{3,2,1,0:T(8,128)(2,1)}, u32[]{:S(2)}, u32[]{:S(2)}) collective-permute-start(bf16[4,2,32,2048]{3,2,1,0:T(8,128)(2,1)} %get-tuple-element.71), channel_id=1, source_target_pairs={{0,4},{4,0},{8,12},{12,8},{16,20},{20,16},{24,28},{28,24},{1,5},{5... | collective-permute-start | bytes 3145736 | tf_op jit(solution)/shard_map/ppermute | solution.py:429
  101.7 45.5 %all-to-all-start.3 = ((bf16[8,3,128,512]{3,2,1,0:T(8,128)(2,1)}), bf16[8,3,128,512]{3,2,1,0:T(8,128)(2,1)S(1)}, u32[]{:S(2)}, u32[]{:S(2)}) async-start(bf16[8,3,128,512]{3,2,1,0:T(8,128)(2,1)} %column_backward.1), calls=%async_computation.3 | async-start | bytes 6291456 | tf_op jit(solution)/shard_map/all_to_all | solution.py:524
  107.7 34.7 %collective-permute-start.24 = (bf16[2,32,2048]{2,1,0:T(8,128)(2,1)S(1)}, bf16[2,32,2048]{2,1,0:T(8,128)(2,1)S(1)}, u32[]{:S(2)}, u32[]{:S(2)}) collective-permute-start(bf16[2,32,2048]{2,1,0:T(8,128)(2,1)S(1)} %get-tuple-element.96), channel_id=1, source_target_pairs={{0,3},{1,2},{2,1},{3,0},{4,7},{5,6},{6,5},{7,4},{8,11},{9,10},{10,... | collective-permute-start | bytes 786440 | tf_op jit(solution)/shard_map/ppermute | solution.py:429
  111.0 31.5 %collective-permute-start.23 = (bf16[2,32,2048]{2,1,0:T(8,128)(2,1)S(1)}, bf16[2,32,2048]{2,1,0:T(8,128)(2,1)S(1)}, u32[]{:S(2)}, u32[]{:S(2)}) collective-permute-start(bf16[2,32,2048]{2,1,0:T(8,128)(2,1)S(1)} %get-tuple-element.97), channel_id=1, source_target_pairs={{0,2},{1,3},{2,0},{3,1},{4,6},{5,7},{6,4},{7,5},{8,10},{9,11},{10,... | collective-permute-start | bytes 786440 | tf_op jit(solution)/shard_map/ppermute | solution.py:429
  111.0 31.5 %collective-permute-start.22 = (bf16[2,32,2048]{2,1,0:T(8,128)(2,1)S(1)}, bf16[2,32,2048]{2,1,0:T(8,128)(2,1)S(1)}, u32[]{:S(2)}, u32[]{:S(2)}) collective-permute-start(bf16[2,32,2048]{2,1,0:T(8,128)(2,1)S(1)} %get-tuple-element.98), channel_id=1, source_target_pairs={{0,1},{1,0},{2,3},{3,2},{4,5},{5,4},{6,7},{7,6},{8,9},{9,8},{10,11... | collective-permute-start | bytes 786440 | tf_op jit(solution)/shard_map/ppermute | solution.py:429
  112.2 30.3 %collective-permute-start.21 = (bf16[2,32,2048]{2,1,0:T(8,128)(2,1)S(1)}, bf16[2,32,2048]{2,1,0:T(8,128)(2,1)S(1)}, u32[]{:S(2)}, u32[]{:S(2)}) collective-permute-start(bf16[2,32,2048]{2,1,0:T(8,128)(2,1)S(1)} %copy-done.7), channel_id=1, source_target_pairs={{0,3},{1,2},{2,1},{3,0},{4,7},{5,6},{6,5},{7,4},{8,11},{9,10},{10,... | collective-permute-start | bytes 786440 | tf_op jit(solution)/shard_map/ppermute | solution.py:429
  (21 other events, 123.5 us)

commit v4 on v3

--- a/solution.py
+++ b/solution.py
@@ -22,7 +22,7 @@
 LOW = -1e30
 BF16 = jnp.bfloat16
 F32 = jnp.float32
-VMEM = 56 * 1024 * 1024
+VMEM = 58 * 1024 * 1024
 DECLARED = {
     "pack": 0.6, "unpack": 0.6, "row_forward": 100.0, "row_backward": 1.4, "column_forward": 110.0,
     "column_backward": 120.0, "upstream_col": 70.0, "upstream_row": 0.1, "weight_row": 0.6,

time: 155 us -> 153 us (0.987)
  waiting for transfers between devices: 28.6 us -> 26.4 us
    unnamed x26 -> x30, local copies, waits for them, and re-layouts: 1.44 us -> 3.34 us
    pallas_call x1, Pallas kernels: 1.77 us -> 3.65 us  [unpack(): pl.pallas_call(unpack_kernel, grid=(2,), in_specs=[RESIDENT] + [anywhere]...]
    ppermute x28, waiting for transfers between devices: 23.8 us -> 22.2 us  [flip(): return lax.ppermute(array, axis, [(n, n ^ bits) for n in range(size)])]
  transfers between devices with their start and end apart: 32 -> 32, of which waited for: 10 -> 9; matrix products, arithmetic and copies ran while one was open for 5% -> 4% of each run, Pallas kernels for 43% -> 45%
where the time goes in v4:
time: 153 us; the launch traced here: 152 us
  Pallas kernels  67.7 us (44%)
  starting transfers between devices  46 us (30%)
  waiting for transfers between devices  26.4 us (17%)
  other arithmetic  6.77 us (4%)
  local copies, waits for them, and re-layouts  3.98 us (3%)
    ppermute x28, starting transfers between devices, flip(): return lax.ppermute(array, axis, [(n, n ^ bits) for n in range(size)])  30 us
    ppermute x28, waiting for transfers between devices, flip(): return lax.ppermute(array, axis, [(n, n ^ bits) for n in range(size)])  22.2 us
    all_to_all x4, starting transfers between devices, exchange(): lax.all_to_all(member, 'seq', split_axis=0, concat_axis=0, tiled=True)  16.1 us
    pallas_call x2, Pallas kernels, weight_parts(): pl.pallas_call(functools.partial(weight_kernel, factor), grid=(model // b...  12.6 us
    pallas_call x2, Pallas kernels, upstream_of(): pl.pallas_call(upstream_kernel, grid=(steps // block,), in_specs=[pl.Bloc...  12.4 us
    pallas_call x1, Pallas kernels, row_backward(): pl.pallas_call(row_backward_kernel, grid=(ROW_HEADS,), in_specs=[head] *...  12.2 us
    pallas_call x1, Pallas kernels, layer_output(): pl.pallas_call(layer_kernel, grid=(steps // block,), in_specs=[pl.BlockSp...  8.66 us
    pallas_call x2, Pallas kernels, column_call(): pl.pallas_call(kernel, in_specs=[RESIDENT] * len(operands), out_specs=RES...  7.69 us
  transfers between devices with their start and end apart: 32, of which 9 were waited for; matrix products, arithmetic and copies ran while one was open for 4% of the time, Pallas kernels for 45%

profile of v4, /device:TPU:0, one launch (start us, length us, event | category | flops | bytes accessed | tf_op | source)
XLA Modules:
  0.0 151.7 jit_solution(11813167155857212289)
XLA Ops:
  0.6 3.0 %collective-permute-start = (bf16[32,2048]{1,0:T(8,128)(2,1)}, bf16[32,2048]{1,0:T(8,128)(2,1)S(1)}, u32[]{:S(2)}, u32[]{:S(2)}) collective-permute-start(bf16[32,2048]{1,0:T(8,128)(2,1)} %param.8), channel_id=1, source_target_pairs={{0,8},{4,12},{8,0},{12,4},{16,24},{20,28},{24,16},{28,20},{1,9},{5... | collective-permute-start | bytes 393224 | tf_op jit(solution)/shard_map/ppermute | solution.py:429
  5.2 3.1 %pack.1.refs_0_ = bf16[8,3,128,512]{3,2,1,0:T(8,128)(2,1)} custom-call(bf16[1024,1024]{1,0:T(8,128)(2,1)} %bitcast.44, bf16[1024,1024]{1,0:T(8,128)(2,1)} %bitcast.47, bf16[1024,1024]{1,0:T(8,128)(2,1)} %bitcast.50), custom_call_target="tpu_custom_call" | custom-call | flops 690000000 | tf_op jit(solution)/shard_map/pack/pallas_call | solution.py:223
  8.3 4.3 %all-to-all-start = ((bf16[8,3,128,512]{3,2,1,0:T(8,128)(2,1)}), bf16[8,3,128,512]{3,2,1,0:T(8,128)(2,1)S(1)}, u32[]{:S(2)}, u32[]{:S(2)}) async-start(bf16[8,3,128,512]{3,2,1,0:T(8,128)(2,1)} %pack.1.refs_0_), calls=%async_computation | async-start | bytes 6291456 | tf_op jit(solution)/shard_map/all_to_all | solution.py:524
  14.7 3.6 %collective-permute-start.5 = (bf16[2,32,2048]{2,1,0:T(8,128)(2,1)}, bf16[2,32,2048]{2,1,0:T(8,128)(2,1)}, u32[]{:S(2)}, u32[]{:S(2)}) collective-permute-start(bf16[2,32,2048]{2,1,0:T(8,128)(2,1)} %get-tuple-element.51.refs_1_.refs_0_), channel_id=1, source_target_pairs={{0,3},{1,2},{2,1},{3,0},{4,7},{5,6},{6,5},{7,4},{8,11},{9,10},{10,... | collective-permute-start | bytes 786440 | tf_op jit(solution)/shard_map/ppermute | solution.py:429
  19.1 6.8 %row_forward.1.attn_ref.row_ref = bf16[1024,512]{1,0:T(8,128)(2,1)} custom-call(bf16[1024,1024]{1,0:T(8,128)(2,1)} %bitcast.45, bf16[1024,1024]{1,0:T(8,128)(2,1)} %bitcast.48, bf16[1024,1024]{1,0:T(8,128)(2,1)} %bitcast.51, bf16[8,3,128,512]{3,2,1,0:T(8,128)(2,1)} %pack.1.refs_0_, bf16[2,32,2048]{2,1,0:T(8,128)(2,1)} %get-tuple-element.51.refs_1_.refs_0_), custom_call_target="tpu_custom_call" | custom-call | flops 115000000512 | tf_op jit(solution)/shard_map/row_forward/pallas_call | solution.py:178
  25.9 6.3 %weight_row.1 = (f32[4,2,32,2048]{3,2,1,0:T(8,128)}, bf16[4,2,32,2048]{3,2,1,0:T(8,128)(2,1)}) custom-call(s32[1]{0:T(128)} %bitcast.7.core_ref, bf16[1024,512]{1,0:T(8,128)(2,1)} %row_forward.1.attn_ref.row_ref, bf16[1024,2048]{1,0:T(8,128)(2,1)} %bitcast.38), custom_call_target="tpu_custom_call" | custom-call | flops 690000000 | tf_op jit(solution)/shard_map/weight_row/pallas_call | solution.py:412
  32.3 9.1 %collective-permute-done.4.refs_2_ = bf16[2,32,2048]{2,1,0:T(8,128)(2,1)} collective-permute-done((bf16[2,32,2048]{2,1,0:T(8,128)(2,1)}, bf16[2,32,2048]{2,1,0:T(8,128)(2,1)}, u32[]{:S(2)}, u32[]{:S(2)}) %collective-permute-start.4) | collective-permute-done | bytes 262176 | tf_op jit(solution)/shard_map/ppermute | solution.py:429
  47.1 3.4 %all-to-all-done.in_ref = bf16[8,3,128,512]{3,2,1,0:T(8,128)(2,1)S(1)} async-done(((bf16[8,3,128,512]{3,2,1,0:T(8,128)(2,1)}), bf16[8,3,128,512]{3,2,1,0:T(8,128)(2,1)S(1)}, u32[]{:S(2)}, u32[]{:S(2)}) %all-to-all-start) | async-done | bytes 3145760 | tf_op jit(solution)/shard_map/all_to_all | solution.py:524
  50.5 2.9 %column_forward.1 = bf16[8,128,512]{2,1,0:T(8,128)(2,1)} custom-call(bf16[8,3,128,512]{3,2,1,0:T(8,128)(2,1)S(1)} %all-to-all-done.in_ref), custom_call_target="tpu_custom_call" | custom-call | flops 126500003840 | tf_op jit(solution)/shard_map/column_forward/pallas_call | solution.py:321
  53.4 3.6 %all-to-all-start.1 = ((bf16[8,128,512]{2,1,0:T(8,128)(2,1)}), bf16[8,128,512]{2,1,0:T(8,128)(2,1)S(1)}, u32[]{:S(2)}, u32[]{:S(2)}) async-start(bf16[8,128,512]{2,1,0:T(8,128)(2,1)} %column_forward.1), calls=%async_computation.1 | async-start | bytes 2097152 | tf_op jit(solution)/shard_map/all_to_all | solution.py:524
  57.0 6.0 %collective-permute-done.6.refs_1_ = bf16[2,32,2048]{2,1,0:T(8,128)(2,1)S(1)} collective-permute-done((bf16[2,32,2048]{2,1,0:T(8,128)(2,1)}, bf16[2,32,2048]{2,1,0:T(8,128)(2,1)S(1)}, u32[]{:S(2)}, u32[]{:S(2)}) %collective-permute-start.6) | collective-permute-done | bytes 262176 | tf_op jit(solution)/shard_map/ppermute | solution.py:429
  62.9 6.3 %upstream_col.1 = (bf16[1024,512]{1,0:T(8,128)(2,1)}, bf16[512,2048]{1,0:T(8,128)(2,1)}) custom-call(s32[16]{0:T(128)} %mul.26.place_ref, bf16[2,32,2048]{2,1,0:T(8,128)(2,1)} %get-tuple-element.51.refs_1_.refs_0_, bf16[2,32,2048]{2,1,0:T(8,128)(2,1)} %copy-done.14, bf16[2,32,2048]{2,1,0:T(8,128)(2,1)} %collective-permute-done.4.refs_2_, ...), custom_call_target="tpu_custom_call" | custom-call | flops 80499998720 | tf_op jit(solution)/shard_map/upstream_col/pallas_call | solution.py:351
  72.3 3.6 %all-to-all-start.2 = ((bf16[8,128,512]{2,1,0:T(8,128)(2,1)}), bf16[8,128,512]{2,1,0:T(8,128)(2,1)S(1)}, u32[]{:S(2)}, u32[]{:S(2)}) async-start(bf16[8,128,512]{2,1,0:T(8,128)(2,1)} %bitcast.57), calls=%async_computation.2 | async-start | bytes 2097152 | tf_op jit(solution)/shard_map/all_to_all | solution.py:524
  81.1 6.3 %weight_col.1 = (f32[4,2,32,2048]{3,2,1,0:T(8,128)}, bf16[4,2,32,2048]{3,2,1,0:T(8,128)(2,1)}) custom-call(s32[1]{0:T(128)} %bitcast.7.core_ref, bf16[1024,512]{1,0:T(8,128)(2,1)} %bitcast.42, bf16[1024,2048]{1,0:T(8,128)(2,1)} %bitcast.40), custom_call_target="tpu_custom_call" | custom-call | flops 115000000 | tf_op jit(solution)/shard_map/weight_col/pallas_call | solution.py:412
  87.6 3.7 %collective-permute-done.18.refs_1_ = bf16[2,32,2048]{2,1,0:T(8,128)(2,1)S(1)} collective-permute-done((bf16[2,32,2048]{2,1,0:T(8,128)(2,1)}, bf16[2,32,2048]{2,1,0:T(8,128)(2,1)S(1)}, u32[]{:S(2)}, u32[]{:S(2)}) %collective-permute-start.18) | collective-permute-done | bytes 262176 | tf_op jit(solution)/shard_map/ppermute | solution.py:429
  96.4 4.8 %column_backward.1 = bf16[8,3,128,512]{3,2,1,0:T(8,128)(2,1)} custom-call(bf16[8,3,128,512]{3,2,1,0:T(8,128)(2,1)S(1)} %copy-done.1, bf16[8,128,512]{2,1,0:T(8,128)(2,1)S(1)} %all-to-all-done.2.u_ref), custom_call_target="tpu_custom_call" | custom-call | flops 138000007168 | tf_op jit(solution)/shard_map/column_backward/pallas_call | solution.py:321
  101.2 4.6 %all-to-all-start.3 = ((bf16[8,3,128,512]{3,2,1,0:T(8,128)(2,1)}), bf16[8,3,128,512]{3,2,1,0:T(8,128)(2,1)}, u32[]{:S(2)}, u32[]{:S(2)}) async-start(bf16[8,3,128,512]{3,2,1,0:T(8,128)(2,1)} %column_backward.1), calls=%async_computation.3 | async-start | bytes 6291456 | tf_op jit(solution)/shard_map/all_to_all | solution.py:524
  107.7 2.8 %collective-permute-start.24 = (bf16[2,32,2048]{2,1,0:T(8,128)(2,1)S(1)}, bf16[2,32,2048]{2,1,0:T(8,128)(2,1)S(1)}, u32[]{:S(2)}, u32[]{:S(2)}) collective-permute-start(bf16[2,32,2048]{2,1,0:T(8,128)(2,1)S(1)} %get-tuple-element.96), channel_id=1, source_target_pairs={{0,3},{1,2},{2,1},{3,0},{4,7},{5,6},{6,5},{7,4},{8,11},{9,10},{10,... | collective-permute-start | bytes 786440 | tf_op jit(solution)/shard_map/ppermute | solution.py:429
  112.2 2.7 %collective-permute-start.21 = (bf16[2,32,2048]{2,1,0:T(8,128)(2,1)S(1)}, bf16[2,32,2048]{2,1,0:T(8,128)(2,1)S(1)}, u32[]{:S(2)}, u32[]{:S(2)}) collective-permute-start(bf16[2,32,2048]{2,1,0:T(8,128)(2,1)S(1)} %copy-done.9), channel_id=1, source_target_pairs={{0,3},{1,2},{2,1},{3,0},{4,7},{5,6},{6,5},{7,4},{8,11},{9,10},{10,... | collective-permute-start | bytes 786440 | tf_op jit(solution)/shard_map/ppermute | solution.py:429
  114.9 6.2 %upstream_row.1 = (bf16[1024,512]{1,0:T(8,128)(2,1)}, bf16[512,2048]{1,0:T(8,128)(2,1)}) custom-call(s32[16]{0:T(128)} %mul.26.place_ref, bf16[2,32,2048]{2,1,0:T(8,128)(2,1)} %get-tuple-element.59.refs_0_, bf16[2,32,2048]{2,1,0:T(8,128)(2,1)} %copy-done.8, bf16[2,32,2048]{2,1,0:T(8,128)(2,1)} %collective-permute-done.7.refs_2_, ...), custom_call_target="tpu_custom_call" | custom-call | flops 115000000 | tf_op jit(solution)/shard_map/upstream_row/pallas_call | solution.py:351
  121.1 12.2 %row_backward.1 = (bf16[1024,1024]{1,0:T(8,128)(2,1)}, bf16[1024,1024]{1,0:T(8,128)(2,1)}, bf16[1024,1024]{1,0:T(8,128)(2,1)}) custom-call(bf16[1024,1024]{1,0:T(8,128)(2,1)} %bitcast.46, bf16[1024,1024]{1,0:T(8,128)(2,1)} %bitcast.49, bf16[1024,1024]{1,0:T(8,128)(2,1)} %bitcast.52, bf16[1024,512]{1,0:T(8,128)(2,1)} %get-tuple-element.75.u_ref), custom_call_target="tpu_custom_call" | custom-call | flops 1610000000 | tf_op jit(solution)/shard_map/row_backward/pallas_call | solution.py:193
  133.3 8.7 %layer_output.1 = bf16[1024,2048]{1,0:T(8,128)(2,1)} custom-call(bf16[1024,512]{1,0:T(8,128)(2,1)} %row_forward.1.attn_ref.row_ref, bf16[1024,512]{1,0:T(8,128)(2,1)} %bitcast.43, bf16[512,2048]{1,0:T(8,128)(2,1)} %get-tuple-element.78.w_row_ref, bf16[512,2048]{1,0:T(8,128)(2,1)} %get-tuple-element.79.w_col_ref), custom_call_target="tpu_custom_call" | custom-call | flops 1035000000 | tf_op jit(solution)/shard_map/layer_output/pallas_call | solution.py:380
  142.5 2.7 %collective-permute-start.27 = (bf16[32,2048]{1,0:T(8,128)(2,1)S(1)}, bf16[32,2048]{1,0:T(8,128)(2,1)S(1)}, u32[]{:S(2)}, u32[]{:S(2)}) collective-permute-start(bf16[32,2048]{1,0:T(8,128)(2,1)S(1)} %get-tuple-element.105), channel_id=1, source_target_pairs={{0,24},{4,28},{8,16},{12,20},{16,8},{20,12},{24,0},{28,4},{1,25},{... | collective-permute-start | bytes 393224 | tf_op jit(solution)/shard_map/ppermute | solution.py:429
  146.0 3.6 %unpack.1 = (bf16[1024,1024]{1,0:T(8,128)(2,1)}, bf16[1024,1024]{1,0:T(8,128)(2,1)}, bf16[1024,1024]{1,0:T(8,128)(2,1)}) custom-call(bf16[8,3,128,512]{3,2,1,0:T(8,128)(2,1)} %all-to-all-done.3.in_ref, bf16[1024,1024]{1,0:T(8,128)(2,1)} %get-tuple-element.76._q, ...), custom_call_target="tpu_custom_call", output_to_operand_aliasing={{0}: (1, {}), {1}: (2, {}), {2}: (3, {})} | custom-call | flops 690000000 | tf_op jit(solution)/shard_map/unpack/pallas_call | solution.py:246
  (92 shorter events, 30.5 us)
Async XLA Ops:
  0.6 12.1 %collective-permute-start = (bf16[32,2048]{1,0:T(8,128)(2,1)}, bf16[32,2048]{1,0:T(8,128)(2,1)S(1)}, u32[]{:S(2)}, u32[]{:S(2)}) collective-permute-start(bf16[32,2048]{1,0:T(8,128)(2,1)} %param.8), channel_id=1, source_target_pairs={{0,8},{4,12},{8,0},{12,4},{16,24},{20,28},{24,16},{28,20},{1,9},{5... | collective-permute-start | bytes 393224 | tf_op jit(solution)/shard_map/ppermute | solution.py:429
  3.6 9.1 %collective-permute-start.2 = (bf16[32,2048]{1,0:T(8,128)(2,1)}, bf16[32,2048]{1,0:T(8,128)(2,1)S(1)}, u32[]{:S(2)}, u32[]{:S(2)}) collective-permute-start(bf16[32,2048]{1,0:T(8,128)(2,1)} %param.8), channel_id=1, source_target_pairs={{0,24},{4,28},{8,16},{12,20},{16,8},{20,12},{24,0},{28,4},{1,25},{... | collective-permute-start | bytes 393224 | tf_op jit(solution)/shard_map/ppermute | solution.py:429
  8.3 42.2 %all-to-all-start = ((bf16[8,3,128,512]{3,2,1,0:T(8,128)(2,1)}), bf16[8,3,128,512]{3,2,1,0:T(8,128)(2,1)S(1)}, u32[]{:S(2)}, u32[]{:S(2)}) async-start(bf16[8,3,128,512]{3,2,1,0:T(8,128)(2,1)} %pack.1.refs_0_), calls=%async_computation | async-start | bytes 6291456 | tf_op jit(solution)/shard_map/all_to_all | solution.py:524
  14.7 17.6 %collective-permute-start.5 = (bf16[2,32,2048]{2,1,0:T(8,128)(2,1)}, bf16[2,32,2048]{2,1,0:T(8,128)(2,1)}, u32[]{:S(2)}, u32[]{:S(2)}) collective-permute-start(bf16[2,32,2048]{2,1,0:T(8,128)(2,1)} %get-tuple-element.51.refs_1_.refs_0_), channel_id=1, source_target_pairs={{0,3},{1,2},{2,1},{3,0},{4,7},{5,6},{6,5},{7,4},{8,11},{9,10},{10,... | collective-permute-start | bytes 786440 | tf_op jit(solution)/shard_map/ppermute | solution.py:429
  18.3 23.1 %collective-permute-start.4 = (bf16[2,32,2048]{2,1,0:T(8,128)(2,1)}, bf16[2,32,2048]{2,1,0:T(8,128)(2,1)}, u32[]{:S(2)}, u32[]{:S(2)}) collective-permute-start(bf16[2,32,2048]{2,1,0:T(8,128)(2,1)} %get-tuple-element.51.refs_1_.refs_0_), channel_id=1, source_target_pairs={{0,2},{1,3},{2,0},{3,1},{4,6},{5,7},{6,4},{7,5},{8,10},{9,11},{10,... | collective-permute-start | bytes 786440 | tf_op jit(solution)/shard_map/ppermute | solution.py:429
  18.3 23.1 %collective-permute-start.3 = (bf16[2,32,2048]{2,1,0:T(8,128)(2,1)}, bf16[2,32,2048]{2,1,0:T(8,128)(2,1)S(1)}, u32[]{:S(2)}, u32[]{:S(2)}) collective-permute-start(bf16[2,32,2048]{2,1,0:T(8,128)(2,1)} %get-tuple-element.51.refs_1_.refs_0_), channel_id=1, source_target_pairs={{0,1},{1,0},{2,3},{3,2},{4,5},{5,4},{6,7},{7,6},{8,9},{9,8},{10,11... | collective-permute-start | bytes 786440 | tf_op jit(solution)/shard_map/ppermute | solution.py:429
  32.3 12.9 %collective-permute-start.9 = (bf16[2,32,2048]{2,1,0:T(8,128)(2,1)}, bf16[2,32,2048]{2,1,0:T(8,128)(2,1)}, u32[]{:S(2)}, u32[]{:S(2)}) collective-permute-start(bf16[2,32,2048]{2,1,0:T(8,128)(2,1)} %get-tuple-element.51.refs_1_.refs_0_), channel_id=1, source_target_pairs={{0,4},{4,0},{8,12},{12,8},{16,20},{20,16},{24,28},{28,24},{1,5},{5... | collective-permute-start | bytes 786440 | tf_op jit(solution)/shard_map/ppermute | solution.py:429
  42.6 28.8 %collective-permute-start.8 = (bf16[2,32,2048]{2,1,0:T(8,128)(2,1)}, bf16[2,32,2048]{2,1,0:T(8,128)(2,1)}, u32[]{:S(2)}, u32[]{:S(2)}) collective-permute-start(bf16[2,32,2048]{2,1,0:T(8,128)(2,1)} %get-tuple-element.59.refs_0_), channel_id=1, source_target_pairs={{0,3},{1,2},{2,1},{3,0},{4,7},{5,6},{6,5},{7,4},{8,11},{9,10},{10,... | collective-permute-start | bytes 786440 | tf_op jit(solution)/shard_map/ppermute | solution.py:429
  45.1 26.4 %collective-permute-start.7 = (bf16[2,32,2048]{2,1,0:T(8,128)(2,1)}, bf16[2,32,2048]{2,1,0:T(8,128)(2,1)}, u32[]{:S(2)}, u32[]{:S(2)}) collective-permute-start(bf16[2,32,2048]{2,1,0:T(8,128)(2,1)} %get-tuple-element.59.refs_0_), channel_id=1, source_target_pairs={{0,2},{1,3},{2,0},{3,1},{4,6},{5,7},{6,4},{7,5},{8,10},{9,11},{10,... | collective-permute-start | bytes 786440 | tf_op jit(solution)/shard_map/ppermute | solution.py:429
  45.1 17.8 %collective-permute-start.6 = (bf16[2,32,2048]{2,1,0:T(8,128)(2,1)}, bf16[2,32,2048]{2,1,0:T(8,128)(2,1)S(1)}, u32[]{:S(2)}, u32[]{:S(2)}) collective-permute-start(bf16[2,32,2048]{2,1,0:T(8,128)(2,1)} %get-tuple-element.59.refs_0_), channel_id=1, source_target_pairs={{0,1},{1,0},{2,3},{3,2},{4,5},{5,4},{6,7},{7,6},{8,9},{9,8},{10,11... | collective-permute-start | bytes 786440 | tf_op jit(solution)/shard_map/ppermute | solution.py:429
  47.1 22.2 %collective-permute-start.17 = (bf16[4,2,32,2048]{3,2,1,0:T(8,128)(2,1)}, bf16[4,2,32,2048]{3,2,1,0:T(8,128)(2,1)}, u32[]{:S(2)}, u32[]{:S(2)}) collective-permute-start(bf16[4,2,32,2048]{3,2,1,0:T(8,128)(2,1)} %get-tuple-element.65), channel_id=1, source_target_pairs={{0,4},{4,0},{8,12},{12,8},{16,20},{20,16},{24,28},{28,24},{1,5},{5... | collective-permute-start | bytes 3145736 | tf_op jit(solution)/shard_map/ppermute | solution.py:429
  53.4 18.9 %all-to-all-start.1 = ((bf16[8,128,512]{2,1,0:T(8,128)(2,1)}), bf16[8,128,512]{2,1,0:T(8,128)(2,1)S(1)}, u32[]{:S(2)}, u32[]{:S(2)}) async-start(bf16[8,128,512]{2,1,0:T(8,128)(2,1)} %column_forward.1), calls=%async_computation.1 | async-start | bytes 2097152 | tf_op jit(solution)/shard_map/all_to_all | solution.py:524
  72.3 22.2 %all-to-all-start.2 = ((bf16[8,128,512]{2,1,0:T(8,128)(2,1)}), bf16[8,128,512]{2,1,0:T(8,128)(2,1)S(1)}, u32[]{:S(2)}, u32[]{:S(2)}) async-start(bf16[8,128,512]{2,1,0:T(8,128)(2,1)} %bitcast.57), calls=%async_computation.2 | async-start | bytes 2097152 | tf_op jit(solution)/shard_map/all_to_all | solution.py:524
  76.3 11.2 %collective-permute-start.14 = (bf16[2,32,2048]{2,1,0:T(8,128)(2,1)S(1)}, bf16[2,32,2048]{2,1,0:T(8,128)(2,1)S(1)}, u32[]{:S(2)}, u32[]{:S(2)}) collective-permute-start(bf16[2,32,2048]{2,1,0:T(8,128)(2,1)S(1)} %collective-permute-done.6.refs_1_), channel_id=1, source_target_pairs={{0,4},{4,0},{8,12},{12,8},{16,20},{20,16},{24,28},{28,24},{1,5},{5... | collective-permute-start | bytes 786440 | tf_op jit(solution)/shard_map/ppermute | solution.py:429
  76.4 11.1 %collective-permute-start.15 = (bf16[2,32,2048]{2,1,0:T(8,128)(2,1)}, bf16[2,32,2048]{2,1,0:T(8,128)(2,1)S(1)}, u32[]{:S(2)}, u32[]{:S(2)}) collective-permute-start(bf16[2,32,2048]{2,1,0:T(8,128)(2,1)} %collective-permute-done.7.refs_2_), channel_id=1, source_target_pairs={{0,4},{4,0},{8,12},{12,8},{16,20},{20,16},{24,28},{28,24},{1,5},{5... | collective-permute-start | bytes 786440 | tf_op jit(solution)/shard_map/ppermute | solution.py:429
  76.8 10.8 %collective-permute-start.16 = (bf16[2,32,2048]{2,1,0:T(8,128)(2,1)}, bf16[2,32,2048]{2,1,0:T(8,128)(2,1)S(1)}, u32[]{:S(2)}, u32[]{:S(2)}) collective-permute-start(bf16[2,32,2048]{2,1,0:T(8,128)(2,1)} %collective-permute-done.8.refs_3_), channel_id=1, source_target_pairs={{0,4},{4,0},{8,12},{12,8},{16,20},{20,16},{24,28},{28,24},{1,5},{5... | collective-permute-start | bytes 786440 | tf_op jit(solution)/shard_map/ppermute | solution.py:429
  77.0 14.3 %collective-permute-start.18 = (bf16[2,32,2048]{2,1,0:T(8,128)(2,1)}, bf16[2,32,2048]{2,1,0:T(8,128)(2,1)S(1)}, u32[]{:S(2)}, u32[]{:S(2)}) collective-permute-start(bf16[2,32,2048]{2,1,0:T(8,128)(2,1)} %get-tuple-element.68), channel_id=1, source_target_pairs={{0,1},{1,0},{2,3},{3,2},{4,5},{5,4},{6,7},{7,6},{8,9},{9,8},{10,11... | collective-permute-start | bytes 786440 | tf_op jit(solution)/shard_map/ppermute | solution.py:429
  78.9 14.9 %collective-permute-start.19 = (bf16[2,32,2048]{2,1,0:T(8,128)(2,1)S(1)}, bf16[2,32,2048]{2,1,0:T(8,128)(2,1)S(1)}, u32[]{:S(2)}, u32[]{:S(2)}) collective-permute-start(bf16[2,32,2048]{2,1,0:T(8,128)(2,1)S(1)} %get-tuple-element.69), channel_id=1, source_target_pairs={{0,2},{1,3},{2,0},{3,1},{4,6},{5,7},{6,4},{7,5},{8,10},{9,11},{10,... | collective-permute-start | bytes 786440 | tf_op jit(solution)/shard_map/ppermute | solution.py:429
  87.4 13.8 %collective-permute-start.20 = (bf16[4,2,32,2048]{3,2,1,0:T(8,128)(2,1)}, bf16[4,2,32,2048]{3,2,1,0:T(8,128)(2,1)S(1)}, u32[]{:S(2)}, u32[]{:S(2)}) collective-permute-start(bf16[4,2,32,2048]{3,2,1,0:T(8,128)(2,1)} %get-tuple-element.71), channel_id=1, source_target_pairs={{0,4},{4,0},{8,12},{12,8},{16,20},{20,16},{24,28},{28,24},{1,5},{5... | collective-permute-start | bytes 3145736 | tf_op jit(solution)/shard_map/ppermute | solution.py:429
  101.2 44.8 %all-to-all-start.3 = ((bf16[8,3,128,512]{3,2,1,0:T(8,128)(2,1)}), bf16[8,3,128,512]{3,2,1,0:T(8,128)(2,1)}, u32[]{:S(2)}, u32[]{:S(2)}) async-start(bf16[8,3,128,512]{3,2,1,0:T(8,128)(2,1)} %column_backward.1), calls=%async_computation.3 | async-start | bytes 6291456 | tf_op jit(solution)/shard_map/all_to_all | solution.py:524
  107.7 34.3 %collective-permute-start.24 = (bf16[2,32,2048]{2,1,0:T(8,128)(2,1)S(1)}, bf16[2,32,2048]{2,1,0:T(8,128)(2,1)S(1)}, u32[]{:S(2)}, u32[]{:S(2)}) collective-permute-start(bf16[2,32,2048]{2,1,0:T(8,128)(2,1)S(1)} %get-tuple-element.96), channel_id=1, source_target_pairs={{0,3},{1,2},{2,1},{3,0},{4,7},{5,6},{6,5},{7,4},{8,11},{9,10},{10,... | collective-permute-start | bytes 786440 | tf_op jit(solution)/shard_map/ppermute | solution.py:429
  110.5 31.5 %collective-permute-start.23 = (bf16[2,32,2048]{2,1,0:T(8,128)(2,1)S(1)}, bf16[2,32,2048]{2,1,0:T(8,128)(2,1)S(1)}, u32[]{:S(2)}, u32[]{:S(2)}) collective-permute-start(bf16[2,32,2048]{2,1,0:T(8,128)(2,1)S(1)} %get-tuple-element.97), channel_id=1, source_target_pairs={{0,2},{1,3},{2,0},{3,1},{4,6},{5,7},{6,4},{7,5},{8,10},{9,11},{10,... | collective-permute-start | bytes 786440 | tf_op jit(solution)/shard_map/ppermute | solution.py:429
  110.5 31.5 %collective-permute-start.22 = (bf16[2,32,2048]{2,1,0:T(8,128)(2,1)S(1)}, bf16[2,32,2048]{2,1,0:T(8,128)(2,1)S(1)}, u32[]{:S(2)}, u32[]{:S(2)}) collective-permute-start(bf16[2,32,2048]{2,1,0:T(8,128)(2,1)S(1)} %get-tuple-element.98), channel_id=1, source_target_pairs={{0,1},{1,0},{2,3},{3,2},{4,5},{5,4},{6,7},{7,6},{8,9},{9,8},{10,11... | collective-permute-start | bytes 786440 | tf_op jit(solution)/shard_map/ppermute | solution.py:429
  112.2 29.8 %collective-permute-start.21 = (bf16[2,32,2048]{2,1,0:T(8,128)(2,1)S(1)}, bf16[2,32,2048]{2,1,0:T(8,128)(2,1)S(1)}, u32[]{:S(2)}, u32[]{:S(2)}) collective-permute-start(bf16[2,32,2048]{2,1,0:T(8,128)(2,1)S(1)} %copy-done.9), channel_id=1, source_target_pairs={{0,3},{1,2},{2,1},{3,0},{4,7},{5,6},{6,5},{7,4},{8,11},{9,10},{10,... | collective-permute-start | bytes 786440 | tf_op jit(solution)/shard_map/ppermute | solution.py:429
  (23 other events, 127.5 us)

commit v5 on v4

--- a/solution.py
+++ b/solution.py
@@ -278,6 +278,13 @@
     return [units[n : n + together] for n in range(0, len(units), together)]
 
 
+def placed(units, width, span):
+    base = pl.program_id(0) * width
+    return [
+        (pl.ds(pl.multiple_of(base + cols.start, span), span), lanes) for cols, lanes in units
+    ]
+
+
 def column_scores(in_ref, units, mask):
     return [
         [jnp.where(mask, dot(head_tokens(in_ref, 1, unit), head_tokens(in_ref, 0, unit), 1, 1), LOW)]
@@ -286,26 +293,28 @@
 
 
 def column_forward_kernel(in_ref, out_ref):
-    rows, _, width, _ = in_ref.shape
+    rows, width, _ = out_ref.shape
     span = min(COLUMN_SPAN, width)
     mask = column_mask(rows, span)
     for units in column_units(rows, width, span):
-        scores = column_scores(in_ref, units, mask)
-        results = forward_units(scores, [head_tokens(in_ref, 2, unit) for unit in units])
+        sources = placed(units, width, span)
+        scores = column_scores(in_ref, sources, mask)
+        results = forward_units(scores, [head_tokens(in_ref, 2, unit) for unit in sources])
         for (cols, lanes), result in zip(units, results):
             out_ref[:, cols, lanes] = result.reshape(rows, span, DH)
 
 
 def column_backward_kernel(in_ref, u_ref, out_ref):
-    rows, _, width, _ = in_ref.shape
+    rows, _, width, _ = out_ref.shape
     span = min(COLUMN_SPAN, width)
     mask = column_mask(rows, span)
     for units in column_units(rows, width, span):
+        sources = placed(units, width, span)
         queries, keys, values = [
-            [head_tokens(in_ref, n, unit) for unit in units] for n in range(3)
+            [head_tokens(in_ref, n, unit) for unit in sources] for n in range(3)
         ]
-        upstreams = [head_tokens(u_ref, None, unit) for unit in units]
-        scores = column_scores(in_ref, units, mask)
+        upstreams = [head_tokens(u_ref, None, unit) for unit in sources]
+        scores = column_scores(in_ref, sources, mask)
         share_grads = [[dot(v, u, 1, 1)] for v, u in zip(values, upstreams)]
         grads = backward_units(scores, share_grads, queries, keys, upstreams)
         for (cols, lanes), query_grad, key_grad, value_grad in zip(units, *grads):
@@ -317,11 +326,17 @@
     rows, _, cols, width = packed.shape
     forward = upstream is None
     shape = (rows, cols, width) if forward else (rows, 3, cols, width)
+    block = max(min(COLUMN_SPAN, cols), cols // 2)
+    if forward:
+        out_spec = pl.BlockSpec((rows, block, width), lambda c: (0, c, 0))
+    else:
+        out_spec = pl.BlockSpec((rows, 3, block, width), lambda c: (0, 0, c, 0))
     operands = (packed,) if forward else (packed, upstream)
     return pl.pallas_call(
         kernel,
+        grid=(cols // block,),
         in_specs=[RESIDENT] * len(operands),
-        out_specs=RESIDENT,
+        out_specs=out_spec,
         out_shape=COLUMN_OUT(shape, BF16),
         compiler_params=params(),
         cost_estimate=cost(name),

time: 153 us -> 152 us (level)
  no operation moved by 1% of the time
where the time goes in v5:
time: 152 us
  Pallas kernels  67.5 us (44%)
  starting transfers between devices  46.1 us (30%)
  waiting for transfers between devices  26.3 us (17%)
  other arithmetic  6.77 us (4%)
  local copies, waits for them, and re-layouts  3.98 us (3%)
    ppermute x28, starting transfers between devices, flip(): return lax.ppermute(array, axis, [(n, n ^ bits) for n in range(size)])  30 us
    ppermute x28, waiting for transfers between devices, flip(): return lax.ppermute(array, axis, [(n, n ^ bits) for n in range(size)])  22 us
    all_to_all x4, starting transfers between devices, exchange(): lax.all_to_all(member, 'seq', split_axis=0, concat_axis=0, tiled=True)  16.1 us
    pallas_call x2, Pallas kernels, weight_parts(): pl.pallas_call(functools.partial(weight_kernel, factor), grid=(model // b...  12.6 us
    pallas_call x2, Pallas kernels, upstream_of(): pl.pallas_call(upstream_kernel, grid=(steps // block,), in_specs=[pl.Bloc...  12.4 us
    pallas_call x1, Pallas kernels, row_backward(): pl.pallas_call(row_backward_kernel, grid=(ROW_HEADS,), in_specs=[head] *...  12.2 us
    pallas_call x1, Pallas kernels, layer_output(): pl.pallas_call(layer_kernel, grid=(steps // block,), in_specs=[pl.BlockSp...  8.67 us
    pallas_call x2, Pallas kernels, column_call(): pl.pallas_call(kernel, grid=(cols // block,), in_specs=[RESIDENT] * len(o...  7.49 us
  transfers between devices with their start and end apart: 32, of which 9 were waited for; matrix products, arithmetic and copies ran while one was open for 4% of the time, Pallas kernels for 45%

profile of v5, /device:TPU:0, one launch (start us, length us, event | category | flops | bytes accessed | tf_op | source)
XLA Modules:
  0.0 151.5 jit_solution(6936684989181648752)
XLA Ops:
  0.6 3.0 %collective-permute-start = (bf16[32,2048]{1,0:T(8,128)(2,1)}, bf16[32,2048]{1,0:T(8,128)(2,1)S(1)}, u32[]{:S(2)}, u32[]{:S(2)}) collective-permute-start(bf16[32,2048]{1,0:T(8,128)(2,1)} %param.8), channel_id=1, source_target_pairs={{0,8},{4,12},{8,0},{12,4},{16,24},{20,28},{24,16},{28,20},{1,9},{5... | collective-permute-start | bytes 393224 | tf_op jit(solution)/shard_map/ppermute | solution.py:444
  5.2 3.1 %pack.1.refs_0_ = bf16[8,3,128,512]{3,2,1,0:T(8,128)(2,1)} custom-call(bf16[1024,1024]{1,0:T(8,128)(2,1)} %bitcast.44, bf16[1024,1024]{1,0:T(8,128)(2,1)} %bitcast.47, bf16[1024,1024]{1,0:T(8,128)(2,1)} %bitcast.50), custom_call_target="tpu_custom_call" | custom-call | flops 690000000 | tf_op jit(solution)/shard_map/pack/pallas_call | solution.py:223
  8.3 4.3 %all-to-all-start = ((bf16[8,3,128,512]{3,2,1,0:T(8,128)(2,1)}), bf16[8,3,128,512]{3,2,1,0:T(8,128)(2,1)S(1)}, u32[]{:S(2)}, u32[]{:S(2)}) async-start(bf16[8,3,128,512]{3,2,1,0:T(8,128)(2,1)} %pack.1.refs_0_), calls=%async_computation | async-start | bytes 6291456 | tf_op jit(solution)/shard_map/all_to_all | solution.py:539
  14.7 3.6 %collective-permute-start.5 = (bf16[2,32,2048]{2,1,0:T(8,128)(2,1)}, bf16[2,32,2048]{2,1,0:T(8,128)(2,1)}, u32[]{:S(2)}, u32[]{:S(2)}) collective-permute-start(bf16[2,32,2048]{2,1,0:T(8,128)(2,1)} %get-tuple-element.51.refs_1_.refs_0_), channel_id=1, source_target_pairs={{0,3},{1,2},{2,1},{3,0},{4,7},{5,6},{6,5},{7,4},{8,11},{9,10},{10,... | collective-permute-start | bytes 786440 | tf_op jit(solution)/shard_map/ppermute | solution.py:444
  19.1 6.8 %row_forward.1.attn_ref.row_ref = bf16[1024,512]{1,0:T(8,128)(2,1)} custom-call(bf16[1024,1024]{1,0:T(8,128)(2,1)} %bitcast.45, bf16[1024,1024]{1,0:T(8,128)(2,1)} %bitcast.48, bf16[1024,1024]{1,0:T(8,128)(2,1)} %bitcast.51, bf16[8,3,128,512]{3,2,1,0:T(8,128)(2,1)} %pack.1.refs_0_, bf16[2,32,2048]{2,1,0:T(8,128)(2,1)} %get-tuple-element.51.refs_1_.refs_0_), custom_call_target="tpu_custom_call" | custom-call | flops 115000000512 | tf_op jit(solution)/shard_map/row_forward/pallas_call | solution.py:178
  25.9 6.3 %weight_row.1 = (f32[4,2,32,2048]{3,2,1,0:T(8,128)}, bf16[4,2,32,2048]{3,2,1,0:T(8,128)(2,1)}) custom-call(s32[1]{0:T(128)} %bitcast.7.core_ref, bf16[1024,512]{1,0:T(8,128)(2,1)} %row_forward.1.attn_ref.row_ref, bf16[1024,2048]{1,0:T(8,128)(2,1)} %bitcast.38), custom_call_target="tpu_custom_call" | custom-call | flops 690000000 | tf_op jit(solution)/shard_map/weight_row/pallas_call | solution.py:427
  32.3 9.1 %collective-permute-done.4.refs_2_ = bf16[2,32,2048]{2,1,0:T(8,128)(2,1)} collective-permute-done((bf16[2,32,2048]{2,1,0:T(8,128)(2,1)}, bf16[2,32,2048]{2,1,0:T(8,128)(2,1)}, u32[]{:S(2)}, u32[]{:S(2)}) %collective-permute-start.4) | collective-permute-done | bytes 262176 | tf_op jit(solution)/shard_map/ppermute | solution.py:444
  47.1 3.4 %all-to-all-done.in_ref = bf16[8,3,128,512]{3,2,1,0:T(8,128)(2,1)S(1)} async-done(((bf16[8,3,128,512]{3,2,1,0:T(8,128)(2,1)}), bf16[8,3,128,512]{3,2,1,0:T(8,128)(2,1)S(1)}, u32[]{:S(2)}, u32[]{:S(2)}) %all-to-all-start) | async-done | bytes 3145760 | tf_op jit(solution)/shard_map/all_to_all | solution.py:539
  50.5 3.0 %column_forward.1 = bf16[8,128,512]{2,1,0:T(8,128)(2,1)} custom-call(bf16[8,3,128,512]{3,2,1,0:T(8,128)(2,1)S(1)} %all-to-all-done.in_ref), custom_call_target="tpu_custom_call" | custom-call | flops 126500003840 | tf_op jit(solution)/shard_map/column_forward/pallas_call | solution.py:335
  53.5 3.6 %all-to-all-start.1 = ((bf16[8,128,512]{2,1,0:T(8,128)(2,1)}), bf16[8,128,512]{2,1,0:T(8,128)(2,1)S(1)}, u32[]{:S(2)}, u32[]{:S(2)}) async-start(bf16[8,128,512]{2,1,0:T(8,128)(2,1)} %column_forward.1), calls=%async_computation.1 | async-start | bytes 2097152 | tf_op jit(solution)/shard_map/all_to_all | solution.py:539
  57.0 5.9 %collective-permute-done.6.refs_1_ = bf16[2,32,2048]{2,1,0:T(8,128)(2,1)S(1)} collective-permute-done((bf16[2,32,2048]{2,1,0:T(8,128)(2,1)}, bf16[2,32,2048]{2,1,0:T(8,128)(2,1)S(1)}, u32[]{:S(2)}, u32[]{:S(2)}) %collective-permute-start.6) | collective-permute-done | bytes 262176 | tf_op jit(solution)/shard_map/ppermute | solution.py:444
  62.9 6.3 %upstream_col.1 = (bf16[1024,512]{1,0:T(8,128)(2,1)}, bf16[512,2048]{1,0:T(8,128)(2,1)}) custom-call(s32[16]{0:T(128)} %mul.26.place_ref, bf16[2,32,2048]{2,1,0:T(8,128)(2,1)} %get-tuple-element.51.refs_1_.refs_0_, bf16[2,32,2048]{2,1,0:T(8,128)(2,1)} %copy-done.14, bf16[2,32,2048]{2,1,0:T(8,128)(2,1)} %collective-permute-done.4.refs_2_, ...), custom_call_target="tpu_custom_call" | custom-call | flops 80499998720 | tf_op jit(solution)/shard_map/upstream_col/pallas_call | solution.py:366
  72.4 3.6 %all-to-all-start.2 = ((bf16[8,128,512]{2,1,0:T(8,128)(2,1)}), bf16[8,128,512]{2,1,0:T(8,128)(2,1)S(1)}, u32[]{:S(2)}, u32[]{:S(2)}) async-start(bf16[8,128,512]{2,1,0:T(8,128)(2,1)} %bitcast.57), calls=%async_computation.2 | async-start | bytes 2097152 | tf_op jit(solution)/shard_map/all_to_all | solution.py:539
  81.2 6.3 %weight_col.1 = (f32[4,2,32,2048]{3,2,1,0:T(8,128)}, bf16[4,2,32,2048]{3,2,1,0:T(8,128)(2,1)}) custom-call(s32[1]{0:T(128)} %bitcast.7.core_ref, bf16[1024,512]{1,0:T(8,128)(2,1)} %bitcast.42, bf16[1024,2048]{1,0:T(8,128)(2,1)} %bitcast.40), custom_call_target="tpu_custom_call" | custom-call | flops 115000000 | tf_op jit(solution)/shard_map/weight_col/pallas_call | solution.py:427
  87.6 3.7 %collective-permute-done.18.refs_1_ = bf16[2,32,2048]{2,1,0:T(8,128)(2,1)S(1)} collective-permute-done((bf16[2,32,2048]{2,1,0:T(8,128)(2,1)}, bf16[2,32,2048]{2,1,0:T(8,128)(2,1)S(1)}, u32[]{:S(2)}, u32[]{:S(2)}) %collective-permute-start.18) | collective-permute-done | bytes 262176 | tf_op jit(solution)/shard_map/ppermute | solution.py:444
  96.4 4.5 %column_backward.1 = bf16[8,3,128,512]{3,2,1,0:T(8,128)(2,1)} custom-call(bf16[8,3,128,512]{3,2,1,0:T(8,128)(2,1)S(1)} %copy-done.1, bf16[8,128,512]{2,1,0:T(8,128)(2,1)S(1)} %all-to-all-done.2.u_ref), custom_call_target="tpu_custom_call" | custom-call | flops 138000007168 | tf_op jit(solution)/shard_map/column_backward/pallas_call | solution.py:335
  100.9 4.6 %all-to-all-start.3 = ((bf16[8,3,128,512]{3,2,1,0:T(8,128)(2,1)}), bf16[8,3,128,512]{3,2,1,0:T(8,128)(2,1)}, u32[]{:S(2)}, u32[]{:S(2)}) async-start(bf16[8,3,128,512]{3,2,1,0:T(8,128)(2,1)} %column_backward.1), calls=%async_computation.3 | async-start | bytes 6291456 | tf_op jit(solution)/shard_map/all_to_all | solution.py:539
  107.4 2.9 %collective-permute-start.24 = (bf16[2,32,2048]{2,1,0:T(8,128)(2,1)S(1)}, bf16[2,32,2048]{2,1,0:T(8,128)(2,1)S(1)}, u32[]{:S(2)}, u32[]{:S(2)}) collective-permute-start(bf16[2,32,2048]{2,1,0:T(8,128)(2,1)S(1)} %get-tuple-element.96), channel_id=1, source_target_pairs={{0,3},{1,2},{2,1},{3,0},{4,7},{5,6},{6,5},{7,4},{8,11},{9,10},{10,... | collective-permute-start | bytes 786440 | tf_op jit(solution)/shard_map/ppermute | solution.py:444
  111.9 2.8 %collective-permute-start.21 = (bf16[2,32,2048]{2,1,0:T(8,128)(2,1)S(1)}, bf16[2,32,2048]{2,1,0:T(8,128)(2,1)S(1)}, u32[]{:S(2)}, u32[]{:S(2)}) collective-permute-start(bf16[2,32,2048]{2,1,0:T(8,128)(2,1)S(1)} %copy-done.9), channel_id=1, source_target_pairs={{0,3},{1,2},{2,1},{3,0},{4,7},{5,6},{6,5},{7,4},{8,11},{9,10},{10,... | collective-permute-start | bytes 786440 | tf_op jit(solution)/shard_map/ppermute | solution.py:444
  114.7 6.2 %upstream_row.1 = (bf16[1024,512]{1,0:T(8,128)(2,1)}, bf16[512,2048]{1,0:T(8,128)(2,1)}) custom-call(s32[16]{0:T(128)} %mul.26.place_ref, bf16[2,32,2048]{2,1,0:T(8,128)(2,1)} %get-tuple-element.59.refs_0_, bf16[2,32,2048]{2,1,0:T(8,128)(2,1)} %copy-done.8, bf16[2,32,2048]{2,1,0:T(8,128)(2,1)} %collective-permute-done.7.refs_2_, ...), custom_call_target="tpu_custom_call" | custom-call | flops 115000000 | tf_op jit(solution)/shard_map/upstream_row/pallas_call | solution.py:366
  120.9 12.2 %row_backward.1 = (bf16[1024,1024]{1,0:T(8,128)(2,1)}, bf16[1024,1024]{1,0:T(8,128)(2,1)}, bf16[1024,1024]{1,0:T(8,128)(2,1)}) custom-call(bf16[1024,1024]{1,0:T(8,128)(2,1)} %bitcast.46, bf16[1024,1024]{1,0:T(8,128)(2,1)} %bitcast.49, bf16[1024,1024]{1,0:T(8,128)(2,1)} %bitcast.52, bf16[1024,512]{1,0:T(8,128)(2,1)} %get-tuple-element.75.u_ref), custom_call_target="tpu_custom_call" | custom-call | flops 1610000000 | tf_op jit(solution)/shard_map/row_backward/pallas_call | solution.py:193
  133.1 8.7 %layer_output.1 = bf16[1024,2048]{1,0:T(8,128)(2,1)} custom-call(bf16[1024,512]{1,0:T(8,128)(2,1)} %row_forward.1.attn_ref.row_ref, bf16[1024,512]{1,0:T(8,128)(2,1)} %bitcast.43, bf16[512,2048]{1,0:T(8,128)(2,1)} %get-tuple-element.78.w_row_ref, bf16[512,2048]{1,0:T(8,128)(2,1)} %get-tuple-element.79.w_col_ref), custom_call_target="tpu_custom_call" | custom-call | flops 1035000000 | tf_op jit(solution)/shard_map/layer_output/pallas_call | solution.py:395
  142.3 2.7 %collective-permute-start.27 = (bf16[32,2048]{1,0:T(8,128)(2,1)S(1)}, bf16[32,2048]{1,0:T(8,128)(2,1)S(1)}, u32[]{:S(2)}, u32[]{:S(2)}) collective-permute-start(bf16[32,2048]{1,0:T(8,128)(2,1)S(1)} %get-tuple-element.105), channel_id=1, source_target_pairs={{0,24},{4,28},{8,16},{12,20},{16,8},{20,12},{24,0},{28,4},{1,25},{... | collective-permute-start | bytes 393224 | tf_op jit(solution)/shard_map/ppermute | solution.py:444
  145.8 3.6 %unpack.1 = (bf16[1024,1024]{1,0:T(8,128)(2,1)}, bf16[1024,1024]{1,0:T(8,128)(2,1)}, bf16[1024,1024]{1,0:T(8,128)(2,1)}) custom-call(bf16[8,3,128,512]{3,2,1,0:T(8,128)(2,1)} %all-to-all-done.3.in_ref, bf16[1024,1024]{1,0:T(8,128)(2,1)} %get-tuple-element.76._q, ...), custom_call_target="tpu_custom_call", output_to_operand_aliasing={{0}: (1, {}), {1}: (2, {}), {2}: (3, {})} | custom-call | flops 690000000 | tf_op jit(solution)/shard_map/unpack/pallas_call | solution.py:246
  (92 shorter events, 30.4 us)
Async XLA Ops:
  0.6 12.1 %collective-permute-start = (bf16[32,2048]{1,0:T(8,128)(2,1)}, bf16[32,2048]{1,0:T(8,128)(2,1)S(1)}, u32[]{:S(2)}, u32[]{:S(2)}) collective-permute-start(bf16[32,2048]{1,0:T(8,128)(2,1)} %param.8), channel_id=1, source_target_pairs={{0,8},{4,12},{8,0},{12,4},{16,24},{20,28},{24,16},{28,20},{1,9},{5... | collective-permute-start | bytes 393224 | tf_op jit(solution)/shard_map/ppermute | solution.py:444
  3.6 9.1 %collective-permute-start.2 = (bf16[32,2048]{1,0:T(8,128)(2,1)}, bf16[32,2048]{1,0:T(8,128)(2,1)S(1)}, u32[]{:S(2)}, u32[]{:S(2)}) collective-permute-start(bf16[32,2048]{1,0:T(8,128)(2,1)} %param.8), channel_id=1, source_target_pairs={{0,24},{4,28},{8,16},{12,20},{16,8},{20,12},{24,0},{28,4},{1,25},{... | collective-permute-start | bytes 393224 | tf_op jit(solution)/shard_map/ppermute | solution.py:444
  8.3 42.2 %all-to-all-start = ((bf16[8,3,128,512]{3,2,1,0:T(8,128)(2,1)}), bf16[8,3,128,512]{3,2,1,0:T(8,128)(2,1)S(1)}, u32[]{:S(2)}, u32[]{:S(2)}) async-start(bf16[8,3,128,512]{3,2,1,0:T(8,128)(2,1)} %pack.1.refs_0_), calls=%async_computation | async-start | bytes 6291456 | tf_op jit(solution)/shard_map/all_to_all | solution.py:539
  14.7 17.6 %collective-permute-start.5 = (bf16[2,32,2048]{2,1,0:T(8,128)(2,1)}, bf16[2,32,2048]{2,1,0:T(8,128)(2,1)}, u32[]{:S(2)}, u32[]{:S(2)}) collective-permute-start(bf16[2,32,2048]{2,1,0:T(8,128)(2,1)} %get-tuple-element.51.refs_1_.refs_0_), channel_id=1, source_target_pairs={{0,3},{1,2},{2,1},{3,0},{4,7},{5,6},{6,5},{7,4},{8,11},{9,10},{10,... | collective-permute-start | bytes 786440 | tf_op jit(solution)/shard_map/ppermute | solution.py:444
  18.3 23.1 %collective-permute-start.4 = (bf16[2,32,2048]{2,1,0:T(8,128)(2,1)}, bf16[2,32,2048]{2,1,0:T(8,128)(2,1)}, u32[]{:S(2)}, u32[]{:S(2)}) collective-permute-start(bf16[2,32,2048]{2,1,0:T(8,128)(2,1)} %get-tuple-element.51.refs_1_.refs_0_), channel_id=1, source_target_pairs={{0,2},{1,3},{2,0},{3,1},{4,6},{5,7},{6,4},{7,5},{8,10},{9,11},{10,... | collective-permute-start | bytes 786440 | tf_op jit(solution)/shard_map/ppermute | solution.py:444
  18.3 23.1 %collective-permute-start.3 = (bf16[2,32,2048]{2,1,0:T(8,128)(2,1)}, bf16[2,32,2048]{2,1,0:T(8,128)(2,1)S(1)}, u32[]{:S(2)}, u32[]{:S(2)}) collective-permute-start(bf16[2,32,2048]{2,1,0:T(8,128)(2,1)} %get-tuple-element.51.refs_1_.refs_0_), channel_id=1, source_target_pairs={{0,1},{1,0},{2,3},{3,2},{4,5},{5,4},{6,7},{7,6},{8,9},{9,8},{10,11... | collective-permute-start | bytes 786440 | tf_op jit(solution)/shard_map/ppermute | solution.py:444
  32.3 12.9 %collective-permute-start.9 = (bf16[2,32,2048]{2,1,0:T(8,128)(2,1)}, bf16[2,32,2048]{2,1,0:T(8,128)(2,1)}, u32[]{:S(2)}, u32[]{:S(2)}) collective-permute-start(bf16[2,32,2048]{2,1,0:T(8,128)(2,1)} %get-tuple-element.51.refs_1_.refs_0_), channel_id=1, source_target_pairs={{0,4},{4,0},{8,12},{12,8},{16,20},{20,16},{24,28},{28,24},{1,5},{5... | collective-permute-start | bytes 786440 | tf_op jit(solution)/shard_map/ppermute | solution.py:444
  42.6 28.8 %collective-permute-start.8 = (bf16[2,32,2048]{2,1,0:T(8,128)(2,1)}, bf16[2,32,2048]{2,1,0:T(8,128)(2,1)}, u32[]{:S(2)}, u32[]{:S(2)}) collective-permute-start(bf16[2,32,2048]{2,1,0:T(8,128)(2,1)} %get-tuple-element.59.refs_0_), channel_id=1, source_target_pairs={{0,3},{1,2},{2,1},{3,0},{4,7},{5,6},{6,5},{7,4},{8,11},{9,10},{10,... | collective-permute-start | bytes 786440 | tf_op jit(solution)/shard_map/ppermute | solution.py:444
  45.1 26.4 %collective-permute-start.7 = (bf16[2,32,2048]{2,1,0:T(8,128)(2,1)}, bf16[2,32,2048]{2,1,0:T(8,128)(2,1)}, u32[]{:S(2)}, u32[]{:S(2)}) collective-permute-start(bf16[2,32,2048]{2,1,0:T(8,128)(2,1)} %get-tuple-element.59.refs_0_), channel_id=1, source_target_pairs={{0,2},{1,3},{2,0},{3,1},{4,6},{5,7},{6,4},{7,5},{8,10},{9,11},{10,... | collective-permute-start | bytes 786440 | tf_op jit(solution)/shard_map/ppermute | solution.py:444
  45.1 17.8 %collective-permute-start.6 = (bf16[2,32,2048]{2,1,0:T(8,128)(2,1)}, bf16[2,32,2048]{2,1,0:T(8,128)(2,1)S(1)}, u32[]{:S(2)}, u32[]{:S(2)}) collective-permute-start(bf16[2,32,2048]{2,1,0:T(8,128)(2,1)} %get-tuple-element.59.refs_0_), channel_id=1, source_target_pairs={{0,1},{1,0},{2,3},{3,2},{4,5},{5,4},{6,7},{7,6},{8,9},{9,8},{10,11... | collective-permute-start | bytes 786440 | tf_op jit(solution)/shard_map/ppermute | solution.py:444
  47.1 22.2 %collective-permute-start.17 = (bf16[4,2,32,2048]{3,2,1,0:T(8,128)(2,1)}, bf16[4,2,32,2048]{3,2,1,0:T(8,128)(2,1)}, u32[]{:S(2)}, u32[]{:S(2)}) collective-permute-start(bf16[4,2,32,2048]{3,2,1,0:T(8,128)(2,1)} %get-tuple-element.65), channel_id=1, source_target_pairs={{0,4},{4,0},{8,12},{12,8},{16,20},{20,16},{24,28},{28,24},{1,5},{5... | collective-permute-start | bytes 3145736 | tf_op jit(solution)/shard_map/ppermute | solution.py:444
  53.5 18.9 %all-to-all-start.1 = ((bf16[8,128,512]{2,1,0:T(8,128)(2,1)}), bf16[8,128,512]{2,1,0:T(8,128)(2,1)S(1)}, u32[]{:S(2)}, u32[]{:S(2)}) async-start(bf16[8,128,512]{2,1,0:T(8,128)(2,1)} %column_forward.1), calls=%async_computation.1 | async-start | bytes 2097152 | tf_op jit(solution)/shard_map/all_to_all | solution.py:539
  72.4 22.1 %all-to-all-start.2 = ((bf16[8,128,512]{2,1,0:T(8,128)(2,1)}), bf16[8,128,512]{2,1,0:T(8,128)(2,1)S(1)}, u32[]{:S(2)}, u32[]{:S(2)}) async-start(bf16[8,128,512]{2,1,0:T(8,128)(2,1)} %bitcast.57), calls=%async_computation.2 | async-start | bytes 2097152 | tf_op jit(solution)/shard_map/all_to_all | solution.py:539
  76.3 11.2 %collective-permute-start.14 = (bf16[2,32,2048]{2,1,0:T(8,128)(2,1)S(1)}, bf16[2,32,2048]{2,1,0:T(8,128)(2,1)S(1)}, u32[]{:S(2)}, u32[]{:S(2)}) collective-permute-start(bf16[2,32,2048]{2,1,0:T(8,128)(2,1)S(1)} %collective-permute-done.6.refs_1_), channel_id=1, source_target_pairs={{0,4},{4,0},{8,12},{12,8},{16,20},{20,16},{24,28},{28,24},{1,5},{5... | collective-permute-start | bytes 786440 | tf_op jit(solution)/shard_map/ppermute | solution.py:444
  76.5 11.1 %collective-permute-start.15 = (bf16[2,32,2048]{2,1,0:T(8,128)(2,1)}, bf16[2,32,2048]{2,1,0:T(8,128)(2,1)S(1)}, u32[]{:S(2)}, u32[]{:S(2)}) collective-permute-start(bf16[2,32,2048]{2,1,0:T(8,128)(2,1)} %collective-permute-done.7.refs_2_), channel_id=1, source_target_pairs={{0,4},{4,0},{8,12},{12,8},{16,20},{20,16},{24,28},{28,24},{1,5},{5... | collective-permute-start | bytes 786440 | tf_op jit(solution)/shard_map/ppermute | solution.py:444
  76.9 10.7 %collective-permute-start.16 = (bf16[2,32,2048]{2,1,0:T(8,128)(2,1)}, bf16[2,32,2048]{2,1,0:T(8,128)(2,1)S(1)}, u32[]{:S(2)}, u32[]{:S(2)}) collective-permute-start(bf16[2,32,2048]{2,1,0:T(8,128)(2,1)} %collective-permute-done.8.refs_3_), channel_id=1, source_target_pairs={{0,4},{4,0},{8,12},{12,8},{16,20},{20,16},{24,28},{28,24},{1,5},{5... | collective-permute-start | bytes 786440 | tf_op jit(solution)/shard_map/ppermute | solution.py:444
  77.0 14.3 %collective-permute-start.18 = (bf16[2,32,2048]{2,1,0:T(8,128)(2,1)}, bf16[2,32,2048]{2,1,0:T(8,128)(2,1)S(1)}, u32[]{:S(2)}, u32[]{:S(2)}) collective-permute-start(bf16[2,32,2048]{2,1,0:T(8,128)(2,1)} %get-tuple-element.68), channel_id=1, source_target_pairs={{0,1},{1,0},{2,3},{3,2},{4,5},{5,4},{6,7},{7,6},{8,9},{9,8},{10,11... | collective-permute-start | bytes 786440 | tf_op jit(solution)/shard_map/ppermute | solution.py:444
  78.9 14.9 %collective-permute-start.19 = (bf16[2,32,2048]{2,1,0:T(8,128)(2,1)S(1)}, bf16[2,32,2048]{2,1,0:T(8,128)(2,1)S(1)}, u32[]{:S(2)}, u32[]{:S(2)}) collective-permute-start(bf16[2,32,2048]{2,1,0:T(8,128)(2,1)S(1)} %get-tuple-element.69), channel_id=1, source_target_pairs={{0,2},{1,3},{2,0},{3,1},{4,6},{5,7},{6,4},{7,5},{8,10},{9,11},{10,... | collective-permute-start | bytes 786440 | tf_op jit(solution)/shard_map/ppermute | solution.py:444
  87.5 13.4 %collective-permute-start.20 = (bf16[4,2,32,2048]{3,2,1,0:T(8,128)(2,1)}, bf16[4,2,32,2048]{3,2,1,0:T(8,128)(2,1)S(1)}, u32[]{:S(2)}, u32[]{:S(2)}) collective-permute-start(bf16[4,2,32,2048]{3,2,1,0:T(8,128)(2,1)} %get-tuple-element.71), channel_id=1, source_target_pairs={{0,4},{4,0},{8,12},{12,8},{16,20},{20,16},{24,28},{28,24},{1,5},{5... | collective-permute-start | bytes 3145736 | tf_op jit(solution)/shard_map/ppermute | solution.py:444
  100.9 44.9 %all-to-all-start.3 = ((bf16[8,3,128,512]{3,2,1,0:T(8,128)(2,1)}), bf16[8,3,128,512]{3,2,1,0:T(8,128)(2,1)}, u32[]{:S(2)}, u32[]{:S(2)}) async-start(bf16[8,3,128,512]{3,2,1,0:T(8,128)(2,1)} %column_backward.1), calls=%async_computation.3 | async-start | bytes 6291456 | tf_op jit(solution)/shard_map/all_to_all | solution.py:539
  107.4 34.3 %collective-permute-start.24 = (bf16[2,32,2048]{2,1,0:T(8,128)(2,1)S(1)}, bf16[2,32,2048]{2,1,0:T(8,128)(2,1)S(1)}, u32[]{:S(2)}, u32[]{:S(2)}) collective-permute-start(bf16[2,32,2048]{2,1,0:T(8,128)(2,1)S(1)} %get-tuple-element.96), channel_id=1, source_target_pairs={{0,3},{1,2},{2,1},{3,0},{4,7},{5,6},{6,5},{7,4},{8,11},{9,10},{10,... | collective-permute-start | bytes 786440 | tf_op jit(solution)/shard_map/ppermute | solution.py:444
  110.3 31.5 %collective-permute-start.23 = (bf16[2,32,2048]{2,1,0:T(8,128)(2,1)S(1)}, bf16[2,32,2048]{2,1,0:T(8,128)(2,1)S(1)}, u32[]{:S(2)}, u32[]{:S(2)}) collective-permute-start(bf16[2,32,2048]{2,1,0:T(8,128)(2,1)S(1)} %get-tuple-element.97), channel_id=1, source_target_pairs={{0,2},{1,3},{2,0},{3,1},{4,6},{5,7},{6,4},{7,5},{8,10},{9,11},{10,... | collective-permute-start | bytes 786440 | tf_op jit(solution)/shard_map/ppermute | solution.py:444
  110.3 31.5 %collective-permute-start.22 = (bf16[2,32,2048]{2,1,0:T(8,128)(2,1)S(1)}, bf16[2,32,2048]{2,1,0:T(8,128)(2,1)S(1)}, u32[]{:S(2)}, u32[]{:S(2)}) collective-permute-start(bf16[2,32,2048]{2,1,0:T(8,128)(2,1)S(1)} %get-tuple-element.98), channel_id=1, source_target_pairs={{0,1},{1,0},{2,3},{3,2},{4,5},{5,4},{6,7},{7,6},{8,9},{9,8},{10,11... | collective-permute-start | bytes 786440 | tf_op jit(solution)/shard_map/ppermute | solution.py:444
  111.9 29.9 %collective-permute-start.21 = (bf16[2,32,2048]{2,1,0:T(8,128)(2,1)S(1)}, bf16[2,32,2048]{2,1,0:T(8,128)(2,1)S(1)}, u32[]{:S(2)}, u32[]{:S(2)}) collective-permute-start(bf16[2,32,2048]{2,1,0:T(8,128)(2,1)S(1)} %copy-done.9), channel_id=1, source_target_pairs={{0,3},{1,2},{2,1},{3,0},{4,7},{5,6},{6,5},{7,4},{8,11},{9,10},{10,... | collective-permute-start | bytes 786440 | tf_op jit(solution)/shard_map/ppermute | solution.py:444
  (23 other events, 127.5 us)
